TPU v7x, 32 devices: a whole 2x2x4 slice. The times are simulated.
32 devices in a mesh: shot: 8 (over z, core), dom: 4 (over y, x).
Axes of the slice: x: 2, y: 2, z: 4, core: 2. Of those that a mesh axis runs over, the one named last changes fastest.
Arguments:
- kappa: float32 [8, 512, 128], P('dom'), may hold values from 0.05 to 0.15
- wave_now: float32 [8, 8, 512, 128], P('shot', 'dom'), may hold values from -6 to 6
- wave_before: float32 [8, 8, 512, 128], P('shot', 'dom'), may hold values from -6 to 6
- wavelet: float32 [8, 4], P('shot'), may hold values from -8 to 8
- source_cell: int32 [8], P('shot'), may hold values from 0 to 524287
- receiver_cells: int32 [8, 2048], P('shot'), may hold values from 0 to 524287
- observed: float32 [8, 4, 2048], P('shot'), may hold values from -6 to 6
Outputs:
- total_gradient: float32 [8, 512, 128], P('dom', 'shot')
- wave_next: float32 [8, 8, 512, 128], P('shot', 'dom')
Inputs may be any that keep to these rules, and one draw needn't show every extreme that they name: `source_cell`: a cell index x * 512 * 128 + y * 128 + z. `receiver_cells`: cell indices x * 512 * 128 + y * 128 + z; a cell may hold several receivers.
All inputs are finite; a program needn't handle non-finite values.
Results may differ from a plain program's by a relative error of at most 0.00013.
Values sent between devices are 32-bit elements; how exact they have to be, the bound alone decides.
No kernel may reach another device: no remote copies, remote signals or barrier semaphores. Data moves between devices by JAX's collectives and lax.ppermute only.
A program may use at most 64 MiB of HBM per device.

v0:
```python
import jax
import jax.numpy as jnp
from jax import lax
from jax.sharding import PartitionSpec as P

NT = 4


PRIOR_GAIN = 50.0


def with_halo(cells, sides, width):
    for axis, dim in sides:
        count = lax.axis_size(axis)
        ends = count - 1
        head = lax.slice_in_dim(cells, 0, width, axis=dim)
        tail = lax.slice_in_dim(cells, cells.shape[dim] - width, cells.shape[dim], axis=dim)
        cells = jnp.concatenate(
            [
                lax.ppermute(tail, axis, [(i, (i + 1) % count) for i in range(ends)]),
                cells,
                lax.ppermute(head, axis, [((i + 1) % count, i) for i in range(ends)]),
            ],
            axis=dim,
        )
    return cells


def neighbours(padded):
    core = padded[..., 1:-1, :, :]
    widths = [(0, 0)] * (core.ndim - 2) + [(1, 1), (1, 1)]
    flank = jnp.pad(core, widths)
    total = padded[..., 2:, :, :] + padded[..., :-2, :, :]
    total = total + flank[..., 2:, 1:-1] + flank[..., :-2, 1:-1]
    total = total + flank[..., 1:-1, 2:] + flank[..., 1:-1, :-2]
    return total


def shards(kappa, wave_now, wave_before, wavelet, source_cell, receiver_cells, observed):
    shots, planes, rows_y, depth = wave_now.shape
    cells = planes * rows_y * depth
    offset = lax.axis_index("dom") * cells
    source_local = source_cell - offset
    source_mine = (source_local >= 0) & (source_local < cells)
    source_at = jnp.clip(source_local, 0, cells - 1)
    receiver_local = receiver_cells - offset
    receiver_mine = (receiver_local >= 0) & (receiver_local < cells)
    receiver_at = jnp.clip(receiver_local, 0, cells - 1)
    shot_rows = jnp.arange(shots)

    def inject_misfit(field, miss):
        flat = field.reshape(shots, cells)
        flat = flat.at[shot_rows[:, None], receiver_at].add(miss)
        return flat.reshape(field.shape)

    now, before = (wave_now, wave_before)
    history = []
    residues = []
    lap = now
    for step in range(NT):
        forward_padded = with_halo(now, (("dom", 1),), 1)
        lap = neighbours(forward_padded) - 6.0 * now
        history.append(lap)
        after = 2.0 * now - before + kappa * lap
        inject_flat = after.reshape(shots, cells)
        inject_flat = inject_flat.at[shot_rows, source_at].add(
            jnp.where(source_mine, wavelet[:, step], 0.0)
        )
        after = inject_flat.reshape(after.shape)
        misfit_flat = after.reshape(shots, cells)
        taken = jnp.take_along_axis(misfit_flat, receiver_at, axis=1)
        residues.append(jnp.where(receiver_mine, taken - observed[:, step], 0.0))
        before, now = (now, after)
    zeros = jnp.zeros_like(now)
    adjoint_next = inject_misfit(zeros, residues[NT - 1])
    adjoint_after = zeros
    image = jnp.sum(adjoint_next * history[NT - 1], axis=0)
    for level in range(NT - 1, 0, -1):
        weighted = kappa * adjoint_next
        padded = with_halo(weighted, (("dom", 1),), 1)
        lap_weighted = neighbours(padded) - 6.0 * weighted
        adjoint_now = 2.0 * adjoint_next + lap_weighted - adjoint_after
        adjoint_now = inject_misfit(adjoint_now, residues[level - 1])
        image = image + jnp.sum(adjoint_now * history[level - 1], axis=0)
        adjoint_after, adjoint_next = (adjoint_next, adjoint_now)
    owned = lax.psum_scatter(image, "shot", scatter_dimension=1, tiled=True)
    band = owned.shape[1]
    start = lax.axis_index("shot") * band
    widened = jnp.pad(kappa, ((0, 0), (1, 1), (0, 0)))
    strip = lax.dynamic_slice_in_dim(widened, start, band + 2, 1)
    rim = with_halo(strip, (("dom", 0),), 1)
    core = rim[1:-1, 1:-1]
    flank = jnp.pad(core, ((0, 0), (0, 0), (1, 1)))
    total = rim[2:, 1:-1] + rim[:-2, 1:-1]
    total = total + rim[1:-1, 2:] + rim[1:-1, :-2]
    total = total + flank[..., 2:] + flank[..., :-2]
    smooth = total / 6.0
    score = (smooth - core) * PRIOR_GAIN
    total_gradient = owned / NT - score
    return (total_gradient, now)


def solution(mesh):
    return jax.shard_map(
        shards,
        mesh=mesh,
        in_specs=(
            P("dom", None, None),
            P("shot", "dom", None, None),
            P("shot", "dom", None, None),
            P("shot", None),
            P("shot"),
            P("shot", None),
            P("shot", None, None),
        ),
        out_specs=(P("dom", "shot", None), P("shot", "dom", None, None)),
        check_vma=False,
    )
```

profile of v0, /device:TPU:0, one launch (start us, length us, event | category | flops | bytes accessed | tf_op | source)
XLA Modules:
  0.0 248.9 jit_solution(2666002190781109482)
XLA Ops:
  7.2 1.1 fusion.77
  8.4 1.3 collective-permute-start
  9.7 5.5 %collective-permute-start.1 = (f32[1,1,512,128]{3,2,1,0:T(8,128)S(1)}, f32[1,1,512,128]{3,2,1,0:T(8,128)S(1)}, u32[]{:S(2)}, u32[]{:S(2)}) collective-permute-start(f32[1,1,512,128]{3,2,1,0:T(8,128)S(1)} %get-tuple-element.72), channel_id=1, source_target_pairs={{0,1},{1,2},{2,3},{4,5},{5,6},{6,7},{8,9},{9,10},{10,11},{12,13},{... | collective-permute-start | bytes 786440 | tf_op jit(solution)/shard_map/ppermute | solution.py:20
  15.9 0.7 fusion.78
  16.5 0.8 and_reduce_fusion.1
  18.6 1.7 collective-permute-done
  20.4 0.4 collective-permute-done.1
  20.7 1.4 fusion.47
  22.1 0.6 fusion.79
  24.6 0.1 scatter-add.48
  24.8 1.3 collective-permute-start.2
  26.1 6.5 %collective-permute-start.3 = (f32[1,1,512,128]{3,2,1,0:T(8,128)S(1)}, f32[1,1,512,128]{3,2,1,0:T(8,128)S(1)}, u32[]{:S(2)}, u32[]{:S(2)}) collective-permute-start(f32[1,1,512,128]{3,2,1,0:T(8,128)S(1)} %get-tuple-element.70), channel_id=1, source_target_pairs={{0,1},{1,2},{2,3},{4,5},{5,6},{6,7},{8,9},{9,10},{10,11},{12,13},{... | collective-permute-start | bytes 786440 | tf_op jit(solution)/shard_map/ppermute | solution.py:20
  32.7 4.2 %collective-permute-done.2 = f32[1,1,512,128]{3,2,1,0:T(8,128)S(1)} collective-permute-done((f32[1,1,512,128]{3,2,1,0:T(8,128)S(1)}, f32[1,1,512,128]{3,2,1,0:T(8,128)S(1)}, u32[]{:S(2)}, u32[]{:S(2)}) %collective-permute-start.2) | collective-permute-done | bytes 262176 | tf_op jit(solution)/shard_map/ppermute | solution.py:22
  36.9 0.6 collective-permute-done.3
  37.5 1.2 fusion.48
  38.7 0.6 fusion.80
  41.3 0.1 scatter-add.49
  41.4 1.3 collective-permute-start.4
  42.7 6.5 %collective-permute-start.5 = (f32[1,1,512,128]{3,2,1,0:T(8,128)S(1)}, f32[1,1,512,128]{3,2,1,0:T(8,128)S(1)}, u32[]{:S(2)}, u32[]{:S(2)}) collective-permute-start(f32[1,1,512,128]{3,2,1,0:T(8,128)S(1)} %get-tuple-element.68), channel_id=1, source_target_pairs={{0,1},{1,2},{2,3},{4,5},{5,6},{6,7},{8,9},{9,10},{10,11},{12,13},{... | collective-permute-start | bytes 786440 | tf_op jit(solution)/shard_map/ppermute | solution.py:20
  49.3 0.1 and_reduce_fusion
  50.1 3.1 %collective-permute-done.4 = f32[1,1,512,128]{3,2,1,0:T(8,128)S(1)} collective-permute-done((f32[1,1,512,128]{3,2,1,0:T(8,128)S(1)}, f32[1,1,512,128]{3,2,1,0:T(8,128)S(1)}, u32[]{:S(2)}, u32[]{:S(2)}) %collective-permute-start.4) | collective-permute-done | bytes 262176 | tf_op jit(solution)/shard_map/ppermute | solution.py:22
  53.2 0.6 collective-permute-done.5
  53.9 1.1 fusion.49
  55.0 0.6 fusion.81
  57.6 0.1 scatter-add.50
  57.7 0.7 fusion.74
  58.5 1.3 collective-permute-start.6
  59.8 6.5 %collective-permute-start.7 = (f32[1,1,512,128]{3,2,1,0:T(8,128)S(1)}, f32[1,1,512,128]{3,2,1,0:T(8,128)S(1)}, u32[]{:S(2)}, u32[]{:S(2)}) collective-permute-start(f32[1,1,512,128]{3,2,1,0:T(8,128)S(1)} %get-tuple-element.66), channel_id=1, source_target_pairs={{0,1},{1,2},{2,3},{4,5},{5,6},{6,7},{8,9},{9,10},{10,11},{12,13},{... | collective-permute-start | bytes 786440 | tf_op jit(solution)/shard_map/ppermute | solution.py:20
  66.3 0.1 fusion.62
  67.0 11.8 %gather_fusion.3 = f32[2048]{0:T(1024)S(1)} fusion(f32[131072]{0:T(1024)S(1)} %bitcast.103, s32[2048]{0:T(1024)S(1)} %broadcast_clamp_fusion), kind=kCustom, calls=%fused_computation.3.clone | custom fusion | bytes 24576 | tf_op jit(solution)/shard_map/jit(take_along_axis)/gather | solution.py:71
  78.8 11.8 %gather_fusion.2 = f32[2048]{0:T(1024)S(1)} fusion(f32[131072]{0:T(1024)S(1)} %bitcast.108, s32[2048]{0:T(1024)S(1)} %broadcast_clamp_fusion), kind=kCustom, calls=%fused_computation.2.clone | custom fusion | bytes 24576 | tf_op jit(solution)/shard_map/jit(take_along_axis)/gather | solution.py:71
  90.6 11.8 %gather_fusion.1 = f32[2048]{0:T(1024)S(1)} fusion(f32[131072]{0:T(1024)S(1)} %bitcast.113, s32[2048]{0:T(1024)S(1)} %broadcast_clamp_fusion), kind=kCustom, calls=%fused_computation.1.clone | custom fusion | bytes 24576 | tf_op jit(solution)/shard_map/jit(take_along_axis)/gather | solution.py:71
  102.4 1.1 fusion.50
  103.5 0.6 fusion.82
  106.1 0.1 scatter-add.51
  106.2 11.8 %gather_fusion = f32[2048]{0:T(1024)S(1)} fusion(f32[131072]{0:T(1024)S(1)} %bitcast.119, s32[2048]{0:T(1024)S(1)} %broadcast_clamp_fusion), kind=kCustom, calls=%fused_computation.clone | custom fusion | bytes 24576 | tf_op jit(solution)/shard_map/jit(take_along_axis)/gather | solution.py:71
  118.0 0.1 fusion.63
  118.1 11.8 %scatter_custom_fusion = f32[131072]{0:T(1024)S(1)} fusion(s32[2048]{0:T(1024)S(1)} %broadcast_select_fusion, f32[2048]{0:T(1024)S(1)} %bitcast.134, f32[]{:T(128)} %constant.123.clone.1), kind=kCustom, calls=%fused_computation.112 | custom fusion | flops 2048 | bytes 524292
  129.9 0.1 multiply_bitcast_fusion.2
  130.0 1.3 collective-permute-start.8
  131.3 5.4 %collective-permute-start.9 = (f32[1,1,512,128]{3,2,1,0:T(8,128)S(1)}, f32[1,1,512,128]{3,2,1,0:T(8,128)S(1)}, u32[]{:S(2)}, u32[]{:S(2)}) collective-permute-start(f32[1,1,512,128]{3,2,1,0:T(8,128)S(1)} %get-tuple-element.64), channel_id=1, source_target_pairs={{0,1},{1,2},{2,3},{4,5},{5,6},{6,7},{8,9},{9,10},{10,11},{12,13},{... | collective-permute-start | bytes 786440 | tf_op jit(solution)/shard_map/ppermute | solution.py:20
  136.8 4.1 %collective-permute-done.8 = f32[1,1,512,128]{3,2,1,0:T(8,128)S(1)} collective-permute-done((f32[1,1,512,128]{3,2,1,0:T(8,128)S(1)}, f32[1,1,512,128]{3,2,1,0:T(8,128)S(1)}, u32[]{:S(2)}, u32[]{:S(2)}) %collective-permute-start.8) | collective-permute-done | bytes 262176 | tf_op jit(solution)/shard_map/ppermute | solution.py:22
  140.9 0.4 fusion.25
  141.3 12.2 %scatter_fusion = f32[131072]{0:T(1024)S(1)} fusion(f32[131072]{0:T(1024)S(1)} %bitcast.87, s32[2048]{0:T(1024)S(1)} %broadcast_select_fusion, f32[2048]{0:T(1024)S(1)} %bitcast.128), kind=kCustom, calls=%fused_computation.5 | custom fusion | flops 2048 | bytes 32768
  153.5 0.1 multiply_bitcast_fusion.1
  153.6 1.3 collective-permute-start.10
  154.9 6.2 %collective-permute-start.11 = (f32[1,1,512,128]{3,2,1,0:T(8,128)S(1)}, f32[1,1,512,128]{3,2,1,0:T(8,128)S(1)}, u32[]{:S(2)}, u32[]{:S(2)}) collective-permute-start(f32[1,1,512,128]{3,2,1,0:T(8,128)S(1)} %get-tuple-element.62), channel_id=1, source_target_pairs={{0,1},{1,2},{2,3},{4,5},{5,6},{6,7},{8,9},{9,10},{10,11},{12,13},{... | collective-permute-start | bytes 786440 | tf_op jit(solution)/shard_map/ppermute | solution.py:20
  161.1 3.3 %collective-permute-done.10 = f32[1,1,512,128]{3,2,1,0:T(8,128)S(1)} collective-permute-done((f32[1,1,512,128]{3,2,1,0:T(8,128)S(1)}, f32[1,1,512,128]{3,2,1,0:T(8,128)S(1)}, u32[]{:S(2)}, u32[]{:S(2)}) %collective-permute-start.10) | collective-permute-done | bytes 262176 | tf_op jit(solution)/shard_map/ppermute | solution.py:22
  164.4 0.7 collective-permute-done.11
  165.0 0.5 fusion.32
  165.5 12.2 %scatter_fusion.1 = f32[131072]{0:T(1024)S(1)} fusion(f32[131072]{0:T(1024)S(1)} %bitcast.93, s32[2048]{0:T(1024)S(1)} %broadcast_select_fusion, f32[2048]{0:T(1024)S(1)} %bitcast.127), kind=kCustom, calls=%fused_computation.6 | custom fusion | flops 2048 | bytes 32768
  177.7 0.1 multiply_bitcast_fusion
  177.8 1.3 collective-permute-start.12
  179.1 6.6 %collective-permute-start.13 = (f32[1,1,512,128]{3,2,1,0:T(8,128)S(1)}, f32[1,1,512,128]{3,2,1,0:T(8,128)S(1)}, u32[]{:S(2)}, u32[]{:S(2)}) collective-permute-start(f32[1,1,512,128]{3,2,1,0:T(8,128)S(1)} %get-tuple-element.60), channel_id=1, source_target_pairs={{0,1},{1,2},{2,3},{4,5},{5,6},{6,7},{8,9},{9,10},{10,11},{12,13},{... | collective-permute-start | bytes 786440 | tf_op jit(solution)/shard_map/ppermute | solution.py:20
  185.7 3.1 %collective-permute-done.12 = f32[1,1,512,128]{3,2,1,0:T(8,128)S(1)} collective-permute-done((f32[1,1,512,128]{3,2,1,0:T(8,128)S(1)}, f32[1,1,512,128]{3,2,1,0:T(8,128)S(1)}, u32[]{:S(2)}, u32[]{:S(2)}) %collective-permute-start.12) | collective-permute-done | bytes 262176 | tf_op jit(solution)/shard_map/ppermute | solution.py:22
  188.8 0.7 collective-permute-done.13
  189.5 0.5 fusion.39
  190.0 12.2 %scatter_fusion.2 = f32[131072]{0:T(1024)S(1)} fusion(f32[131072]{0:T(1024)S(1)} %bitcast.115, s32[2048]{0:T(1024)S(1)} %broadcast_select_fusion, f32[2048]{0:T(1024)S(1)} %bitcast.126), kind=kCustom, calls=%fused_computation.7 | custom fusion | flops 2048 | bytes 32768
  202.2 2.4 add_bitcast_fusion
  204.6 1.3 collective-permute-start.14
  205.9 5.8 %collective-permute-start.15 = (f32[1,66,128]{2,1,0:T(8,128)S(1)}, f32[1,66,128]{2,1,0:T(8,128)S(1)}, u32[]{:S(2)}, u32[]{:S(2)}) collective-permute-start(f32[1,66,128]{2,1,0:T(8,128)S(1)} %get-tuple-element.74), channel_id=1, source_target_pairs={{0,1},{1,2},{2,3},{4,5},{5,6},{6,7},{8,9},{9,10},{10,11},{12,13},{... | collective-permute-start | bytes 101384 | tf_op jit(solution)/shard_map/ppermute | solution.py:20
  211.8 1.5 collective-permute-done.15
  213.4 27.1 %reduce-scatter.2.cloned.1.call-done = f32[2,64,128]{2,1,0:T(8,128)} async-done(((f32[2,512,128]{2,1,0:T(8,128)}), f32[2,64,128]{2,1,0:T(8,128)}) %reduce-scatter.2.cloned.1.call-update) | async-done | bytes 65552 | tf_op jit(solution)/shard_map/reduce_scatter | solution.py:86
  240.4 1.6 fusion.58
  (34 shorter events, 0.4 us)
Async XLA Ops:
  7.2 13.6 %copy-start.2 = (f32[1,2,512,128]{3,2,1,0:T(8,128)S(1)}, f32[1,2,512,128]{3,2,1,0:T(8,128)}, u32[]{:S(2)}) copy-start(f32[1,2,512,128]{3,2,1,0:T(8,128)} %param.18) | copy-start | bytes 1572868
  7.2 8.7 %copy-start.5 = (f32[1,4]{1,0:T(1,128)S(1)}, f32[1,4]{1,0:T(1,128)}, u32[]{:S(2)}) copy-start(f32[1,4]{1,0:T(1,128)} %param.20) | copy-start | bytes 52
  7.2 11.4 %copy-start.3 = (s32[1,2048]{1,0:T(1,128)S(1)}, s32[1,2048]{1,0:T(1,128)}, u32[]{:S(2)}) copy-start(s32[1,2048]{1,0:T(1,128)} %param.22) | copy-start | bytes 24580
  7.2 13.5 %copy-start.1 = (f32[2,512,128]{2,1,0:T(8,128)S(1)}, f32[2,512,128]{2,1,0:T(8,128)}, u32[]{:S(2)}) copy-start(f32[2,512,128]{2,1,0:T(8,128)} %param.17) | copy-start | bytes 1572868
  7.2 233.2 %reduce-scatter.2.cloned.1.call-start = ((), (), s32[]{:S(2)}) async-start(), calls=%async_computation.1 | async-start | bytes 589824 | tf_op jit(solution)/shard_map/reduce_scatter | solution.py:86
  8.4 12.0 %collective-permute-start = (f32[1,1,512,128]{3,2,1,0:T(8,128)S(1)}, f32[1,1,512,128]{3,2,1,0:T(8,128)S(1)}, u32[]{:S(2)}, u32[]{:S(2)}) collective-permute-start(f32[1,1,512,128]{3,2,1,0:T(8,128)S(1)} %get-tuple-element.71), channel_id=1, source_target_pairs={{1,0},{2,1},{3,2},{5,4},{6,5},{7,6},{9,8},{10,9},{11,10},{13,12},{... | collective-permute-start | bytes 786440 | tf_op jit(solution)/shard_map/ppermute | solution.py:22
  9.7 11.0 %collective-permute-start.1 = (f32[1,1,512,128]{3,2,1,0:T(8,128)S(1)}, f32[1,1,512,128]{3,2,1,0:T(8,128)S(1)}, u32[]{:S(2)}, u32[]{:S(2)}) collective-permute-start(f32[1,1,512,128]{3,2,1,0:T(8,128)S(1)} %get-tuple-element.72), channel_id=1, source_target_pairs={{0,1},{1,2},{2,3},{4,5},{5,6},{6,7},{8,9},{9,10},{10,11},{12,13},{... | collective-permute-start | bytes 786440 | tf_op jit(solution)/shard_map/ppermute | solution.py:20
  24.8 12.1 %collective-permute-start.2 = (f32[1,1,512,128]{3,2,1,0:T(8,128)S(1)}, f32[1,1,512,128]{3,2,1,0:T(8,128)S(1)}, u32[]{:S(2)}, u32[]{:S(2)}) collective-permute-start(f32[1,1,512,128]{3,2,1,0:T(8,128)S(1)} %get-tuple-element.69), channel_id=1, source_target_pairs={{1,0},{2,1},{3,2},{5,4},{6,5},{7,6},{9,8},{10,9},{11,10},{13,12},{... | collective-permute-start | bytes 786440 | tf_op jit(solution)/shard_map/ppermute | solution.py:22
  26.1 11.5 %collective-permute-start.3 = (f32[1,1,512,128]{3,2,1,0:T(8,128)S(1)}, f32[1,1,512,128]{3,2,1,0:T(8,128)S(1)}, u32[]{:S(2)}, u32[]{:S(2)}) collective-permute-start(f32[1,1,512,128]{3,2,1,0:T(8,128)S(1)} %get-tuple-element.70), channel_id=1, source_target_pairs={{0,1},{1,2},{2,3},{4,5},{5,6},{6,7},{8,9},{9,10},{10,11},{12,13},{... | collective-permute-start | bytes 786440 | tf_op jit(solution)/shard_map/ppermute | solution.py:20
  41.4 7.9 %copy-start.7 = (s32[2]{0:T(128)S(1)}, s32[2]{0:T(128)}, u32[]{:S(2)}) copy-start(s32[2]{0:T(128)} %constant.172) | copy-start | bytes 28
  41.4 11.8 %collective-permute-start.4 = (f32[1,1,512,128]{3,2,1,0:T(8,128)S(1)}, f32[1,1,512,128]{3,2,1,0:T(8,128)S(1)}, u32[]{:S(2)}, u32[]{:S(2)}) collective-permute-start(f32[1,1,512,128]{3,2,1,0:T(8,128)S(1)} %get-tuple-element.67), channel_id=1, source_target_pairs={{1,0},{2,1},{3,2},{5,4},{6,5},{7,6},{9,8},{10,9},{11,10},{13,12},{... | collective-permute-start | bytes 786440 | tf_op jit(solution)/shard_map/ppermute | solution.py:22
  42.7 11.1 %collective-permute-start.5 = (f32[1,1,512,128]{3,2,1,0:T(8,128)S(1)}, f32[1,1,512,128]{3,2,1,0:T(8,128)S(1)}, u32[]{:S(2)}, u32[]{:S(2)}) collective-permute-start(f32[1,1,512,128]{3,2,1,0:T(8,128)S(1)} %get-tuple-element.68), channel_id=1, source_target_pairs={{0,1},{1,2},{2,3},{4,5},{5,6},{6,7},{8,9},{9,10},{10,11},{12,13},{... | collective-permute-start | bytes 786440 | tf_op jit(solution)/shard_map/ppermute | solution.py:20
  57.7 8.6 %copy-start.6 = (s32[2]{0:T(128)S(1)}, s32[2]{0:T(128)}, u32[]{:S(2)}) copy-start(s32[2]{0:T(128)} %constant.169) | copy-start | bytes 28
  58.5 43.9 %collective-permute-start.6 = (f32[1,1,512,128]{3,2,1,0:T(8,128)}, f32[1,1,512,128]{3,2,1,0:T(8,128)S(1)}, u32[]{:S(2)}, u32[]{:S(2)}) collective-permute-start(f32[1,1,512,128]{3,2,1,0:T(8,128)} %get-tuple-element.65), channel_id=1, source_target_pairs={{1,0},{2,1},{3,2},{5,4},{6,5},{7,6},{9,8},{10,9},{11,10},{13,12},{... | collective-permute-start | bytes 786440 | tf_op jit(solution)/shard_map/ppermute | solution.py:22
  59.8 42.6 %collective-permute-start.7 = (f32[1,1,512,128]{3,2,1,0:T(8,128)S(1)}, f32[1,1,512,128]{3,2,1,0:T(8,128)S(1)}, u32[]{:S(2)}, u32[]{:S(2)}) collective-permute-start(f32[1,1,512,128]{3,2,1,0:T(8,128)S(1)} %get-tuple-element.66), channel_id=1, source_target_pairs={{0,1},{1,2},{2,3},{4,5},{5,6},{6,7},{8,9},{9,10},{10,11},{12,13},{... | collective-permute-start | bytes 786440 | tf_op jit(solution)/shard_map/ppermute | solution.py:20
  106.2 11.8 %copy-start = (f32[1,131072]{1,0:T(1,128)}, f32[1,131072]{1,0:T(1,128)S(1)}, u32[]{:S(2)}) copy-start(f32[1,131072]{1,0:T(1,128)S(1)} %scatter-add.51) | copy-start | bytes 1572868
  106.2 11.8 %copy-start.4 = (f32[1,4,2048]{2,1,0:T(4,128)S(1)}, f32[1,4,2048]{2,1,0:T(4,128)}, u32[]{:S(2)}) copy-start(f32[1,4,2048]{2,1,0:T(4,128)} %param.23) | copy-start | bytes 98308
  130.0 10.8 %collective-permute-start.8 = (f32[1,1,512,128]{3,2,1,0:T(8,128)S(1)}, f32[1,1,512,128]{3,2,1,0:T(8,128)S(1)}, u32[]{:S(2)}, u32[]{:S(2)}) collective-permute-start(f32[1,1,512,128]{3,2,1,0:T(8,128)S(1)} %get-tuple-element.63), channel_id=1, source_target_pairs={{1,0},{2,1},{3,2},{5,4},{6,5},{7,6},{9,8},{10,9},{11,10},{13,12},{... | collective-permute-start | bytes 786440 | tf_op jit(solution)/shard_map/ppermute | solution.py:22
  131.3 9.5 %collective-permute-start.9 = (f32[1,1,512,128]{3,2,1,0:T(8,128)S(1)}, f32[1,1,512,128]{3,2,1,0:T(8,128)S(1)}, u32[]{:S(2)}, u32[]{:S(2)}) collective-permute-start(f32[1,1,512,128]{3,2,1,0:T(8,128)S(1)} %get-tuple-element.64), channel_id=1, source_target_pairs={{0,1},{1,2},{2,3},{4,5},{5,6},{6,7},{8,9},{9,10},{10,11},{12,13},{... | collective-permute-start | bytes 786440 | tf_op jit(solution)/shard_map/ppermute | solution.py:20
  153.6 10.8 %collective-permute-start.10 = (f32[1,1,512,128]{3,2,1,0:T(8,128)S(1)}, f32[1,1,512,128]{3,2,1,0:T(8,128)S(1)}, u32[]{:S(2)}, u32[]{:S(2)}) collective-permute-start(f32[1,1,512,128]{3,2,1,0:T(8,128)S(1)} %get-tuple-element.61), channel_id=1, source_target_pairs={{1,0},{2,1},{3,2},{5,4},{6,5},{7,6},{9,8},{10,9},{11,10},{13,12},{... | collective-permute-start | bytes 786440 | tf_op jit(solution)/shard_map/ppermute | solution.py:22
  154.9 10.1 %collective-permute-start.11 = (f32[1,1,512,128]{3,2,1,0:T(8,128)S(1)}, f32[1,1,512,128]{3,2,1,0:T(8,128)S(1)}, u32[]{:S(2)}, u32[]{:S(2)}) collective-permute-start(f32[1,1,512,128]{3,2,1,0:T(8,128)S(1)} %get-tuple-element.62), channel_id=1, source_target_pairs={{0,1},{1,2},{2,3},{4,5},{5,6},{6,7},{8,9},{9,10},{10,11},{12,13},{... | collective-permute-start | bytes 786440 | tf_op jit(solution)/shard_map/ppermute | solution.py:20
  177.8 11.0 %collective-permute-start.12 = (f32[1,1,512,128]{3,2,1,0:T(8,128)S(1)}, f32[1,1,512,128]{3,2,1,0:T(8,128)S(1)}, u32[]{:S(2)}, u32[]{:S(2)}) collective-permute-start(f32[1,1,512,128]{3,2,1,0:T(8,128)S(1)} %get-tuple-element.59), channel_id=1, source_target_pairs={{1,0},{2,1},{3,2},{5,4},{6,5},{7,6},{9,8},{10,9},{11,10},{13,12},{... | collective-permute-start | bytes 786440 | tf_op jit(solution)/shard_map/ppermute | solution.py:22
  179.1 10.4 %collective-permute-start.13 = (f32[1,1,512,128]{3,2,1,0:T(8,128)S(1)}, f32[1,1,512,128]{3,2,1,0:T(8,128)S(1)}, u32[]{:S(2)}, u32[]{:S(2)}) collective-permute-start(f32[1,1,512,128]{3,2,1,0:T(8,128)S(1)} %get-tuple-element.60), channel_id=1, source_target_pairs={{0,1},{1,2},{2,3},{4,5},{5,6},{6,7},{8,9},{9,10},{10,11},{12,13},{... | collective-permute-start | bytes 786440 | tf_op jit(solution)/shard_map/ppermute | solution.py:20
  204.6 7.2 %collective-permute-start.14 = (f32[1,66,128]{2,1,0:T(8,128)S(1)}, f32[1,66,128]{2,1,0:T(8,128)S(1)}, u32[]{:S(2)}, u32[]{:S(2)}) collective-permute-start(f32[1,66,128]{2,1,0:T(8,128)S(1)} %get-tuple-element.73), channel_id=1, source_target_pairs={{1,0},{2,1},{3,2},{5,4},{6,5},{7,6},{9,8},{10,9},{11,10},{13,12},{... | collective-permute-start | bytes 101384 | tf_op jit(solution)/shard_map/ppermute | solution.py:22
  205.9 7.4 %collective-permute-start.15 = (f32[1,66,128]{2,1,0:T(8,128)S(1)}, f32[1,66,128]{2,1,0:T(8,128)S(1)}, u32[]{:S(2)}, u32[]{:S(2)}) collective-permute-start(f32[1,66,128]{2,1,0:T(8,128)S(1)} %get-tuple-element.74), channel_id=1, source_target_pairs={{0,1},{1,2},{2,3},{4,5},{5,6},{6,7},{8,9},{9,10},{10,11},{12,13},{... | collective-permute-start | bytes 101384 | tf_op jit(solution)/shard_map/ppermute | solution.py:20
Sparse Core Ops, SparseCore 0:
  204.7 35.7 reduce-scatter.1
where the time goes:
time: 250 us; the launch traced here: 249 us
  other arithmetic  62.3 us (25%)
  starting transfers between devices  59.5 us (24%)
  waiting for transfers between devices  51.3 us (21%)
  local copies, waits for them, and re-layouts  50.4 us (20%)
  between operations  25.4 us (10%)
    ppermute x8, starting transfers between devices, with_halo(): lax.ppermute(tail, axis, [(i, (i + 1) % count) for i in range(ends)])  49.1 us
    unnamed x7, other arithmetic  48.5 us
    gather x4, local copies, waits for them, and re-layouts, shards(): taken = jnp.take_along_axis(misfit_flat, receiver_at, axis=1)  47.1 us
    reduce_scatter x1, waiting for transfers between devices, shards(): owned = lax.psum_scatter(image, 'shot', scatter_dimension=1, tiled=True)  27.1 us
    ppermute x8, waiting for transfers between devices, with_halo(): lax.ppermute(head, axis, [((i + 1) % count, i) for i in range(ends)])  19.6 us
    ppermute x8, starting transfers between devices, with_halo(): lax.ppermute(head, axis, [((i + 1) % count, i) for i in range(ends)])  10.3 us
  transfers between devices with their start and end apart: 17, of which 13 were waited for; matrix products, arithmetic and copies ran while one was open for 15% of the time, Pallas kernels for 0%

commit v1 on v0

v1 whole, which is shorter than its diff:
```python
import functools

import jax
import jax.numpy as jnp
from jax import lax
from jax.experimental import pallas as pl
from jax.experimental.pallas import tpu as pltpu
from jax.sharding import PartitionSpec as P

NT = 4
PRIOR_GAIN = 50.0
EDGE = 8
VMEM = pl.BlockSpec(memory_space=pltpu.VMEM)
SMEM = pl.BlockSpec(memory_space=pltpu.SMEM)
LIMIT = 48 * 1024 * 1024


def call(body, out_rows, scratch=(), in_specs=(), flops=0, moved=0):
    return pl.pallas_call(
        body,
        out_shape=[jax.ShapeDtypeStruct(s, jnp.float32) for s in out_rows],
        in_specs=list(in_specs),
        out_specs=[VMEM] * len(out_rows),
        scratch_shapes=list(scratch),
        compiler_params=pltpu.CompilerParams(vmem_limit_bytes=LIMIT),
        cost_estimate=pl.CostEstimate(flops=flops, bytes_accessed=moved, transcendentals=0),
    )


def window(field, plane, block, blocks, rows):
    first = pl.multiple_of(block * rows, 8)
    above = pl.multiple_of(jnp.maximum(first - EDGE, 0), 8)
    below = pl.multiple_of(jnp.minimum(first + rows, (blocks * rows) - EDGE), 8)
    top = field[plane, pl.ds(above, EDGE), :]
    bottom = field[plane, pl.ds(below, EDGE), :]
    top = jnp.where(block > 0, top, 0.0)
    bottom = jnp.where(block < blocks - 1, bottom, 0.0)
    return top, field[plane, pl.ds(first, rows), :], bottom


def pack(blocks, planes, rows, *refs):
    fields, outs = refs[: len(refs) - blocks], refs[len(refs) - blocks :]
    dom = lax.axis_index("dom")
    tall = rows + 2 * EDGE
    for s in range(blocks):
        block = lax.bitwise_xor(dom, s)
        for f, field in enumerate(fields):
            for p in range(planes):
                top, core, bottom = window(field, p, block, blocks, rows)
                at = (f * planes + p) * tall
                outs[s][at : at + EDGE, :] = top
                outs[s][at + EDGE : at + EDGE + rows, :] = core
                outs[s][at + EDGE + rows : at + tall, :] = bottom


def spread(depth, ny, rows, count, cells_ref, observed_ref, count_ref, *rest):
    outs, (value, picks) = rest[:NT], rest[NT:]
    tall = rows + 2 * EDGE
    planes = count_ref.shape[0] // tall
    dom = lax.axis_index("dom")
    cells = cells_ref[...]
    line = cells // depth
    x = line // ny
    y = line - x * ny - (dom * rows - EDGE)
    row = jnp.where((y >= 0) & (y < tall), x * tall + y, -1)
    lane = (cells - line * depth).astype(jnp.float32)
    picks[...] = row
    stack = jnp.concatenate([lane, observed_ref[0], jnp.zeros((3, count), jnp.float32)], axis=0)
    columns = 128
    for j in range(count // columns):
        turned = stack[:, j * columns : (j + 1) * columns].T
        hot = lax.broadcasted_iota(jnp.int32, (columns, depth), 1).astype(jnp.float32) == turned[:, 0:1]
        at = slice(j * columns, (j + 1) * columns)
        value[at, 0:depth] = jnp.where(hot, 1.0, 0.0).astype(jnp.bfloat16)
        for n in range(NT):
            left = jnp.where(hot, turned[:, n + 1 : n + 2], 0.0)
            for part in range(3):
                piece = left.astype(jnp.bfloat16)
                left = left - piece.astype(jnp.float32)
                to = (1 + 3 * n + part) * depth
                value[at, to : to + depth] = piece
    some = tall * 2

    def chunk(i, _):
        first = pl.multiple_of(i * some, 8)
        ids = lax.broadcasted_iota(jnp.int32, (some, count), 0) + first
        hot = jnp.where(ids == picks[...], 1.0, 0.0).astype(jnp.bfloat16)
        out = jnp.dot(hot, value[...], preferred_element_type=jnp.float32)
        count_ref[pl.ds(first, some), :] = out[:, 0:depth]
        for n in range(NT):
            at = (1 + 3 * n) * depth
            total = out[:, at + depth : at + 2 * depth] + out[:, at + 2 * depth : at + 3 * depth]
            outs[n][pl.ds(first, some), :] = out[:, at : at + depth] + total
        return 0

    lax.fori_loop(0, planes // 2, chunk, 0)


def sixth(field, x, first, some, low, high):
    mid = field[x, first : first + some, :]
    total = field[x + 1, first : first + some, :] + field[x - 1, first : first + some, :]
    total = total + (field[x, first + 1 : first + some + 1, :] + field[x, first - 1 : first + some - 1, :])
    up = jnp.where(high, 0.0, pltpu.roll(mid, mid.shape[1] - 1, 1))
    down = jnp.where(low, 0.0, pltpu.roll(mid, 1, 1))
    return total + (up + down), mid


def steps(blocks, planes, rows, depth, ny, *refs):
    refs = list(refs)
    source, wavelet = refs[:2]
    early = refs[2 : 2 + blocks]
    late = refs[2 + blocks : 2 + 2 * blocks]
    count = refs[2 + 2 * blocks]
    heard = refs[3 + 2 * blocks : 3 + NT + 2 * blocks]
    refs = refs[3 + NT + 2 * blocks :]
    turned, (keep, give) = refs[:blocks], refs[blocks : blocks + 2]
    refs = refs[blocks + 2 :]
    wave, refs = refs[: NT + 1], refs[NT + 1 :]
    lap, refs = refs[:NT], refs[NT:]
    before, model, image = refs[:3]
    adjoint = refs[3:6]
    weighted = refs[6:8]
    tall = rows + 2 * EDGE
    nx = blocks * planes
    dom = lax.axis_index("dom")
    shot = lax.axis_index("shot")
    core = lax.rem(shot, 2)

    zero_plane = jnp.zeros((tall + 16, depth), jnp.float32)
    zero_edge = jnp.zeros((8, depth), jnp.float32)
    for field in (*wave, model, *weighted):
        field[0] = zero_plane
        field[nx + 1] = zero_plane
        for x in range(1, nx + 1):
            field[x, 0:8, :] = zero_edge
            field[x, 8 + tall : 16 + tall, :] = zero_edge
    for s in range(blocks):
        first = planes * lax.bitwise_xor(dom, s)
        for p in range(planes):
            at = slice(p * tall, (p + 1) * tall)
            wave[0][1 + first + p, 8 : 8 + tall, :] = early[s][at, :]
            more = slice((planes + p) * tall, (planes + p + 1) * tall)
            model[1 + first + p, 8 : 8 + tall, :] = early[s][more, :]
            before[first + p] = late[s][at, :]

    some = 48
    lanes = lax.broadcasted_iota(jnp.int32, (some, depth), 1)
    low, high = lanes == 0, lanes == depth - 1

    line = source[0] // depth
    spot = source[0] - line * depth
    sx = line // ny
    sy = line - sx * ny - (dom * rows - EDGE)
    source_here = (sy >= 0) & (sy < tall)
    sy = jnp.clip(sy, 0, tall - 1)
    source_lane = lax.broadcasted_iota(jnp.int32, (1, depth), 1) == spot

    for n in range(NT):

        def forward(x, _, n=n):
            for a in range(0, tall, some):
                total, mid = sixth(wave[n], x + 1, 8 + a, some, low, high)
                bend = total - 6.0 * mid
                lap[n][x, a : a + some, :] = bend
                old = before[x, a : a + some, :] if n == 0 else wave[n - 1][x + 1, 8 + a : 8 + a + some, :]
                new = 2.0 * mid - old + model[x + 1, 8 + a : 8 + a + some, :] * bend
                wave[n + 1][x + 1, 8 + a : 8 + a + some, :] = new
            return 0

        lax.fori_loop(0, nx, forward, 0)

        @pl.when(source_here)
        def _():
            row = wave[n + 1][sx + 1, pl.ds(8 + sy, 1), :]
            wave[n + 1][sx + 1, pl.ds(8 + sy, 1), :] = row + jnp.where(source_lane, wavelet[0, n], 0.0)

    for s in range(blocks):
        first = planes * lax.bitwise_xor(dom, s)
        for p in range(planes):
            turned[s][p * rows : (p + 1) * rows, :] = wave[NT][1 + first + p, 8 + EDGE : 8 + EDGE + rows, :]

    for level in range(NT, 0, -1):
        now, after, last = adjoint[level % 3], adjoint[(level + 1) % 3], adjoint[(level + 2) % 3]
        push, pull = weighted[level % 2], weighted[(level + 1) % 2]

        def backward(x, _, level=level, now=now, after=after, last=last, push=push, pull=pull):
            for a in range(0, tall, some):
                at = pl.ds(pl.multiple_of(x * tall + a, 8), some)
                miss = count[at, :] * wave[level][x + 1, 8 + a : 8 + a + some, :] - heard[level - 1][at, :]
                if level < NT:
                    total, mid = sixth(pull, x + 1, 8 + a, some, low, high)
                    miss = miss + 2.0 * after[x, a : a + some, :] + (total - 6.0 * mid)
                if level < NT - 1:
                    miss = miss - last[x, a : a + some, :]
                if level > 1:
                    now[x, a : a + some, :] = miss
                    push[x + 1, 8 + a : 8 + a + some, :] = miss * model[x + 1, 8 + a : 8 + a + some, :]
                part = miss * lap[level - 1][x, a : a + some, :]
                if level < NT:
                    part = part + image[x, a : a + some, :]
                if level == 1:
                    total, mid = sixth(model, x + 1, 8 + a, some, low, high)
                    score = (total / 6.0 - mid) * PRIOR_GAIN
                    part = part / NT - jnp.where(shot == 0, score, 0.0)
                image[x, a : a + some, :] = part
            return 0

        lax.fori_loop(0, nx, backward, 0)

    half = rows // 2
    mine = pl.multiple_of(EDGE + core * half, 8)
    mates = pl.multiple_of(EDGE + (1 - core) * half, 8)
    for x in range(nx):
        keep[x * half : (x + 1) * half, :] = image[x, pl.ds(mine, half), :]
        give[x * half : (x + 1) * half, :] = image[x, pl.ds(mates, half), :]


def cut(blocks, keep, got, *outs):
    dom = lax.axis_index("dom")
    size = outs[0].shape[0]
    for s in range(blocks):
        at = pl.ds(pl.multiple_of(lax.bitwise_xor(dom, s) * size, 8), size)
        outs[s][...] = keep[at, :] + got[at, :]


def sort(blocks, *refs):
    came, outs, held = refs[:blocks], refs[blocks : 2 * blocks], refs[2 * blocks]
    dom, pair = lax.axis_index("dom"), lax.axis_index("shot") // 2
    for s in range(blocks):
        held[lax.bitwise_xor(dom, s)] = came[s][...]
    for s in range(blocks):
        outs[s][...] = held[lax.bitwise_xor(pair, s)]


def add(planes, *refs):
    out = refs[-1]
    size = out.shape[1]
    for p in range(planes):
        total = refs[0][p * size : (p + 1) * size, :]
        for ref in refs[1:-1]:
            total = total + ref[p * size : (p + 1) * size, :]
        out[p] = total


def join(planes, rows, *refs):
    out = refs[-1]
    dom = lax.axis_index("dom")
    for s, ref in enumerate(refs[:-1]):
        at = pl.ds(pl.multiple_of(lax.bitwise_xor(dom, s) * rows, 8), rows)
        for p in range(planes):
            out[p, at, :] = ref[p * rows : (p + 1) * rows, :]


def shards(kappa, wave_now, wave_before, wavelet, source_cell, receiver_cells, observed):
    shots, blocks = lax.axis_size("shot"), lax.axis_size("dom")
    _, planes, ny, depth = wave_now.shape
    rows = ny // blocks
    tall = rows + 2 * EDGE
    nx = planes * blocks
    listed = receiver_cells.shape[1]

    def across(array, to):
        pairs = []
        for shot in range(shots):
            for dom in range(blocks):
                there = to(shot, dom)
                pairs.append((shot * blocks + dom, there[0] * blocks + there[1]))
        return lax.ppermute(array, ("shot", "dom"), pairs)

    def over_dom(arrays):
        return [arrays[0]] + [across(arrays[s], lambda shot, dom, s=s: (shot, dom ^ s)) for s in range(1, blocks)]

    def over_pairs(arrays):
        return [arrays[0]] + [across(arrays[s], lambda shot, dom, s=s: (shot ^ (2 * s), dom)) for s in range(1, blocks)]

    packed = functools.partial(pack, blocks, planes, rows)
    now, before = wave_now[0], wave_before[0]
    early = call(packed, [(2 * planes * tall, depth)] * blocks, in_specs=[VMEM] * 2)(now, kappa)
    late = call(packed, [(planes * tall, depth)] * blocks, in_specs=[VMEM])(before)
    early, late = over_dom(early), over_dom(late)

    wide = (1 + 3 * NT) * depth
    heard = call(
        functools.partial(spread, depth, ny, rows, listed),
        [(nx * tall, depth)] * (1 + NT),
        in_specs=[VMEM, VMEM],
        scratch=[pltpu.VMEM((listed, wide), jnp.bfloat16), pltpu.VMEM((1, listed), jnp.int32)],
        flops=2 * nx * tall * listed * wide,
        moved=4 * (1 + NT) * nx * tall * depth,
    )(receiver_cells, observed)

    padded = pltpu.VMEM((nx + 2, tall + 16, depth), jnp.float32)
    plain = pltpu.VMEM((nx, tall, depth), jnp.float32)
    half = rows // 2
    *turned, keep, give = call(
        functools.partial(steps, blocks, planes, rows, depth, ny),
        [(planes * rows, depth)] * blocks + [(nx * half, depth)] * 2,
        in_specs=[SMEM, SMEM] + [VMEM] * (2 * blocks + 1 + NT),
        scratch=[padded] * (NT + 1) + [plain] * NT + [plain, padded, plain] + [plain] * 3 + [padded] * 2,
        flops=2 * NT * 20 * nx * tall * depth,
        moved=4 * 10 * nx * tall * depth,
    )(source_cell, wavelet, *early, *late, *heard)

    got = across(give, lambda shot, dom: (shot ^ 1, dom))
    pieces = call(functools.partial(cut, blocks), [(planes * half, depth)] * blocks, in_specs=[VMEM] * 2)(keep, got)
    pieces = over_dom(pieces)
    turned = over_dom(turned)
    pieces = call(
        functools.partial(sort, blocks),
        [(planes * half, depth)] * blocks,
        in_specs=[VMEM] * blocks,
        scratch=[pltpu.VMEM((blocks, planes * half, depth), jnp.float32)],
    )(*pieces)
    pieces = over_pairs(pieces)
    (wave_next,) = call(functools.partial(join, planes, rows), [(planes, ny, depth)], in_specs=[VMEM] * blocks)(*turned)
    (total,) = call(functools.partial(add, planes), [(planes, half, depth)], in_specs=[VMEM] * blocks)(*pieces)
    return total, wave_next[None]


def solution(mesh):
    return jax.shard_map(
        shards,
        mesh=mesh,
        in_specs=(
            P("dom", None, None),
            P("shot", "dom", None, None),
            P("shot", "dom", None, None),
            P("shot", None),
            P("shot"),
            P("shot", None),
            P("shot", None, None),
        ),
        out_specs=(P("dom", "shot", None), P("shot", "dom", None, None)),
        check_vma=False,
    )
```

time: 250 us -> 57.6 us (0.23)
  other arithmetic: 62.3 us -> 0 us
  local copies, waits for them, and re-layouts: 50.4 us -> 2.74 us
  waiting for transfers between devices: 51.3 us -> 11.2 us
  starting transfers between devices: 59.5 us -> 21.1 us
  between operations: 25.4 us -> 1.37 us
  Pallas kernels: 0 us -> 20.9 us
    unnamed x7 -> x0, other arithmetic: 48.5 us -> none
    gather x4 -> x0, local copies, waits for them, and re-layouts: 47.1 us -> none  [shards(): taken = jnp.take_along_axis(misfit_flat, receiver_at, axis=1)]
    ppermute x16, starting transfers between devices: 59.5 us -> 21.1 us  [across(): return lax.ppermute(array, ('shot', 'dom'), pairs)]
    reduce_scatter x1 -> x0, waiting for transfers between devices: 27.1 us -> none  [shards(): owned = lax.psum_scatter(image, 'shot', scatter_dimension=1, tiled=True)]
    pallas_call x0 -> x8, Pallas kernels: none -> 20.9 us  [the longest x1 11.3 us: shards(): call(functools.partial(spread, depth, ny, rows, listed), [(nx * tall, dep...]
    ppermute x16, waiting for transfers between devices: 24.2 us -> 11.2 us  [across(): return lax.ppermute(array, ('shot', 'dom'), pairs)]
    add x10 -> x0, other arithmetic: 10.2 us -> none  [the longest x4 4.84 us: shards(): after = 2.0 * now - before + kappa * lap]
    slice x10 -> x0, local copies, waits for them, and re-layouts: 2.76 us -> none  [the longest x8 2.09 us: with_halo(): head = lax.slice_in_dim(cells, 0, width, axis=dim)]
  transfers between devices with their start and end apart: 17 -> 16, of which waited for: 13 -> 5; matrix products, arithmetic and copies ran while one was open for 15% -> 0% of each run, Pallas kernels for 0% -> 21%
where the time goes in v1:
time: 57.6 us; the launch traced here: 57.3 us
  starting transfers between devices  21.1 us (37%)
  Pallas kernels  20.9 us (36%)
  waiting for transfers between devices  11.2 us (19%)
  local copies, waits for them, and re-layouts  2.74 us (5%)
  between operations  1.37 us (2%)
    ppermute x16, starting transfers between devices, across(): return lax.ppermute(array, ('shot', 'dom'), pairs)  21.1 us
    pallas_call x1, Pallas kernels, shards(): call(functools.partial(spread, depth, ny, rows, listed), [(nx * tall, dep...  11.3 us
    ppermute x16, waiting for transfers between devices, across(): return lax.ppermute(array, ('shot', 'dom'), pairs)  11.2 us
    pallas_call x1, Pallas kernels, shards(): call(functools.partial(steps, blocks, planes, rows, depth, ny), [(planes...  7.91 us
    unnamed x12, local copies, waits for them, and re-layouts  2.74 us
  transfers between devices with their start and end apart: 16, of which 5 were waited for; matrix products, arithmetic and copies ran while one was open for 0% of the time, Pallas kernels for 21%

profile of v1, /device:TPU:0, one launch (start us, length us, event | category | flops | bytes accessed | tf_op | source)
XLA Modules:
  0.0 57.3 jit_solution(11912638003139150879)
XLA Ops:
  0.6 0.0 copy-start
  0.6 1.0 %copy-done = f32[1,2,512,128]{3,2,1,0:T(8,128)S(1)} copy-done((f32[1,2,512,128]{3,2,1,0:T(8,128)S(1)}, f32[1,2,512,128]{3,2,1,0:T(8,128)}, u32[]{:S(2)}) %copy-start) | copy-done | bytes 524312
  1.7 0.0 copy-start.1
  1.7 3.0 %collective-permute-start.3 = (f32[288,128]{1,0:T(8,128)S(1)}, f32[288,128]{1,0:T(8,128)S(1)}, u32[]{:S(2)}, u32[]{:S(2)}) collective-permute-start(f32[288,128]{1,0:T(8,128)S(1)} %get-tuple-element.34), channel_id=1, source_target_pairs={{0,1},{1,0},{2,3},{3,2},{4,5},{5,4},{6,7},{7,6},{8,9},{9,8},{10,11... | collective-permute-start | bytes 442376 | tf_op jit(solution)/shard_map/ppermute | solution.py:268
  4.7 1.5 %collective-permute-start.4 = (f32[288,128]{1,0:T(8,128)S(1)}, f32[288,128]{1,0:T(8,128)S(1)}, u32[]{:S(2)}, u32[]{:S(2)}) collective-permute-start(f32[288,128]{1,0:T(8,128)S(1)} %get-tuple-element.35), channel_id=1, source_target_pairs={{0,2},{1,3},{2,0},{3,1},{4,6},{5,7},{6,4},{7,5},{8,10},{9,11},{10,... | collective-permute-start | bytes 442376 | tf_op jit(solution)/shard_map/ppermute | solution.py:268
  6.2 0.0 collective-permute-start.5
  6.3 0.0 copy-done.1
  6.3 0.0 copy-start.2
  6.3 1.0 %copy-done.2 = f32[2,512,128]{2,1,0:T(8,128)S(1)} copy-done((f32[2,512,128]{2,1,0:T(8,128)S(1)}, f32[2,512,128]{2,1,0:T(8,128)}, u32[]{:S(2)}) %copy-start.2) | copy-done | bytes 524312
  7.3 0.0 copy-start.4
  7.3 0.0 copy-start.5
  7.3 0.1 shard_map.86
  7.4 2.0 %collective-permute-start = (f32[576,128]{1,0:T(8,128)S(1)}, f32[576,128]{1,0:T(8,128)S(1)}, u32[]{:S(2)}, u32[]{:S(2)}) collective-permute-start(f32[576,128]{1,0:T(8,128)S(1)} %get-tuple-element.30), channel_id=1, source_target_pairs={{0,1},{1,0},{2,3},{3,2},{4,5},{5,4},{6,7},{7,6},{8,9},{9,8},{10,11... | collective-permute-start | bytes 884744 | tf_op jit(solution)/shard_map/ppermute | solution.py:268
  9.4 1.5 %collective-permute-start.1 = (f32[576,128]{1,0:T(8,128)S(1)}, f32[576,128]{1,0:T(8,128)S(1)}, u32[]{:S(2)}, u32[]{:S(2)}) collective-permute-start(f32[576,128]{1,0:T(8,128)S(1)} %get-tuple-element.31), channel_id=1, source_target_pairs={{0,2},{1,3},{2,0},{3,1},{4,6},{5,7},{6,4},{7,5},{8,10},{9,11},{10,... | collective-permute-start | bytes 884744 | tf_op jit(solution)/shard_map/ppermute | solution.py:268
  10.9 0.0 collective-permute-done.3.refs_7_
  10.9 1.5 %collective-permute-start.2 = (f32[576,128]{1,0:T(8,128)S(1)}, f32[576,128]{1,0:T(8,128)S(1)}, u32[]{:S(2)}, u32[]{:S(2)}) collective-permute-start(f32[576,128]{1,0:T(8,128)S(1)} %get-tuple-element.32), channel_id=1, source_target_pairs={{0,3},{1,2},{2,1},{3,0},{4,7},{5,6},{6,5},{7,4},{8,11},{9,10},{10,... | collective-permute-start | bytes 884744 | tf_op jit(solution)/shard_map/ppermute | solution.py:268
  12.4 0.0 copy-done.4
  12.4 0.0 copy-done.5
  12.4 11.3 %shard_map.88 = (f32[1152,128]{1,0:T(8,128)S(1)}, f32[1152,128]{1,0:T(8,128)S(1)}, f32[1152,128]{1,0:T(8,128)S(1)}, f32[1152,128]{1,0:T(8,128)S(1)}, f32[1152,128]{1,0:T(8,128)S(1)}) custom-call(s32[1,2048]{1,0:T(1,128)S(1)} %copy-done.5, f32[1,4,2048]{2,1,0:T(4,128)S(1)} %copy-done.4), custom_call_target="tpu_custom_call" | custom-call | flops 7851737088 | bytes 2949120 | tf_op jit(solution)/shard_map/pallas_call | solution.py:283
  24.4 0.0 collective-permute-done.4.refs_8_
  24.4 0.0 collective-permute-done.5.refs_9_
  24.4 0.0 collective-permute-done.refs_3_
  24.4 1.4 %collective-permute-done.1.refs_4_ = f32[576,128]{1,0:T(8,128)S(1)} collective-permute-done((f32[576,128]{1,0:T(8,128)S(1)}, f32[576,128]{1,0:T(8,128)S(1)}, u32[]{:S(2)}, u32[]{:S(2)}) %collective-permute-start.1) | collective-permute-done | bytes 294944 | tf_op jit(solution)/shard_map/ppermute | solution.py:268
  25.8 0.0 collective-permute-done.2.refs_5_
  25.8 0.0 copy-start.3
  25.8 0.7 %copy-done.3 = f32[1,4]{1,0:T(1,128)S(1)} copy-done((f32[1,4]{1,0:T(1,128)S(1)}, f32[1,4]{1,0:T(1,128)}, u32[]{:S(2)}) %copy-start.3) | copy-done | bytes 40
  26.5 7.9 %shard_map.89 = (f32[256,128]{1,0:T(8,128)S(1)}, f32[256,128]{1,0:T(8,128)S(1)}, f32[256,128]{1,0:T(8,128)S(1)}, f32[256,128]{1,0:T(8,128)S(1)}, f32[512,128]{1,0:T(8,128)S(1)}, /*index=5*/f32[512,128]{1,0:T(8,128)S(1)}) custom-call(s32[1]{0:T(128)S(6)} %copy.9.refs_0_, f32[1,4]{1,0:T(1,128)S(1)} %copy-done.3, f32[576,128]{1,0:T(8,128)S(1)} %get-tuple-element.29.refs_2_, ...), custom_call_target="tpu_custom_call" | custom-call | flops 23592960 | bytes 5898240 | tf_op jit(solution)/shard_map/pallas_call | solution.py:295
  34.4 0.1 collective-permute-start.6
  34.5 1.5 %collective-permute-done.6.got = f32[512,128]{1,0:T(8,128)S(1)} collective-permute-done((f32[512,128]{1,0:T(8,128)S(1)}, f32[512,128]{1,0:T(8,128)S(1)}, u32[]{:S(2)}, u32[]{:S(2)}) %collective-permute-start.6) | collective-permute-done | bytes 262176 | tf_op jit(solution)/shard_map/ppermute | solution.py:268
  36.0 1.3 %collective-permute-start.7 = (f32[128,128]{1,0:T(8,128)S(1)}, f32[128,128]{1,0:T(8,128)S(1)}, u32[]{:S(2)}, u32[]{:S(2)}) collective-permute-start(f32[128,128]{1,0:T(8,128)S(1)} %get-tuple-element.45), channel_id=1, source_target_pairs={{0,1},{1,0},{2,3},{3,2},{4,5},{5,4},{6,7},{7,6},{8,9},{9,8},{10,11... | collective-permute-start | bytes 196616 | tf_op jit(solution)/shard_map/ppermute | solution.py:268
  37.3 0.8 %collective-permute-start.13 = (f32[256,128]{1,0:T(8,128)S(1)}, f32[256,128]{1,0:T(8,128)S(1)}, u32[]{:S(2)}, u32[]{:S(2)}) collective-permute-start(f32[256,128]{1,0:T(8,128)S(1)} %get-tuple-element.53), channel_id=1, source_target_pairs={{0,1},{1,0},{2,3},{3,2},{4,5},{5,4},{6,7},{7,6},{8,9},{9,8},{10,11... | collective-permute-start | bytes 393224 | tf_op jit(solution)/shard_map/ppermute | solution.py:268
  38.1 1.5 %collective-permute-start.8 = (f32[128,128]{1,0:T(8,128)S(1)}, f32[128,128]{1,0:T(8,128)S(1)}, u32[]{:S(2)}, u32[]{:S(2)}) collective-permute-start(f32[128,128]{1,0:T(8,128)S(1)} %get-tuple-element.46), channel_id=1, source_target_pairs={{0,2},{1,3},{2,0},{3,1},{4,6},{5,7},{6,4},{7,5},{8,10},{9,11},{10,... | collective-permute-start | bytes 196616 | tf_op jit(solution)/shard_map/ppermute | solution.py:268
  39.7 1.2 %collective-permute-start.9 = (f32[128,128]{1,0:T(8,128)S(1)}, f32[128,128]{1,0:T(8,128)S(1)}, u32[]{:S(2)}, u32[]{:S(2)}) collective-permute-start(f32[128,128]{1,0:T(8,128)S(1)} %get-tuple-element.47), channel_id=1, source_target_pairs={{0,3},{1,2},{2,1},{3,0},{4,7},{5,6},{6,5},{7,4},{8,11},{9,10},{10,... | collective-permute-start | bytes 196616 | tf_op jit(solution)/shard_map/ppermute | solution.py:268
  40.8 0.8 %collective-permute-start.14 = (f32[256,128]{1,0:T(8,128)S(1)}, f32[256,128]{1,0:T(8,128)S(1)}, u32[]{:S(2)}, u32[]{:S(2)}) collective-permute-start(f32[256,128]{1,0:T(8,128)S(1)} %get-tuple-element.54), channel_id=1, source_target_pairs={{0,2},{1,3},{2,0},{3,1},{4,6},{5,7},{6,4},{7,5},{8,10},{9,11},{10,... | collective-permute-start | bytes 393224 | tf_op jit(solution)/shard_map/ppermute | solution.py:268
  41.7 0.0 collective-permute-done.7.refs_1_
  41.7 1.4 %collective-permute-start.15 = (f32[256,128]{1,0:T(8,128)S(1)}, f32[256,128]{1,0:T(8,128)S(1)}, u32[]{:S(2)}, u32[]{:S(2)}) collective-permute-start(f32[256,128]{1,0:T(8,128)S(1)} %get-tuple-element.55), channel_id=1, source_target_pairs={{0,3},{1,2},{2,1},{3,0},{4,7},{5,6},{6,5},{7,4},{8,11},{9,10},{10,... | collective-permute-start | bytes 393224 | tf_op jit(solution)/shard_map/ppermute | solution.py:268
  43.1 0.0 collective-permute-done.8.refs_2_
  43.1 3.2 %collective-permute-done.9.refs_3_ = f32[128,128]{1,0:T(8,128)S(1)} collective-permute-done((f32[128,128]{1,0:T(8,128)S(1)}, f32[128,128]{1,0:T(8,128)S(1)}, u32[]{:S(2)}, u32[]{:S(2)}) %collective-permute-start.9) | collective-permute-done | bytes 65568 | tf_op jit(solution)/shard_map/ppermute | solution.py:268
  46.4 1.7 %collective-permute-start.10 = (f32[128,128]{1,0:T(8,128)S(1)}, f32[128,128]{1,0:T(8,128)S(1)}, u32[]{:S(2)}, u32[]{:S(2)}) collective-permute-start(f32[128,128]{1,0:T(8,128)S(1)} %get-tuple-element.49), channel_id=1, source_target_pairs={{0,8},{1,9},{2,10},{3,11},{4,12},{5,13},{6,14},{7,15},{8,0},{9,1},... | collective-permute-start | bytes 196616 | tf_op jit(solution)/shard_map/ppermute | solution.py:268
  48.0 2.6 %collective-permute-start.11 = (f32[128,128]{1,0:T(8,128)S(1)}, f32[128,128]{1,0:T(8,128)S(1)}, u32[]{:S(2)}, u32[]{:S(2)}) collective-permute-start(f32[128,128]{1,0:T(8,128)S(1)} %get-tuple-element.50), channel_id=1, source_target_pairs={{0,16},{1,17},{2,18},{3,19},{4,20},{5,21},{6,22},{7,23},{8,24},{9,... | collective-permute-start | bytes 196616 | tf_op jit(solution)/shard_map/ppermute | solution.py:268
  50.6 0.0 collective-permute-done.13.refs_1_
  50.6 0.2 collective-permute-start.12
  50.8 0.0 collective-permute-done.14.refs_2_
  50.8 0.0 collective-permute-done.15.refs_3_
  50.8 0.8 %shard_map.93 = f32[2,512,128]{2,1,0:T(8,128)} custom-call(f32[256,128]{1,0:T(8,128)S(1)} %get-tuple-element.52.refs_0_, f32[256,128]{1,0:T(8,128)S(1)} %collective-permute-done.13.refs_1_, f32[256,128]{1,0:T(8,128)S(1)} %collective-permute-done.14.refs_2_, f32[256,128]{1,0:T(8,128)S(1)} %collective-permute-done.15.refs_3_), custom_call_target="tpu_custom_call" | custom-call | tf_op jit(solution)/shard_map/pallas_call | solution.py:315
  51.7 0.0 collective-permute-done.10.refs_1_
  51.7 2.9 %collective-permute-done.11.refs_2_ = f32[128,128]{1,0:T(8,128)S(1)} collective-permute-done((f32[128,128]{1,0:T(8,128)S(1)}, f32[128,128]{1,0:T(8,128)S(1)}, u32[]{:S(2)}, u32[]{:S(2)}) %collective-permute-start.11) | collective-permute-done | bytes 65568 | tf_op jit(solution)/shard_map/ppermute | solution.py:268
  54.6 2.1 %collective-permute-done.12.refs_3_ = f32[128,128]{1,0:T(8,128)S(1)} collective-permute-done((f32[128,128]{1,0:T(8,128)S(1)}, f32[128,128]{1,0:T(8,128)S(1)}, u32[]{:S(2)}, u32[]{:S(2)}) %collective-permute-start.12) | collective-permute-done | bytes 65568 | tf_op jit(solution)/shard_map/ppermute | solution.py:268
  56.7 0.6 %shard_map.92 = f32[2,64,128]{2,1,0:T(8,128)} custom-call(f32[128,128]{1,0:T(8,128)S(1)} %get-tuple-element.48.refs_0_, f32[128,128]{1,0:T(8,128)S(1)} %collective-permute-done.10.refs_1_, f32[128,128]{1,0:T(8,128)S(1)} %collective-permute-done.11.refs_2_, f32[128,128]{1,0:T(8,128)S(1)} %collective-permute-done.12.refs_3_), custom_call_target="tpu_custom_call" | custom-call | tf_op jit(solution)/shard_map/pallas_call | solution.py:316
  (3 shorter events, 0.1 us)
Async XLA Ops:
  0.6 1.0 %copy-start = (f32[1,2,512,128]{3,2,1,0:T(8,128)S(1)}, f32[1,2,512,128]{3,2,1,0:T(8,128)}, u32[]{:S(2)}) copy-start(f32[1,2,512,128]{3,2,1,0:T(8,128)} %param.9) | copy-start | bytes 1572868
  1.7 4.6 %copy-start.1 = (f32[1,2,512,128]{3,2,1,0:T(8,128)S(1)}, f32[1,2,512,128]{3,2,1,0:T(8,128)}, u32[]{:S(2)}) copy-start(f32[1,2,512,128]{3,2,1,0:T(8,128)} %param.8) | copy-start | bytes 1572868
  1.7 9.2 %collective-permute-start.3 = (f32[288,128]{1,0:T(8,128)S(1)}, f32[288,128]{1,0:T(8,128)S(1)}, u32[]{:S(2)}, u32[]{:S(2)}) collective-permute-start(f32[288,128]{1,0:T(8,128)S(1)} %get-tuple-element.34), channel_id=1, source_target_pairs={{0,1},{1,0},{2,3},{3,2},{4,5},{5,4},{6,7},{7,6},{8,9},{9,8},{10,11... | collective-permute-start | bytes 442376 | tf_op jit(solution)/shard_map/ppermute | solution.py:268
  4.7 19.6 %collective-permute-start.4 = (f32[288,128]{1,0:T(8,128)S(1)}, f32[288,128]{1,0:T(8,128)S(1)}, u32[]{:S(2)}, u32[]{:S(2)}) collective-permute-start(f32[288,128]{1,0:T(8,128)S(1)} %get-tuple-element.35), channel_id=1, source_target_pairs={{0,2},{1,3},{2,0},{3,1},{4,6},{5,7},{6,4},{7,5},{8,10},{9,11},{10,... | collective-permute-start | bytes 442376 | tf_op jit(solution)/shard_map/ppermute | solution.py:268
  6.2 18.1 %collective-permute-start.5 = (f32[288,128]{1,0:T(8,128)S(1)}, f32[288,128]{1,0:T(8,128)S(1)}, u32[]{:S(2)}, u32[]{:S(2)}) collective-permute-start(f32[288,128]{1,0:T(8,128)S(1)} %get-tuple-element.36), channel_id=1, source_target_pairs={{0,3},{1,2},{2,1},{3,0},{4,7},{5,6},{6,5},{7,4},{8,11},{9,10},{10,... | collective-permute-start | bytes 442376 | tf_op jit(solution)/shard_map/ppermute | solution.py:268
  6.3 1.0 %copy-start.2 = (f32[2,512,128]{2,1,0:T(8,128)S(1)}, f32[2,512,128]{2,1,0:T(8,128)}, u32[]{:S(2)}) copy-start(f32[2,512,128]{2,1,0:T(8,128)} %refs_1_.2) | copy-start | bytes 1572868
  7.3 5.1 %copy-start.4 = (f32[1,4,2048]{2,1,0:T(4,128)S(1)}, f32[1,4,2048]{2,1,0:T(4,128)}, u32[]{:S(2)}) copy-start(f32[1,4,2048]{2,1,0:T(4,128)} %observed_ref.1) | copy-start | bytes 98308
  7.3 5.1 %copy-start.5 = (s32[1,2048]{1,0:T(1,128)S(1)}, s32[1,2048]{1,0:T(1,128)}, u32[]{:S(2)}) copy-start(s32[1,2048]{1,0:T(1,128)} %cells_ref.1) | copy-start | bytes 24580
  7.4 17.0 %collective-permute-start = (f32[576,128]{1,0:T(8,128)S(1)}, f32[576,128]{1,0:T(8,128)S(1)}, u32[]{:S(2)}, u32[]{:S(2)}) collective-permute-start(f32[576,128]{1,0:T(8,128)S(1)} %get-tuple-element.30), channel_id=1, source_target_pairs={{0,1},{1,0},{2,3},{3,2},{4,5},{5,4},{6,7},{7,6},{8,9},{9,8},{10,11... | collective-permute-start | bytes 884744 | tf_op jit(solution)/shard_map/ppermute | solution.py:268
  9.4 16.4 %collective-permute-start.1 = (f32[576,128]{1,0:T(8,128)S(1)}, f32[576,128]{1,0:T(8,128)S(1)}, u32[]{:S(2)}, u32[]{:S(2)}) collective-permute-start(f32[576,128]{1,0:T(8,128)S(1)} %get-tuple-element.31), channel_id=1, source_target_pairs={{0,2},{1,3},{2,0},{3,1},{4,6},{5,7},{6,4},{7,5},{8,10},{9,11},{10,... | collective-permute-start | bytes 884744 | tf_op jit(solution)/shard_map/ppermute | solution.py:268
  10.9 14.9 %collective-permute-start.2 = (f32[576,128]{1,0:T(8,128)S(1)}, f32[576,128]{1,0:T(8,128)S(1)}, u32[]{:S(2)}, u32[]{:S(2)}) collective-permute-start(f32[576,128]{1,0:T(8,128)S(1)} %get-tuple-element.32), channel_id=1, source_target_pairs={{0,3},{1,2},{2,1},{3,0},{4,7},{5,6},{6,5},{7,4},{8,11},{9,10},{10,... | collective-permute-start | bytes 884744 | tf_op jit(solution)/shard_map/ppermute | solution.py:268
  25.8 0.7 %copy-start.3 = (f32[1,4]{1,0:T(1,128)S(1)}, f32[1,4]{1,0:T(1,128)}, u32[]{:S(2)}) copy-start(f32[1,4]{1,0:T(1,128)} %refs_1_.3) | copy-start | bytes 52
  34.4 1.6 %collective-permute-start.6 = (f32[512,128]{1,0:T(8,128)S(1)}, f32[512,128]{1,0:T(8,128)S(1)}, u32[]{:S(2)}, u32[]{:S(2)}) collective-permute-start(f32[512,128]{1,0:T(8,128)S(1)} %get-tuple-element.43), channel_id=1, source_target_pairs={{0,4},{1,5},{2,6},{3,7},{4,0},{5,1},{6,2},{7,3},{8,12},{9,13},{10,... | collective-permute-start | bytes 786440 | tf_op jit(solution)/shard_map/ppermute | solution.py:268
  36.0 5.6 %collective-permute-start.7 = (f32[128,128]{1,0:T(8,128)S(1)}, f32[128,128]{1,0:T(8,128)S(1)}, u32[]{:S(2)}, u32[]{:S(2)}) collective-permute-start(f32[128,128]{1,0:T(8,128)S(1)} %get-tuple-element.45), channel_id=1, source_target_pairs={{0,1},{1,0},{2,3},{3,2},{4,5},{5,4},{6,7},{7,6},{8,9},{9,8},{10,11... | collective-permute-start | bytes 196616 | tf_op jit(solution)/shard_map/ppermute | solution.py:268
  37.3 13.3 %collective-permute-start.13 = (f32[256,128]{1,0:T(8,128)S(1)}, f32[256,128]{1,0:T(8,128)S(1)}, u32[]{:S(2)}, u32[]{:S(2)}) collective-permute-start(f32[256,128]{1,0:T(8,128)S(1)} %get-tuple-element.53), channel_id=1, source_target_pairs={{0,1},{1,0},{2,3},{3,2},{4,5},{5,4},{6,7},{7,6},{8,9},{9,8},{10,11... | collective-permute-start | bytes 393224 | tf_op jit(solution)/shard_map/ppermute | solution.py:268
  38.1 5.0 %collective-permute-start.8 = (f32[128,128]{1,0:T(8,128)S(1)}, f32[128,128]{1,0:T(8,128)S(1)}, u32[]{:S(2)}, u32[]{:S(2)}) collective-permute-start(f32[128,128]{1,0:T(8,128)S(1)} %get-tuple-element.46), channel_id=1, source_target_pairs={{0,2},{1,3},{2,0},{3,1},{4,6},{5,7},{6,4},{7,5},{8,10},{9,11},{10,... | collective-permute-start | bytes 196616 | tf_op jit(solution)/shard_map/ppermute | solution.py:268
  39.7 6.7 %collective-permute-start.9 = (f32[128,128]{1,0:T(8,128)S(1)}, f32[128,128]{1,0:T(8,128)S(1)}, u32[]{:S(2)}, u32[]{:S(2)}) collective-permute-start(f32[128,128]{1,0:T(8,128)S(1)} %get-tuple-element.47), channel_id=1, source_target_pairs={{0,3},{1,2},{2,1},{3,0},{4,7},{5,6},{6,5},{7,4},{8,11},{9,10},{10,... | collective-permute-start | bytes 196616 | tf_op jit(solution)/shard_map/ppermute | solution.py:268
  40.8 10.0 %collective-permute-start.14 = (f32[256,128]{1,0:T(8,128)S(1)}, f32[256,128]{1,0:T(8,128)S(1)}, u32[]{:S(2)}, u32[]{:S(2)}) collective-permute-start(f32[256,128]{1,0:T(8,128)S(1)} %get-tuple-element.54), channel_id=1, source_target_pairs={{0,2},{1,3},{2,0},{3,1},{4,6},{5,7},{6,4},{7,5},{8,10},{9,11},{10,... | collective-permute-start | bytes 393224 | tf_op jit(solution)/shard_map/ppermute | solution.py:268
  41.7 9.1 %collective-permute-start.15 = (f32[256,128]{1,0:T(8,128)S(1)}, f32[256,128]{1,0:T(8,128)S(1)}, u32[]{:S(2)}, u32[]{:S(2)}) collective-permute-start(f32[256,128]{1,0:T(8,128)S(1)} %get-tuple-element.55), channel_id=1, source_target_pairs={{0,3},{1,2},{2,1},{3,0},{4,7},{5,6},{6,5},{7,4},{8,11},{9,10},{10,... | collective-permute-start | bytes 393224 | tf_op jit(solution)/shard_map/ppermute | solution.py:268
  46.4 5.3 %collective-permute-start.10 = (f32[128,128]{1,0:T(8,128)S(1)}, f32[128,128]{1,0:T(8,128)S(1)}, u32[]{:S(2)}, u32[]{:S(2)}) collective-permute-start(f32[128,128]{1,0:T(8,128)S(1)} %get-tuple-element.49), channel_id=1, source_target_pairs={{0,8},{1,9},{2,10},{3,11},{4,12},{5,13},{6,14},{7,15},{8,0},{9,1},... | collective-permute-start | bytes 196616 | tf_op jit(solution)/shard_map/ppermute | solution.py:268
  48.0 6.6 %collective-permute-start.11 = (f32[128,128]{1,0:T(8,128)S(1)}, f32[128,128]{1,0:T(8,128)S(1)}, u32[]{:S(2)}, u32[]{:S(2)}) collective-permute-start(f32[128,128]{1,0:T(8,128)S(1)} %get-tuple-element.50), channel_id=1, source_target_pairs={{0,16},{1,17},{2,18},{3,19},{4,20},{5,21},{6,22},{7,23},{8,24},{9,... | collective-permute-start | bytes 196616 | tf_op jit(solution)/shard_map/ppermute | solution.py:268
  50.6 6.1 %collective-permute-start.12 = (f32[128,128]{1,0:T(8,128)S(1)}, f32[128,128]{1,0:T(8,128)S(1)}, u32[]{:S(2)}, u32[]{:S(2)}) collective-permute-start(f32[128,128]{1,0:T(8,128)S(1)} %get-tuple-element.51), channel_id=1, source_target_pairs={{0,24},{1,25},{2,26},{3,27},{4,28},{5,29},{6,30},{7,31},{8,16},{9,... | collective-permute-start | bytes 196616 | tf_op jit(solution)/shard_map/ppermute | solution.py:268

commit v2 on v1

v2 whole, which is shorter than its diff:
```python
import functools

import jax
import jax.numpy as jnp
from jax import lax
from jax.experimental import pallas as pl
from jax.experimental.pallas import tpu as pltpu
from jax.sharding import PartitionSpec as P

NT = 4
PRIOR_GAIN = 50.0
EDGE = 8
VMEM = pl.BlockSpec(memory_space=pltpu.VMEM)
HBM = pl.BlockSpec(memory_space=pltpu.HBM)
SMEM = pl.BlockSpec(memory_space=pltpu.SMEM)
LIMIT = 48 * 1024 * 1024
BLOCK = 768


def stay(array):
    return pltpu.with_memory_space_constraint(array, pltpu.HBM)


def call(body, out_rows, scratch=(), in_specs=(), flops=0, moved=0):
    return pl.pallas_call(
        body,
        out_shape=[jax.ShapeDtypeStruct(*s) if isinstance(s[0], tuple) else jax.ShapeDtypeStruct(s, jnp.float32) for s in out_rows],
        in_specs=list(in_specs),
        out_specs=[VMEM] * len(out_rows),
        scratch_shapes=list(scratch),
        compiler_params=pltpu.CompilerParams(vmem_limit_bytes=LIMIT),
        cost_estimate=pl.CostEstimate(flops=flops, bytes_accessed=moved, transcendentals=0),
    )


def window(field, plane, block, blocks, rows):
    first = pl.multiple_of(block * rows, 8)
    above = pl.multiple_of(jnp.maximum(first - EDGE, 0), 8)
    below = pl.multiple_of(jnp.minimum(first + rows, (blocks * rows) - EDGE), 8)
    top = field[plane, pl.ds(above, EDGE), :]
    bottom = field[plane, pl.ds(below, EDGE), :]
    top = jnp.where(block > 0, top, 0.0)
    bottom = jnp.where(block < blocks - 1, bottom, 0.0)
    return top, field[plane, pl.ds(first, rows), :], bottom


def put(field, plane, block, blocks, rows, out, at):
    top, core, bottom = window(field, plane, block, blocks, rows)
    out[at : at + EDGE, :] = top
    out[at + EDGE : at + EDGE + rows, :] = core
    out[at + EDGE + rows : at + rows + 2 * EDGE, :] = bottom


def fetch(field, held, semaphores):
    copies = [pltpu.make_async_copy(field.at[p], held.at[p], semaphores.at[p]) for p in range(held.shape[0])]
    for copy in copies:
        copy.start()
    return copies


def pack_kappa(blocks, planes, rows, kappa, *refs):
    outs, (held, whole, semaphores) = refs[:blocks], refs[blocks:]
    copies = fetch(kappa, held, semaphores)
    dom = lax.axis_index("dom")
    core = lax.rem(lax.axis_index("shot"), 2)
    tall = rows + 2 * EDGE
    half = tall // 2
    for p in range(planes):
        copies[p].wait()
        put(held, p, dom, blocks, rows, outs[0], p * tall)
        for s in range(1, blocks):
            put(held, p, lax.bitwise_xor(dom, s), blocks, rows, whole, 0)
            outs[s][p * half : (p + 1) * half, :] = whole[pl.ds(pl.multiple_of(core * half, 8), half), :]


def pack_waves(blocks, planes, rows, now, before, *refs):
    outs, (held_now, held_before, semaphores) = refs[:blocks], refs[blocks:]
    fields = (held_now, held_before)
    copies = fetch(now, held_now, semaphores.at[0]) + fetch(before, held_before, semaphores.at[1])
    dom = lax.axis_index("dom")
    tall = rows + 2 * EDGE
    for f, field in enumerate(fields):
        for p in range(planes):
            copies[f * planes + p].wait()
            for s in range(blocks):
                put(field, p, lax.bitwise_xor(dom, s), blocks, rows, outs[s], (f * planes + p) * tall)


def gather(*refs):
    out = refs[-1]
    size = refs[0].shape[0]
    for i, ref in enumerate(refs[:-1]):
        out[i * size : (i + 1) * size, :] = ref[...]


def spread(depth, ny, rows, count, source, lists_at, cells_at, observed_at, *refs):
    count_ref, heard_ref, pulse_ref, listed, wavelet, cells_ref, observed_ref, semaphores = refs
    copies = [
        pltpu.make_async_copy(lists_at, wavelet, semaphores.at[0]),
        pltpu.make_async_copy(cells_at, cells_ref, semaphores.at[1]),
        pltpu.make_async_copy(observed_at, observed_ref, semaphores.at[2]),
    ]
    for copy in copies:
        copy.start()
    tall = rows + 2 * EDGE
    size = count_ref.shape[0]
    dom = lax.axis_index("dom")
    spot = lax.rem(source[0], depth)
    lane = lax.broadcasted_iota(jnp.int32, (1, depth), 1)
    count_ref[...] = jnp.zeros_like(count_ref)
    heard_ref[...] = jnp.zeros_like(heard_ref)
    for copy in copies:
        copy.wait()
    for n in range(NT):
        pulse_ref[n : n + 1, :] = jnp.where(lane == spot, wavelet[:, n : n + 1], 0.0)
    cells = cells_ref[...]
    line = cells // depth
    x = line // ny
    y = line - x * ny - (dom * rows - EDGE)
    here = (y >= 0) & (y < tall)
    row = x * tall + jnp.clip(y, 0, tall - 1)
    coarse = row // 64
    stack = [array.astype(jnp.float32) for array in (coarse, row - coarse * 64, cells - line * depth)]
    left = observed_ref[0]
    for part in range(3):
        piece = left.astype(jnp.bfloat16).astype(jnp.float32)
        left = left - piece
        stack.append(piece)
    stack = jnp.concatenate(stack + [jnp.zeros((13 - 3 * NT, count), jnp.float32)], axis=0)

    columns = 128
    ones = jnp.where(here, 1.0, 0.0)
    ones = jnp.concatenate([ones[:, j : j + columns] for j in range(0, count, columns)], axis=0)
    square = (columns, columns)
    down, across = lax.broadcasted_iota(jnp.int32, square, 0), lax.broadcasted_iota(jnp.int32, square, 1)
    order = jnp.dot(ones, jnp.where(down < across, 1.0, 0.0), preferred_element_type=jnp.float32)
    order = jnp.where(ones > 0.0, order, -1.0)
    slots = down.astype(jnp.float32)
    total = 0
    for j in range(count // columns):
        turned = stack[:, j * columns : (j + 1) * columns].T.astype(jnp.bfloat16)
        move = jnp.where(slots == order[j : j + 1, :], 1.0, 0.0).astype(jnp.bfloat16)
        listed[pl.ds(total, columns), 0:16] = jnp.dot(move, turned, preferred_element_type=jnp.float32)
        total = total + jnp.sum(ones[j : j + 1, :]).astype(jnp.int32)

    def block(k, _):
        first = pl.multiple_of(k * BLOCK, 8)
        which = lax.broadcasted_iota(jnp.int32, (BLOCK, 16), 0) + first
        some = jnp.where(which < total, listed[pl.ds(first, BLOCK), 0:16], -1.0)
        flat = some.T
        ids = (flat[0:1, :] * 64.0 + flat[1:2, :]).astype(jnp.int32)
        hot = jnp.where(lax.broadcasted_iota(jnp.int32, (size, BLOCK), 0) == ids, 1.0, 0.0).astype(jnp.bfloat16)
        at = lax.broadcasted_iota(jnp.int32, (BLOCK, depth), 1).astype(jnp.float32) == some[:, 2:3]
        at = jnp.where(at, 1.0, 0.0).astype(jnp.bfloat16)
        some = some.astype(jnp.bfloat16)
        value = [at] + [at * some[:, 3 + i : 4 + i] for i in range(3 * NT)]
        out = jnp.dot(hot, jnp.concatenate(value, axis=1), preferred_element_type=jnp.float32)
        count_ref[...] += out[:, 0:depth]
        for n in range(NT):
            high, mid, low = (out[:, i * depth : (i + 1) * depth] for i in (1 + n, 1 + NT + n, 1 + 2 * NT + n))
            heard_ref[n] += high + (mid + low)
        return 0

    lax.fori_loop(0, (total + BLOCK - 1) // BLOCK, block, 0)


def bend(field, at, first, some, nx, x, planes_held, low, high):
    under, mid, over = planes_held
    total = field[(*at, x, pl.ds(first + 1, some))] + field[(*at, x, pl.ds(first - 1, some))]
    up = jnp.where(high, 0.0, pltpu.roll(mid, mid.shape[1] - 1, 1))
    down = jnp.where(low, 0.0, pltpu.roll(mid, 1, 1))
    total = total + (up + down)
    if x > 0:
        total = total + under
    if x < nx - 1:
        total = total + over
    return total


def sweep(field, at, first, some, nx):
    under, mid = None, field[(*at, 0, pl.ds(first, some))]
    for x in range(nx):
        over = field[(*at, x + 1, pl.ds(first, some))] if x < nx - 1 else None
        yield x, (under, mid, over)
        under, mid = mid, over


def steps(blocks, planes, rows, depth, ny, *refs):
    source, pulse, count, heard, refs = *refs[:4], refs[4:]
    kappas, refs = refs[:blocks], refs[blocks:]
    others, waves, refs = refs[0], refs[1 : 1 + blocks], refs[1 + blocks :]
    turned, (keep, give) = refs[:blocks], refs[blocks : blocks + 2]
    wave, lap, model, image, adjoint, weighted = refs[blocks + 2 :]
    tall = rows + 2 * EDGE
    nx = blocks * planes
    dom = lax.axis_index("dom")
    shot = lax.axis_index("shot")
    core = lax.rem(shot, 2)
    body = pl.ds(8, tall)

    half = tall // 2
    near = pl.ds(pl.multiple_of(8 + core * half, 8), half)
    far = pl.ds(pl.multiple_of(8 + (1 - core) * half, 8), half)
    for s in range(blocks):
        first = planes * lax.bitwise_xor(dom, s)
        for p in range(planes):
            wave[1, first + p, body, :] = waves[s][p * tall : (p + 1) * tall, :]
            wave[0, first + p, body, :] = waves[s][(planes + p) * tall : (planes + p + 1) * tall, :]
            if s == 0:
                model[first + p, body, :] = kappas[s][p * tall : (p + 1) * tall, :]
            else:
                model[first + p, near, :] = kappas[s][p * half : (p + 1) * half, :]
                at = ((s - 1) * planes + p) * half
                model[first + p, far, :] = others[at : at + half, :]

    some = 48
    lanes = lax.broadcasted_iota(jnp.int32, (some, depth), 1)
    low, high = lanes == 0, lanes == depth - 1
    line = source[0] // depth
    sx = line // ny
    sy = line - sx * ny - (dom * rows - EDGE)
    source_here = (sy >= 0) & (sy < tall)
    sy = 8 + jnp.clip(sy, 0, tall - 1)

    def forward(n, _):
        for a in range(0, tall, some):
            rows_at = pl.ds(8 + a, some)
            for x, held in sweep(wave, (n + 1,), 8 + a, some, nx):
                mid = held[1]
                bent = bend(wave, (n + 1,), 8 + a, some, nx, x, held, low, high) - 6.0 * mid
                lap[n, x, a : a + some, :] = bent
                new = (mid + mid) - wave[n, x, rows_at, :] + model[x, rows_at, :] * bent
                wave[n + 2, x, rows_at, :] = new

        @pl.when(source_here)
        def _():
            wave[n + 2, sx, pl.ds(sy, 1), :] = wave[n + 2, sx, pl.ds(sy, 1), :] + pulse[pl.ds(n, 1), :]

        return 0

    lax.fori_loop(0, NT, forward, 0)

    for s in range(blocks):
        first = planes * lax.bitwise_xor(dom, s)
        for p in range(planes):
            turned[s][p * rows : (p + 1) * rows, :] = wave[NT + 1, first + p, 8 + EDGE : 8 + EDGE + rows, :]

    for a in range(0, tall, some):
        rows_at = pl.ds(8 + a, some)
        for x in range(nx):
            at = slice(x * tall + a, x * tall + a + some)
            now = count[at, :] * wave[NT + 1, x, rows_at, :] - heard[NT - 1, at, :]
            adjoint[NT % 2, x, a : a + some, :] = now
            adjoint[1 - NT % 2, x, a : a + some, :] = jnp.zeros_like(now)
            weighted[NT % 2, x, rows_at, :] = now * model[x, rows_at, :]
            image[x, a : a + some, :] = now * lap[NT - 1, x, a : a + some, :]

    def level_of(level, last):
        new, old = level % 2, 1 - level % 2
        for a in range(0, tall, some):
            rows_at = pl.ds(8 + a, some)
            for x, held in sweep(weighted, (old,), 8 + a, some, nx):
                at = slice(x * tall + a, x * tall + a + some)
                bent = bend(weighted, (old,), 8 + a, some, nx, x, held, low, high) - 6.0 * held[1]
                after = adjoint[old, x, a : a + some, :]
                now = count[at, :] * wave[level + 1, x, rows_at, :] - heard[level - 1, at, :]
                now = (now + bent) + ((after + after) - adjoint[new, x, a : a + some, :])
                part = image[x, a : a + some, :] + now * lap[level - 1, x, a : a + some, :]
                if not last:
                    adjoint[new, x, a : a + some, :] = now
                    weighted[new, x, rows_at, :] = now * model[x, rows_at, :]
                image[x, a : a + some, :] = part

    def backward(i, _):
        level_of(NT - 1 - i, False)
        return 0

    lax.fori_loop(0, NT - 2, backward, 0)
    level_of(1, True)

    half = rows // 2
    mine = pl.multiple_of(EDGE + core * half, 8)
    mates = pl.multiple_of(EDGE + (1 - core) * half, 8)

    @pl.when(shot == 0)
    def _():
        for a in range(0, tall, some):
            for x, held in sweep(model, (), 8 + a, some, nx):
                total = bend(model, (), 8 + a, some, nx, x, held, low, high)
                score = (total / 6.0 - held[1]) * (PRIOR_GAIN * NT)
                image[x, a : a + some, :] = image[x, a : a + some, :] - score

    for x in range(nx):
        keep[x * half : (x + 1) * half, :] = image[x, pl.ds(mine, half), :] / NT
        give[x * half : (x + 1) * half, :] = image[x, pl.ds(mates, half), :] / NT


def cut(blocks, keep, got, *outs):
    dom = lax.axis_index("dom")
    size = outs[0].shape[0]
    for s in range(blocks):
        at = pl.ds(pl.multiple_of(lax.bitwise_xor(dom, s) * size, 8), size)
        outs[s][...] = keep[at, :] + got[at, :]


def sort(blocks, *refs):
    came, outs, held = refs[:blocks], refs[blocks : 2 * blocks], refs[2 * blocks]
    dom, pair = lax.axis_index("dom"), lax.axis_index("shot") // 2
    for s in range(blocks):
        held[lax.bitwise_xor(dom, s)] = came[s][...]
    for s in range(blocks):
        outs[s][...] = held[lax.bitwise_xor(pair, s)]


def add(planes, *refs):
    out = refs[-1]
    size = out.shape[1]
    for p in range(planes):
        total = refs[0][p * size : (p + 1) * size, :]
        for ref in refs[1:-1]:
            total = total + ref[p * size : (p + 1) * size, :]
        out[p] = total


def join(planes, rows, *refs):
    out = refs[-1]
    dom = lax.axis_index("dom")
    for s, ref in enumerate(refs[:-1]):
        at = pl.ds(pl.multiple_of(lax.bitwise_xor(dom, s) * rows, 8), rows)
        for p in range(planes):
            out[p, at, :] = ref[p * rows : (p + 1) * rows, :]


def shards(kappa, wave_now, wave_before, wavelet, source_cell, receiver_cells, observed):
    shots, blocks = lax.axis_size("shot"), lax.axis_size("dom")
    _, planes, ny, depth = wave_now.shape
    rows = ny // blocks
    tall = rows + 2 * EDGE
    nx = planes * blocks
    listed = receiver_cells.shape[1]

    def across(array, to):
        pairs = []
        for shot in range(shots):
            for dom in range(blocks):
                there = to(shot, dom)
                pairs.append((shot * blocks + dom, there[0] * blocks + there[1]))
        return lax.ppermute(array, ("shot", "dom"), pairs)

    def over_dom(arrays):
        return [arrays[0]] + [across(arrays[s], lambda shot, dom, s=s: (shot, dom ^ s)) for s in range(1, blocks)]

    def over_pairs(arrays):
        return [arrays[0]] + [across(arrays[s], lambda shot, dom, s=s: (shot ^ (2 * s), dom)) for s in range(1, blocks)]

    half = tall // 2
    held = pltpu.VMEM((planes, ny, depth), jnp.float32)
    kappas = call(
        functools.partial(pack_kappa, blocks, planes, rows),
        [(planes * tall, depth)] + [(planes * half, depth)] * (blocks - 1),
        in_specs=[HBM],
        scratch=[held, pltpu.VMEM((tall, depth), jnp.float32), pltpu.SemaphoreType.DMA((planes,))],
    )(stay(kappa))
    waves = call(
        functools.partial(pack_waves, blocks, planes, rows),
        [(2 * planes * tall, depth)] * blocks,
        in_specs=[HBM] * 2,
        scratch=[held, held, pltpu.SemaphoreType.DMA((2, planes))],
    )(stay(wave_now[0]), stay(wave_before[0]))
    kappas = over_dom(kappas)
    waves = over_dom(waves)
    (gathered,) = call(gather, [((blocks - 1) * planes * half, depth)], in_specs=[VMEM] * (blocks - 1))(*kappas[1:])
    others = across(gathered, lambda shot, dom: (shot ^ 1, dom))

    wide = (1 + 3 * NT) * depth
    count, heard, pulse = call(
        functools.partial(spread, depth, ny, rows, listed),
        [(nx * tall, depth), (NT, nx * tall, depth), (NT, depth)],
        in_specs=[SMEM, HBM, HBM, HBM],
        scratch=[pltpu.VMEM((listed + BLOCK, depth), jnp.float32)]
        + [pltpu.VMEM(array.shape, array.dtype) for array in (wavelet, receiver_cells, observed)]
        + [pltpu.SemaphoreType.DMA((3,))],
        flops=2 * nx * tall * BLOCK * wide,
        moved=4 * (1 + NT) * nx * tall * depth,
    )(source_cell, stay(wavelet), stay(receiver_cells), stay(observed))

    half = rows // 2
    *turned, keep, give = call(
        functools.partial(steps, blocks, planes, rows, depth, ny),
        [(planes * rows, depth)] * blocks + [(nx * half, depth)] * 2,
        in_specs=[SMEM] + [VMEM] * (2 * blocks + 4),
        scratch=[
            pltpu.VMEM((NT + 2, nx, tall + 16, depth), jnp.float32),
            pltpu.VMEM((NT, nx, tall, depth), jnp.float32),
            pltpu.VMEM((nx, tall + 16, depth), jnp.float32),
            pltpu.VMEM((nx, tall, depth), jnp.float32),
            pltpu.VMEM((2, nx, tall, depth), jnp.float32),
            pltpu.VMEM((2, nx, tall + 16, depth), jnp.float32),
        ],
        flops=2 * NT * 20 * nx * tall * depth,
        moved=4 * 10 * nx * tall * depth,
    )(source_cell, pulse, count, heard, *kappas, others, *waves)

    got = across(give, lambda shot, dom: (shot ^ 1, dom))
    pieces = call(functools.partial(cut, blocks), [(planes * half, depth)] * blocks, in_specs=[VMEM] * 2)(keep, got)
    pieces = over_dom(pieces)
    turned = over_dom(turned)
    pieces = call(
        functools.partial(sort, blocks),
        [(planes * half, depth)] * blocks,
        in_specs=[VMEM] * blocks,
        scratch=[pltpu.VMEM((blocks, planes * half, depth), jnp.float32)],
    )(*pieces)
    pieces = over_pairs(pieces)
    (wave_next,) = call(functools.partial(join, planes, rows), [(planes, ny, depth)], in_specs=[VMEM] * blocks)(*turned)
    (total,) = call(functools.partial(add, planes), [(planes, half, depth)], in_specs=[VMEM] * blocks)(*pieces)
    return total, wave_next[None]


def solution(mesh):
    return jax.shard_map(
        shards,
        mesh=mesh,
        in_specs=(
            P("dom", None, None),
            P("shot", "dom", None, None),
            P("shot", "dom", None, None),
            P("shot", None),
            P("shot"),
            P("shot", None),
            P("shot", None, None),
        ),
        out_specs=(P("dom", "shot", None), P("shot", "dom", None, None)),
        check_vma=False,
    )
```

time: 57.6 us -> 50.5 us (0.88)
  Pallas kernels: 20.9 us -> 12.9 us
  waiting for transfers between devices: 11.2 us -> 16.4 us
  local copies, waits for them, and re-layouts: 2.74 us -> 0 us
  starting transfers between devices: 21.1 us -> 19.6 us
    pallas_call x1, Pallas kernels: 11.3 us -> 4.95 us  [shards(): call(functools.partial(spread, depth, ny, rows, listed), [(nx * tall, dep...]
    ppermute x16 -> x17, waiting for transfers between devices: 11.2 us -> 16.4 us  [across(): return lax.ppermute(array, ('shot', 'dom'), pairs)]
    pallas_call x1, Pallas kernels: 7.91 us -> 4.07 us  [shards(): call(functools.partial(steps, blocks, planes, rows, depth, ny), [(planes...]
    unnamed x12 -> x0, local copies, waits for them, and re-layouts: 2.74 us -> none
    pallas_call x2 -> x3, Pallas kernels: 0.12 us -> 2.34 us  [the longest x1 1.24 us: shards(): call(functools.partial(pack_waves, blocks, planes, rows), [(2 * planes *...]
    ppermute x16 -> x17, starting transfers between devices: 21.1 us -> 19.6 us  [across(): return lax.ppermute(array, ('shot', 'dom'), pairs)]
  transfers between devices with their start and end apart: 16 -> 17, of which waited for: 5 -> 9; matrix products, arithmetic and copies ran while one was open for 0% -> 0% of each run, Pallas kernels for 21% -> 14%
where the time goes in v2:
time: 50.5 us; the launch traced here: 50.3 us
  starting transfers between devices  19.6 us (39%)
  waiting for transfers between devices  16.4 us (32%)
  Pallas kernels  12.9 us (26%)
  between operations  1.37 us (3%)
    ppermute x17, starting transfers between devices, across(): return lax.ppermute(array, ('shot', 'dom'), pairs)  19.6 us
    ppermute x17, waiting for transfers between devices, across(): return lax.ppermute(array, ('shot', 'dom'), pairs)  16.4 us
    pallas_call x1, Pallas kernels, shards(): call(functools.partial(spread, depth, ny, rows, listed), [(nx * tall, dep...  4.95 us
    pallas_call x1, Pallas kernels, shards(): call(functools.partial(steps, blocks, planes, rows, depth, ny), [(planes...  4.07 us
    pallas_call x1, Pallas kernels, shards(): call(functools.partial(pack_waves, blocks, planes, rows), [(2 * planes *...  1.24 us
    pallas_call x1, Pallas kernels, shards(): call(functools.partial(pack_kappa, blocks, planes, rows), [(planes * tall...  1.09 us
  transfers between devices with their start and end apart: 17, of which 9 were waited for; matrix products, arithmetic and copies ran while one was open for 0% of the time, Pallas kernels for 14%

profile of v2, /device:TPU:0, one launch (start us, length us, event | category | flops | bytes accessed | tf_op | source)
XLA Modules:
  0.0 50.3 jit_solution(4950332520167288300)
XLA Ops:
  0.6 1.1 %shard_map.87 = (f32[288,128]{1,0:T(8,128)S(1)}, f32[144,128]{1,0:T(8,128)S(1)}, f32[144,128]{1,0:T(8,128)S(1)}, f32[144,128]{1,0:T(8,128)S(1)}) custom-call(f32[2,512,128]{2,1,0:T(8,128)} %kappa.1), custom_call_target="tpu_custom_call" | custom-call | tf_op jit(solution)/shard_map/pallas_call | solution.py:358
  1.7 3.0 %collective-permute-start = (f32[144,128]{1,0:T(8,128)S(1)}, f32[144,128]{1,0:T(8,128)S(1)}, u32[]{:S(2)}, u32[]{:S(2)}) collective-permute-start(f32[144,128]{1,0:T(8,128)S(1)} %get-tuple-element.31), channel_id=1, source_target_pairs={{0,1},{1,0},{2,3},{3,2},{4,5},{5,4},{6,7},{7,6},{8,9},{9,8},{10,11... | collective-permute-start | bytes 221192 | tf_op jit(solution)/shard_map/ppermute | solution.py:348
  4.7 1.5 %collective-permute-start.1 = (f32[144,128]{1,0:T(8,128)S(1)}, f32[144,128]{1,0:T(8,128)S(1)}, u32[]{:S(2)}, u32[]{:S(2)}) collective-permute-start(f32[144,128]{1,0:T(8,128)S(1)} %get-tuple-element.32), channel_id=1, source_target_pairs={{0,2},{1,3},{2,0},{3,1},{4,6},{5,7},{6,4},{7,5},{8,10},{9,11},{10,... | collective-permute-start | bytes 221192 | tf_op jit(solution)/shard_map/ppermute | solution.py:348
  6.2 0.0 collective-permute-start.2
  6.3 1.2 %shard_map.89 = (f32[576,128]{1,0:T(8,128)S(1)}, f32[576,128]{1,0:T(8,128)S(1)}, f32[576,128]{1,0:T(8,128)S(1)}, f32[576,128]{1,0:T(8,128)S(1)}) custom-call(f32[2,512,128]{2,1,0:T(8,128)} %bitcast.3, f32[2,512,128]{2,1,0:T(8,128)} %bitcast.4), custom_call_target="tpu_custom_call" | custom-call | tf_op jit(solution)/shard_map/pallas_call | solution.py:364
  7.5 2.0 %collective-permute-start.4 = (f32[576,128]{1,0:T(8,128)S(1)}, f32[576,128]{1,0:T(8,128)S(1)}, u32[]{:S(2)}, u32[]{:S(2)}) collective-permute-start(f32[576,128]{1,0:T(8,128)S(1)} %get-tuple-element.35), channel_id=1, source_target_pairs={{0,1},{1,0},{2,3},{3,2},{4,5},{5,4},{6,7},{7,6},{8,9},{9,8},{10,11... | collective-permute-start | bytes 884744 | tf_op jit(solution)/shard_map/ppermute | solution.py:348
  9.5 1.5 %collective-permute-start.5 = (f32[576,128]{1,0:T(8,128)S(1)}, f32[576,128]{1,0:T(8,128)S(1)}, u32[]{:S(2)}, u32[]{:S(2)}) collective-permute-start(f32[576,128]{1,0:T(8,128)S(1)} %get-tuple-element.36), channel_id=1, source_target_pairs={{0,2},{1,3},{2,0},{3,1},{4,6},{5,7},{6,4},{7,5},{8,10},{9,11},{10,... | collective-permute-start | bytes 884744 | tf_op jit(solution)/shard_map/ppermute | solution.py:348
  11.1 0.0 collective-permute-done.refs_0_.refs_5_
  11.1 0.0 collective-permute-start.6
  11.7 0.0 collective-permute-done.1.refs_1_.refs_6_
  11.7 0.6 %collective-permute-done.2.refs_2_.refs_7_ = f32[144,128]{1,0:T(8,128)S(1)} collective-permute-done((f32[144,128]{1,0:T(8,128)S(1)}, f32[144,128]{1,0:T(8,128)S(1)}, u32[]{:S(2)}, u32[]{:S(2)}) %collective-permute-start.2) | collective-permute-done | bytes 73760 | tf_op jit(solution)/shard_map/ppermute | solution.py:348
  12.3 0.1 collective-permute-start.3
  12.4 5.0 %shard_map.86 = (f32[1152,128]{1,0:T(8,128)S(1)}, f32[4,1152,128]{2,1,0:T(8,128)S(1)}, f32[4,128]{1,0:T(4,128)S(1)}) custom-call(s32[1]{0:T(128)S(6)} %copy.9.source.refs_0_, f32[1,4]{1,0:T(1,128)} %lists_at.1, s32[1,2048]{1,0:T(1,128)} %cells_at.1, f32[1,4,2048]{2,1,0:T(4,128)} %observed_at.1), custom_call_target="tpu_custom_call" | custom-call | flops 2944401408 | bytes 2949120 | tf_op jit(solution)/shard_map/pallas_call | solution.py:376
  17.4 0.0 collective-permute-done.3.refs_8_
  17.4 0.3 collective-permute-done.4.refs_10_
  17.7 6.6 %collective-permute-done.5.refs_11_ = f32[576,128]{1,0:T(8,128)S(1)} collective-permute-done((f32[576,128]{1,0:T(8,128)S(1)}, f32[576,128]{1,0:T(8,128)S(1)}, u32[]{:S(2)}, u32[]{:S(2)}) %collective-permute-start.5) | collective-permute-done | bytes 294944 | tf_op jit(solution)/shard_map/ppermute | solution.py:348
  24.2 0.0 collective-permute-done.6.refs_12_
  24.2 4.1 %shard_map.90 = (f32[256,128]{1,0:T(8,128)S(1)}, f32[256,128]{1,0:T(8,128)S(1)}, f32[256,128]{1,0:T(8,128)S(1)}, f32[256,128]{1,0:T(8,128)S(1)}, f32[512,128]{1,0:T(8,128)S(1)}, /*index=5*/f32[512,128]{1,0:T(8,128)S(1)}) custom-call(s32[1]{0:T(128)S(6)} %copy.9.source.refs_0_, f32[4,128]{1,0:T(4,128)S(1)} %get-tuple-element.27.refs_1_, ...), custom_call_target="tpu_custom_call" | custom-call | flops 23592960 | bytes 5898240 | tf_op jit(solution)/shard_map/pallas_call | solution.py:388
  28.3 0.1 collective-permute-start.7
  28.4 1.5 %collective-permute-done.7.got = f32[512,128]{1,0:T(8,128)S(1)} collective-permute-done((f32[512,128]{1,0:T(8,128)S(1)}, f32[512,128]{1,0:T(8,128)S(1)}, u32[]{:S(2)}, u32[]{:S(2)}) %collective-permute-start.7) | collective-permute-done | bytes 262176 | tf_op jit(solution)/shard_map/ppermute | solution.py:348
  29.9 0.6 %collective-permute-start.8 = (f32[128,128]{1,0:T(8,128)S(1)}, f32[128,128]{1,0:T(8,128)S(1)}, u32[]{:S(2)}, u32[]{:S(2)}) collective-permute-start(f32[128,128]{1,0:T(8,128)S(1)} %get-tuple-element.41), channel_id=1, source_target_pairs={{0,1},{1,0},{2,3},{3,2},{4,5},{5,4},{6,7},{7,6},{8,9},{9,8},{10,11... | collective-permute-start | bytes 196616 | tf_op jit(solution)/shard_map/ppermute | solution.py:348
  30.5 1.5 %collective-permute-start.14 = (f32[256,128]{1,0:T(8,128)S(1)}, f32[256,128]{1,0:T(8,128)S(1)}, u32[]{:S(2)}, u32[]{:S(2)}) collective-permute-start(f32[256,128]{1,0:T(8,128)S(1)} %get-tuple-element.49), channel_id=1, source_target_pairs={{0,1},{1,0},{2,3},{3,2},{4,5},{5,4},{6,7},{7,6},{8,9},{9,8},{10,11... | collective-permute-start | bytes 393224 | tf_op jit(solution)/shard_map/ppermute | solution.py:348
  32.0 1.0 %collective-permute-start.9 = (f32[128,128]{1,0:T(8,128)S(1)}, f32[128,128]{1,0:T(8,128)S(1)}, u32[]{:S(2)}, u32[]{:S(2)}) collective-permute-start(f32[128,128]{1,0:T(8,128)S(1)} %get-tuple-element.42), channel_id=1, source_target_pairs={{0,2},{1,3},{2,0},{3,1},{4,6},{5,7},{6,4},{7,5},{8,10},{9,11},{10,... | collective-permute-start | bytes 196616 | tf_op jit(solution)/shard_map/ppermute | solution.py:348
  33.0 1.0 %collective-permute-start.10 = (f32[128,128]{1,0:T(8,128)S(1)}, f32[128,128]{1,0:T(8,128)S(1)}, u32[]{:S(2)}, u32[]{:S(2)}) collective-permute-start(f32[128,128]{1,0:T(8,128)S(1)} %get-tuple-element.43), channel_id=1, source_target_pairs={{0,3},{1,2},{2,1},{3,0},{4,7},{5,6},{6,5},{7,4},{8,11},{9,10},{10,... | collective-permute-start | bytes 196616 | tf_op jit(solution)/shard_map/ppermute | solution.py:348
  34.0 0.8 %collective-permute-start.15 = (f32[256,128]{1,0:T(8,128)S(1)}, f32[256,128]{1,0:T(8,128)S(1)}, u32[]{:S(2)}, u32[]{:S(2)}) collective-permute-start(f32[256,128]{1,0:T(8,128)S(1)} %get-tuple-element.50), channel_id=1, source_target_pairs={{0,2},{1,3},{2,0},{3,1},{4,6},{5,7},{6,4},{7,5},{8,10},{9,11},{10,... | collective-permute-start | bytes 393224 | tf_op jit(solution)/shard_map/ppermute | solution.py:348
  34.8 0.1 collective-permute-done.8.refs_1_
  34.9 2.0 %collective-permute-start.16 = (f32[256,128]{1,0:T(8,128)S(1)}, f32[256,128]{1,0:T(8,128)S(1)}, u32[]{:S(2)}, u32[]{:S(2)}) collective-permute-start(f32[256,128]{1,0:T(8,128)S(1)} %get-tuple-element.51), channel_id=1, source_target_pairs={{0,3},{1,2},{2,1},{3,0},{4,7},{5,6},{6,5},{7,4},{8,11},{9,10},{10,... | collective-permute-start | bytes 393224 | tf_op jit(solution)/shard_map/ppermute | solution.py:348
  37.0 0.4 collective-permute-done.9.refs_2_
  37.4 2.3 %collective-permute-done.10.refs_3_ = f32[128,128]{1,0:T(8,128)S(1)} collective-permute-done((f32[128,128]{1,0:T(8,128)S(1)}, f32[128,128]{1,0:T(8,128)S(1)}, u32[]{:S(2)}, u32[]{:S(2)}) %collective-permute-start.10) | collective-permute-done | bytes 65568 | tf_op jit(solution)/shard_map/ppermute | solution.py:348
  39.7 1.3 %collective-permute-start.11 = (f32[128,128]{1,0:T(8,128)S(1)}, f32[128,128]{1,0:T(8,128)S(1)}, u32[]{:S(2)}, u32[]{:S(2)}) collective-permute-start(f32[128,128]{1,0:T(8,128)S(1)} %get-tuple-element.45), channel_id=1, source_target_pairs={{0,8},{1,9},{2,10},{3,11},{4,12},{5,13},{6,14},{7,15},{8,0},{9,1},... | collective-permute-start | bytes 196616 | tf_op jit(solution)/shard_map/ppermute | solution.py:348
  41.0 2.6 %collective-permute-start.12 = (f32[128,128]{1,0:T(8,128)S(1)}, f32[128,128]{1,0:T(8,128)S(1)}, u32[]{:S(2)}, u32[]{:S(2)}) collective-permute-start(f32[128,128]{1,0:T(8,128)S(1)} %get-tuple-element.46), channel_id=1, source_target_pairs={{0,16},{1,17},{2,18},{3,19},{4,20},{5,21},{6,22},{7,23},{8,24},{9,... | collective-permute-start | bytes 196616 | tf_op jit(solution)/shard_map/ppermute | solution.py:348
  43.6 0.0 collective-permute-done.14.refs_1_
  43.6 0.6 %collective-permute-start.13 = (f32[128,128]{1,0:T(8,128)S(1)}, f32[128,128]{1,0:T(8,128)S(1)}, u32[]{:S(2)}, u32[]{:S(2)}) collective-permute-start(f32[128,128]{1,0:T(8,128)S(1)} %get-tuple-element.47), channel_id=1, source_target_pairs={{0,24},{1,25},{2,26},{3,27},{4,28},{5,29},{6,30},{7,31},{8,16},{9,... | collective-permute-start | bytes 196616 | tf_op jit(solution)/shard_map/ppermute | solution.py:348
  44.2 0.0 collective-permute-done.15.refs_2_
  44.2 0.0 collective-permute-done.16.refs_3_
  44.2 0.8 %shard_map.94 = f32[2,512,128]{2,1,0:T(8,128)} custom-call(f32[256,128]{1,0:T(8,128)S(1)} %get-tuple-element.48.refs_0_, f32[256,128]{1,0:T(8,128)S(1)} %collective-permute-done.14.refs_1_, f32[256,128]{1,0:T(8,128)S(1)} %collective-permute-done.15.refs_2_, f32[256,128]{1,0:T(8,128)S(1)} %collective-permute-done.16.refs_3_), custom_call_target="tpu_custom_call" | custom-call | tf_op jit(solution)/shard_map/pallas_call | solution.py:415
  45.0 0.0 collective-permute-done.11.refs_1_
  45.0 2.5 %collective-permute-done.12.refs_2_ = f32[128,128]{1,0:T(8,128)S(1)} collective-permute-done((f32[128,128]{1,0:T(8,128)S(1)}, f32[128,128]{1,0:T(8,128)S(1)}, u32[]{:S(2)}, u32[]{:S(2)}) %collective-permute-start.12) | collective-permute-done | bytes 65568 | tf_op jit(solution)/shard_map/ppermute | solution.py:348
  47.6 2.1 %collective-permute-done.13.refs_3_ = f32[128,128]{1,0:T(8,128)S(1)} collective-permute-done((f32[128,128]{1,0:T(8,128)S(1)}, f32[128,128]{1,0:T(8,128)S(1)}, u32[]{:S(2)}, u32[]{:S(2)}) %collective-permute-start.13) | collective-permute-done | bytes 65568 | tf_op jit(solution)/shard_map/ppermute | solution.py:348
  49.7 0.6 %shard_map.93 = f32[2,64,128]{2,1,0:T(8,128)} custom-call(f32[128,128]{1,0:T(8,128)S(1)} %get-tuple-element.44.refs_0_, f32[128,128]{1,0:T(8,128)S(1)} %collective-permute-done.11.refs_1_, f32[128,128]{1,0:T(8,128)S(1)} %collective-permute-done.12.refs_2_, f32[128,128]{1,0:T(8,128)S(1)} %collective-permute-done.13.refs_3_), custom_call_target="tpu_custom_call" | custom-call | tf_op jit(solution)/shard_map/pallas_call | solution.py:416
  (3 shorter events, 0.1 us)
Async XLA Ops:
  1.7 9.3 %collective-permute-start = (f32[144,128]{1,0:T(8,128)S(1)}, f32[144,128]{1,0:T(8,128)S(1)}, u32[]{:S(2)}, u32[]{:S(2)}) collective-permute-start(f32[144,128]{1,0:T(8,128)S(1)} %get-tuple-element.31), channel_id=1, source_target_pairs={{0,1},{1,0},{2,3},{3,2},{4,5},{5,4},{6,7},{7,6},{8,9},{9,8},{10,11... | collective-permute-start | bytes 221192 | tf_op jit(solution)/shard_map/ppermute | solution.py:348
  4.7 7.0 %collective-permute-start.1 = (f32[144,128]{1,0:T(8,128)S(1)}, f32[144,128]{1,0:T(8,128)S(1)}, u32[]{:S(2)}, u32[]{:S(2)}) collective-permute-start(f32[144,128]{1,0:T(8,128)S(1)} %get-tuple-element.32), channel_id=1, source_target_pairs={{0,2},{1,3},{2,0},{3,1},{4,6},{5,7},{6,4},{7,5},{8,10},{9,11},{10,... | collective-permute-start | bytes 221192 | tf_op jit(solution)/shard_map/ppermute | solution.py:348
  6.2 6.0 %collective-permute-start.2 = (f32[144,128]{1,0:T(8,128)S(1)}, f32[144,128]{1,0:T(8,128)S(1)}, u32[]{:S(2)}, u32[]{:S(2)}) collective-permute-start(f32[144,128]{1,0:T(8,128)S(1)} %get-tuple-element.33), channel_id=1, source_target_pairs={{0,3},{1,2},{2,1},{3,0},{4,7},{5,6},{6,5},{7,4},{8,11},{9,10},{10,... | collective-permute-start | bytes 221192 | tf_op jit(solution)/shard_map/ppermute | solution.py:348
  7.5 10.1 %collective-permute-start.4 = (f32[576,128]{1,0:T(8,128)S(1)}, f32[576,128]{1,0:T(8,128)S(1)}, u32[]{:S(2)}, u32[]{:S(2)}) collective-permute-start(f32[576,128]{1,0:T(8,128)S(1)} %get-tuple-element.35), channel_id=1, source_target_pairs={{0,1},{1,0},{2,3},{3,2},{4,5},{5,4},{6,7},{7,6},{8,9},{9,8},{10,11... | collective-permute-start | bytes 884744 | tf_op jit(solution)/shard_map/ppermute | solution.py:348
  9.5 14.7 %collective-permute-start.5 = (f32[576,128]{1,0:T(8,128)S(1)}, f32[576,128]{1,0:T(8,128)S(1)}, u32[]{:S(2)}, u32[]{:S(2)}) collective-permute-start(f32[576,128]{1,0:T(8,128)S(1)} %get-tuple-element.36), channel_id=1, source_target_pairs={{0,2},{1,3},{2,0},{3,1},{4,6},{5,7},{6,4},{7,5},{8,10},{9,11},{10,... | collective-permute-start | bytes 884744 | tf_op jit(solution)/shard_map/ppermute | solution.py:348
  11.1 13.2 %collective-permute-start.6 = (f32[576,128]{1,0:T(8,128)S(1)}, f32[576,128]{1,0:T(8,128)S(1)}, u32[]{:S(2)}, u32[]{:S(2)}) collective-permute-start(f32[576,128]{1,0:T(8,128)S(1)} %get-tuple-element.37), channel_id=1, source_target_pairs={{0,3},{1,2},{2,1},{3,0},{4,7},{5,6},{6,5},{7,4},{8,11},{9,10},{10,... | collective-permute-start | bytes 884744 | tf_op jit(solution)/shard_map/ppermute | solution.py:348
  12.3 5.0 %collective-permute-start.3 = (f32[432,128]{1,0:T(8,128)S(1)}, f32[432,128]{1,0:T(8,128)S(1)}, u32[]{:S(2)}, u32[]{:S(2)}) collective-permute-start(f32[432,128]{1,0:T(8,128)S(1)} %shard_map.88), channel_id=1, source_target_pairs={{0,4},{1,5},{2,6},{3,7},{4,0},{5,1},{6,2},{7,3},{8,12},{9,13},{10,... | collective-permute-start | bytes 663560 | tf_op jit(solution)/shard_map/ppermute | solution.py:348
  28.3 1.6 %collective-permute-start.7 = (f32[512,128]{1,0:T(8,128)S(1)}, f32[512,128]{1,0:T(8,128)S(1)}, u32[]{:S(2)}, u32[]{:S(2)}) collective-permute-start(f32[512,128]{1,0:T(8,128)S(1)} %get-tuple-element.39), channel_id=1, source_target_pairs={{0,4},{1,5},{2,6},{3,7},{4,0},{5,1},{6,2},{7,3},{8,12},{9,13},{10,... | collective-permute-start | bytes 786440 | tf_op jit(solution)/shard_map/ppermute | solution.py:348
  29.9 5.0 %collective-permute-start.8 = (f32[128,128]{1,0:T(8,128)S(1)}, f32[128,128]{1,0:T(8,128)S(1)}, u32[]{:S(2)}, u32[]{:S(2)}) collective-permute-start(f32[128,128]{1,0:T(8,128)S(1)} %get-tuple-element.41), channel_id=1, source_target_pairs={{0,1},{1,0},{2,3},{3,2},{4,5},{5,4},{6,7},{7,6},{8,9},{9,8},{10,11... | collective-permute-start | bytes 196616 | tf_op jit(solution)/shard_map/ppermute | solution.py:348
  30.5 13.1 %collective-permute-start.14 = (f32[256,128]{1,0:T(8,128)S(1)}, f32[256,128]{1,0:T(8,128)S(1)}, u32[]{:S(2)}, u32[]{:S(2)}) collective-permute-start(f32[256,128]{1,0:T(8,128)S(1)} %get-tuple-element.49), channel_id=1, source_target_pairs={{0,1},{1,0},{2,3},{3,2},{4,5},{5,4},{6,7},{7,6},{8,9},{9,8},{10,11... | collective-permute-start | bytes 393224 | tf_op jit(solution)/shard_map/ppermute | solution.py:348
  32.0 5.4 %collective-permute-start.9 = (f32[128,128]{1,0:T(8,128)S(1)}, f32[128,128]{1,0:T(8,128)S(1)}, u32[]{:S(2)}, u32[]{:S(2)}) collective-permute-start(f32[128,128]{1,0:T(8,128)S(1)} %get-tuple-element.42), channel_id=1, source_target_pairs={{0,2},{1,3},{2,0},{3,1},{4,6},{5,7},{6,4},{7,5},{8,10},{9,11},{10,... | collective-permute-start | bytes 196616 | tf_op jit(solution)/shard_map/ppermute | solution.py:348
  33.0 6.7 %collective-permute-start.10 = (f32[128,128]{1,0:T(8,128)S(1)}, f32[128,128]{1,0:T(8,128)S(1)}, u32[]{:S(2)}, u32[]{:S(2)}) collective-permute-start(f32[128,128]{1,0:T(8,128)S(1)} %get-tuple-element.43), channel_id=1, source_target_pairs={{0,3},{1,2},{2,1},{3,0},{4,7},{5,6},{6,5},{7,4},{8,11},{9,10},{10,... | collective-permute-start | bytes 196616 | tf_op jit(solution)/shard_map/ppermute | solution.py:348
  34.0 10.2 %collective-permute-start.15 = (f32[256,128]{1,0:T(8,128)S(1)}, f32[256,128]{1,0:T(8,128)S(1)}, u32[]{:S(2)}, u32[]{:S(2)}) collective-permute-start(f32[256,128]{1,0:T(8,128)S(1)} %get-tuple-element.50), channel_id=1, source_target_pairs={{0,2},{1,3},{2,0},{3,1},{4,6},{5,7},{6,4},{7,5},{8,10},{9,11},{10,... | collective-permute-start | bytes 393224 | tf_op jit(solution)/shard_map/ppermute | solution.py:348
  34.9 9.3 %collective-permute-start.16 = (f32[256,128]{1,0:T(8,128)S(1)}, f32[256,128]{1,0:T(8,128)S(1)}, u32[]{:S(2)}, u32[]{:S(2)}) collective-permute-start(f32[256,128]{1,0:T(8,128)S(1)} %get-tuple-element.51), channel_id=1, source_target_pairs={{0,3},{1,2},{2,1},{3,0},{4,7},{5,6},{6,5},{7,4},{8,11},{9,10},{10,... | collective-permute-start | bytes 393224 | tf_op jit(solution)/shard_map/ppermute | solution.py:348
  39.7 5.3 %collective-permute-start.11 = (f32[128,128]{1,0:T(8,128)S(1)}, f32[128,128]{1,0:T(8,128)S(1)}, u32[]{:S(2)}, u32[]{:S(2)}) collective-permute-start(f32[128,128]{1,0:T(8,128)S(1)} %get-tuple-element.45), channel_id=1, source_target_pairs={{0,8},{1,9},{2,10},{3,11},{4,12},{5,13},{6,14},{7,15},{8,0},{9,1},... | collective-permute-start | bytes 196616 | tf_op jit(solution)/shard_map/ppermute | solution.py:348
  41.0 6.6 %collective-permute-start.12 = (f32[128,128]{1,0:T(8,128)S(1)}, f32[128,128]{1,0:T(8,128)S(1)}, u32[]{:S(2)}, u32[]{:S(2)}) collective-permute-start(f32[128,128]{1,0:T(8,128)S(1)} %get-tuple-element.46), channel_id=1, source_target_pairs={{0,16},{1,17},{2,18},{3,19},{4,20},{5,21},{6,22},{7,23},{8,24},{9,... | collective-permute-start | bytes 196616 | tf_op jit(solution)/shard_map/ppermute | solution.py:348
  43.6 6.1 %collective-permute-start.13 = (f32[128,128]{1,0:T(8,128)S(1)}, f32[128,128]{1,0:T(8,128)S(1)}, u32[]{:S(2)}, u32[]{:S(2)}) collective-permute-start(f32[128,128]{1,0:T(8,128)S(1)} %get-tuple-element.47), channel_id=1, source_target_pairs={{0,24},{1,25},{2,26},{3,27},{4,28},{5,29},{6,30},{7,31},{8,16},{9,... | collective-permute-start | bytes 196616 | tf_op jit(solution)/shard_map/ppermute | solution.py:348

commit v3 on v2

--- a/solution.py
+++ b/solution.py
@@ -13,7 +13,7 @@
 VMEM = pl.BlockSpec(memory_space=pltpu.VMEM)
 HBM = pl.BlockSpec(memory_space=pltpu.HBM)
 SMEM = pl.BlockSpec(memory_space=pltpu.SMEM)
-LIMIT = 48 * 1024 * 1024
+LIMIT = 32 * 1024 * 1024
 BLOCK = 768
 
 
@@ -58,39 +58,48 @@
     return copies
 
 
-def pack_kappa(blocks, planes, rows, kappa, *refs):
-    outs, (held, whole, semaphores) = refs[:blocks], refs[blocks:]
-    copies = fetch(kappa, held, semaphores)
-    dom = lax.axis_index("dom")
-    core = lax.rem(lax.axis_index("shot"), 2)
+def pack_early(blocks, planes, rows, kappa, now, *refs):
+    outs, (held, model, whole, semaphores) = refs[: blocks - 1], refs[blocks - 1 :]
+    dom, core = lax.axis_index("dom"), lax.rem(lax.axis_index("shot"), 2)
+    copies = [pltpu.make_async_copy(now.at[0], held.at[0], semaphores.at[planes])]
+    copies[0].start()
+    copies += fetch(kappa, model, semaphores)
     tall = rows + 2 * EDGE
     half = tall // 2
+    copies[0].wait()
+    for s in range(1, blocks):
+        put(held, 0, lax.bitwise_xor(dom, s), blocks, rows, outs[s - 1], 0)
     for p in range(planes):
-        copies[p].wait()
-        put(held, p, dom, blocks, rows, outs[0], p * tall)
+        copies[1 + p].wait()
         for s in range(1, blocks):
-            put(held, p, lax.bitwise_xor(dom, s), blocks, rows, whole, 0)
-            outs[s][p * half : (p + 1) * half, :] = whole[pl.ds(pl.multiple_of(core * half, 8), half), :]
-
-
-def pack_waves(blocks, planes, rows, now, before, *refs):
-    outs, (held_now, held_before, semaphores) = refs[:blocks], refs[blocks:]
-    fields = (held_now, held_before)
-    copies = fetch(now, held_now, semaphores.at[0]) + fetch(before, held_before, semaphores.at[1])
+            put(model, p, lax.bitwise_xor(dom, s), blocks, rows, whole, 0)
+            at = tall + p * half
+            outs[s - 1][at : at + half, :] = whole[pl.ds(pl.multiple_of(core * half, 8), half), :]
+
+
+def pack_late(blocks, planes, rows, kappa, now, before, *refs):
+    outs, own, refs = refs[: blocks - 1], refs[blocks - 1], refs[blocks:]
+    held, semaphores = refs[:3], refs[3]
+    fields = (now, before, kappa)
+    copies = [fetch(field, ref, semaphores.at[i]) for i, (field, ref) in enumerate(zip(fields, held))]
     dom = lax.axis_index("dom")
     tall = rows + 2 * EDGE
-    for f, field in enumerate(fields):
+    for f in range(3):
         for p in range(planes):
-            copies[f * planes + p].wait()
-            for s in range(blocks):
-                put(field, p, lax.bitwise_xor(dom, s), blocks, rows, outs[s], (f * planes + p) * tall)
-
-
-def gather(*refs):
-    out = refs[-1]
-    size = refs[0].shape[0]
-    for i, ref in enumerate(refs[:-1]):
-        out[i * size : (i + 1) * size, :] = ref[...]
+            copies[f][p].wait()
+            put(held[f], p, dom, blocks, rows, own, (f * planes + p) * tall)
+            to = f * planes + p - 1
+            if f < 2 and to >= 0:
+                for s in range(1, blocks):
+                    put(held[f], p, lax.bitwise_xor(dom, s), blocks, rows, outs[s - 1], to * tall)
+
+
+def gather(planes, half, *refs):
+    parts, outs = refs[:-planes], refs[-planes:]
+    for i, part in enumerate(parts):
+        first = part.shape[0] - planes * half
+        for p, out in enumerate(outs):
+            out[i * half : (i + 1) * half, :] = part[first + p * half : first + (p + 1) * half, :]
 
 
 def spread(depth, ny, rows, count, source, lists_at, cells_at, observed_at, *refs):
@@ -185,114 +194,127 @@
         under, mid = mid, over
 
 
-def steps(blocks, planes, rows, depth, ny, *refs):
-    source, pulse, count, heard, refs = *refs[:4], refs[4:]
-    kappas, refs = refs[:blocks], refs[blocks:]
-    others, waves, refs = refs[0], refs[1 : 1 + blocks], refs[1 + blocks :]
-    turned, (keep, give) = refs[:blocks], refs[blocks : blocks + 2]
-    wave, lap, model, image, adjoint, weighted = refs[blocks + 2 :]
-    tall = rows + 2 * EDGE
-    nx = blocks * planes
-    dom = lax.axis_index("dom")
-    shot = lax.axis_index("shot")
-    core = lax.rem(shot, 2)
-    body = pl.ds(8, tall)
-
+def edges(some, depth):
+    lanes = lax.broadcasted_iota(jnp.int32, (some, depth), 1)
+    return lanes == 0, lanes == depth - 1
+
+
+def forward(blocks, planes, rows, ny, source, pulse, *refs):
+    early, late, own, refs = refs[: blocks - 1], refs[blocks - 1 : 2 * blocks - 2], refs[2 * blocks - 2], refs[2 * blocks - 1 :]
+    swapped, refs = refs[:planes], refs[planes:]
+    wave, lap, model, turned, start = *refs[:3], refs[3:-1], refs[-1]
+    nx, tall, depth = lap.shape[1:]
+    dom, core = lax.axis_index("dom"), lax.rem(lax.axis_index("shot"), 2)
     half = tall // 2
     near = pl.ds(pl.multiple_of(8 + core * half, 8), half)
-    far = pl.ds(pl.multiple_of(8 + (1 - core) * half, 8), half)
+    other = pl.ds(pl.multiple_of(8 + (1 - core) * half, 8), half)
+    body = slice(8, 8 + tall)
     for s in range(blocks):
         first = planes * lax.bitwise_xor(dom, s)
         for p in range(planes):
-            wave[1, first + p, body, :] = waves[s][p * tall : (p + 1) * tall, :]
-            wave[0, first + p, body, :] = waves[s][(planes + p) * tall : (planes + p + 1) * tall, :]
             if s == 0:
-                model[first + p, body, :] = kappas[s][p * tall : (p + 1) * tall, :]
-            else:
-                model[first + p, near, :] = kappas[s][p * half : (p + 1) * half, :]
-                at = ((s - 1) * planes + p) * half
-                model[first + p, far, :] = others[at : at + half, :]
+                for f, to in enumerate((start.at[0], start.at[1], model)):
+                    at = (f * planes + p) * tall
+                    to[first + p, body, :] = own[at : at + tall, :]
+                continue
+            for f in range(2):
+                i = f * planes + p - 1
+                part = late[s - 1][i * tall : (i + 1) * tall, :] if i >= 0 else early[s - 1][0:tall, :]
+                start[f, first + p, body, :] = part
+            at = tall + p * half
+            model[first + p, near, :] = early[s - 1][at : at + half, :]
+            model[first + p, other, :] = swapped[p][(s - 1) * half : s * half, :]
 
     some = 48
-    lanes = lax.broadcasted_iota(jnp.int32, (some, depth), 1)
-    low, high = lanes == 0, lanes == depth - 1
+    low, high = edges(some, depth)
     line = source[0] // depth
     sx = line // ny
     sy = line - sx * ny - (dom * rows - EDGE)
     source_here = (sy >= 0) & (sy < tall)
     sy = 8 + jnp.clip(sy, 0, tall - 1)
 
-    def forward(n, _):
-        for a in range(0, tall, some):
-            rows_at = pl.ds(8 + a, some)
-            for x, held in sweep(wave, (n + 1,), 8 + a, some, nx):
-                mid = held[1]
-                bent = bend(wave, (n + 1,), 8 + a, some, nx, x, held, low, high) - 6.0 * mid
-                lap[n, x, a : a + some, :] = bent
-                new = (mid + mid) - wave[n, x, rows_at, :] + model[x, rows_at, :] * bent
-                wave[n + 2, x, rows_at, :] = new
-
+    def inject(n):
         @pl.when(source_here)
         def _():
-            wave[n + 2, sx, pl.ds(sy, 1), :] = wave[n + 2, sx, pl.ds(sy, 1), :] + pulse[pl.ds(n, 1), :]
-
-        return 0
-
-    lax.fori_loop(0, NT, forward, 0)
+            wave[n, sx, pl.ds(sy, 1), :] = wave[n, sx, pl.ds(sy, 1), :] + pulse[n : n + 1, :]
+
+    for n in range(NT):
+        source_of = (wave, (n - 1,)) if n > 0 else (start, (0,))
+        older = (wave, n - 2) if n > 1 else (start, 1 - n)
+        for a in range(0, tall, some):
+            rows_at = slice(8 + a, 8 + a + some)
+            for x, held in sweep(*source_of, 8 + a, some, nx):
+                mid = held[1]
+                turn = bend(*source_of, 8 + a, some, nx, x, held, low, high) - 6.0 * mid
+                lap[n, x, a : a + some, :] = turn
+                old = older[0][older[1], x, rows_at, :]
+                wave[n, x, rows_at, :] = (mid + mid) - old + model[x, rows_at, :] * turn
+        inject(n)
 
     for s in range(blocks):
         first = planes * lax.bitwise_xor(dom, s)
         for p in range(planes):
-            turned[s][p * rows : (p + 1) * rows, :] = wave[NT + 1, first + p, 8 + EDGE : 8 + EDGE + rows, :]
-
-    for a in range(0, tall, some):
-        rows_at = pl.ds(8 + a, some)
+            turned[s][p * rows : (p + 1) * rows, :] = wave[NT - 1, first + p, 8 + EDGE : 8 + EDGE + rows, :]
+
+
+def backward(mine, rows, count, heard, wave, lap, model, image, adjoint, weighted, gain):
+    nx, tall, depth = lap.shape[1:]
+    shot = lax.axis_index("shot")
+    core = lax.rem(shot, 2)
+    half = rows // 2
+    wide = half + 2 * EDGE
+    first = pl.multiple_of((core if mine else 1 - core) * half, 8)
+    some = 40 if wide % 40 == 0 else 16
+    low, high = edges(some, depth)
+
+    def at(a, size=some, off=0):
+        return pl.ds(pl.multiple_of(first + (a + off), 8), size)
+
+    for a in range(0, wide, some):
+        here = slice(a, a + some)
         for x in range(nx):
-            at = slice(x * tall + a, x * tall + a + some)
-            now = count[at, :] * wave[NT + 1, x, rows_at, :] - heard[NT - 1, at, :]
-            adjoint[NT % 2, x, a : a + some, :] = now
-            adjoint[1 - NT % 2, x, a : a + some, :] = jnp.zeros_like(now)
-            weighted[NT % 2, x, rows_at, :] = now * model[x, rows_at, :]
-            image[x, a : a + some, :] = now * lap[NT - 1, x, a : a + some, :]
-
-    def level_of(level, last):
+            now = count[at(a, off=x * tall), :] * wave[NT - 1, x, at(a, off=8), :] - heard[NT - 1, at(a, off=x * tall), :]
+            adjoint[NT % 2, x, here, :] = now
+            weighted[NT % 2, x, 8 + a : 8 + a + some, :] = now * model[x, at(a, off=8), :]
+            gain[x, here, :] = now * lap[NT - 1, x, at(a), :]
+
+    for level in range(NT - 1, 1, -1):
         new, old = level % 2, 1 - level % 2
-        for a in range(0, tall, some):
-            rows_at = pl.ds(8 + a, some)
+        for a in range(0, wide, some):
+            here = slice(a, a + some)
             for x, held in sweep(weighted, (old,), 8 + a, some, nx):
-                at = slice(x * tall + a, x * tall + a + some)
-                bent = bend(weighted, (old,), 8 + a, some, nx, x, held, low, high) - 6.0 * held[1]
-                after = adjoint[old, x, a : a + some, :]
-                now = count[at, :] * wave[level + 1, x, rows_at, :] - heard[level - 1, at, :]
-                now = (now + bent) + ((after + after) - adjoint[new, x, a : a + some, :])
-                part = image[x, a : a + some, :] + now * lap[level - 1, x, a : a + some, :]
-                if not last:
-                    adjoint[new, x, a : a + some, :] = now
-                    weighted[new, x, rows_at, :] = now * model[x, rows_at, :]
-                image[x, a : a + some, :] = part
-
-    def backward(i, _):
-        level_of(NT - 1 - i, False)
-        return 0
-
-    lax.fori_loop(0, NT - 2, backward, 0)
-    level_of(1, True)
-
-    half = rows // 2
-    mine = pl.multiple_of(EDGE + core * half, 8)
-    mates = pl.multiple_of(EDGE + (1 - core) * half, 8)
+                turn = bend(weighted, (old,), 8 + a, some, nx, x, held, low, high) - 6.0 * held[1]
+                after = adjoint[old, x, here, :]
+                now = count[at(a, off=x * tall), :] * wave[level - 1, x, at(a, off=8), :]
+                now = (now - heard[level - 1, at(a, off=x * tall), :]) + (turn + (after + after))
+                if level < NT - 1:
+                    now = now - adjoint[new, x, here, :]
+                adjoint[new, x, here, :] = now
+                weighted[new, x, 8 + a : 8 + a + some, :] = now * model[x, at(a, off=8), :]
+                gain[x, here, :] = gain[x, here, :] + now * lap[level - 1, x, at(a), :]
+
+    some = 32 if half % 32 == 0 else 16
+    low, high = edges(some, depth)
+    for a in range(EDGE, EDGE + half, some):
+        here = slice(a, a + some)
+        for x, held in sweep(weighted, (0,), 8 + a, some, nx):
+            turn = bend(weighted, (0,), 8 + a, some, nx, x, held, low, high) - 6.0 * held[1]
+            after = adjoint[0, x, here, :]
+            now = count[at(a, some, x * tall), :] * wave[0, x, at(a, some, 8), :]
+            now = (now - heard[0, at(a, some, x * tall), :]) + (turn + (after + after)) - adjoint[1, x, here, :]
+            total = gain[x, here, :] + now * lap[0, x, at(a, some), :]
+            image[x * half + a - EDGE : x * half + a - EDGE + some, :] = total / NT
 
     @pl.when(shot == 0)
     def _():
-        for a in range(0, tall, some):
-            for x, held in sweep(model, (), 8 + a, some, nx):
-                total = bend(model, (), 8 + a, some, nx, x, held, low, high)
-                score = (total / 6.0 - held[1]) * (PRIOR_GAIN * NT)
-                image[x, a : a + some, :] = image[x, a : a + some, :] - score
-
-    for x in range(nx):
-        keep[x * half : (x + 1) * half, :] = image[x, pl.ds(mine, half), :] / NT
-        give[x * half : (x + 1) * half, :] = image[x, pl.ds(mates, half), :] / NT
+        for x in range(nx):
+            weighted[0, x, 0 : wide + 16, :] = model[x, pl.ds(first, wide + 16), :]
+        for a in range(EDGE, EDGE + half, some):
+            for x, held in sweep(weighted, (0,), 8 + a, some, nx):
+                total = bend(weighted, (0,), 8 + a, some, nx, x, held, low, high)
+                score = (total / 6.0 - held[1]) * PRIOR_GAIN
+                to = slice(x * half + a - EDGE, x * half + a - EDGE + some)
+                image[to, :] = image[to, :] - score
 
 
 def cut(blocks, keep, got, *outs):
@@ -355,22 +377,26 @@
 
     half = tall // 2
     held = pltpu.VMEM((planes, ny, depth), jnp.float32)
-    kappas = call(
-        functools.partial(pack_kappa, blocks, planes, rows),
-        [(planes * tall, depth)] + [(planes * half, depth)] * (blocks - 1),
-        in_specs=[HBM],
-        scratch=[held, pltpu.VMEM((tall, depth), jnp.float32), pltpu.SemaphoreType.DMA((planes,))],
-    )(stay(kappa))
-    waves = call(
-        functools.partial(pack_waves, blocks, planes, rows),
-        [(2 * planes * tall, depth)] * blocks,
+    early = call(
+        functools.partial(pack_early, blocks, planes, rows),
+        [(tall + planes * half, depth)] * (blocks - 1),
         in_specs=[HBM] * 2,
-        scratch=[held, held, pltpu.SemaphoreType.DMA((2, planes))],
-    )(stay(wave_now[0]), stay(wave_before[0]))
-    kappas = over_dom(kappas)
-    waves = over_dom(waves)
-    (gathered,) = call(gather, [((blocks - 1) * planes * half, depth)], in_specs=[VMEM] * (blocks - 1))(*kappas[1:])
-    others = across(gathered, lambda shot, dom: (shot ^ 1, dom))
+        scratch=[
+            pltpu.VMEM((1, ny, depth), jnp.float32),
+            held,
+            pltpu.VMEM((tall, depth), jnp.float32),
+            pltpu.SemaphoreType.DMA((planes + 1,)),
+        ],
+    )(stay(kappa), stay(wave_now[0]))
+    early, before = lax.optimization_barrier((early, wave_before[0]))
+    *late, own = call(
+        functools.partial(pack_late, blocks, planes, rows),
+        [((2 * planes - 1) * tall, depth)] * (blocks - 1) + [(3 * planes * tall, depth)],
+        in_specs=[HBM] * 3,
+        scratch=[held, held, held, pltpu.SemaphoreType.DMA((3, planes))],
+    )(stay(kappa), stay(wave_now[0]), stay(before))
+    early = over_dom([None, *early])[1:]
+    late = over_dom([None, *late])[1:]
 
     wide = (1 + 3 * NT) * depth
     count, heard, pulse = call(
@@ -380,26 +406,43 @@
         scratch=[pltpu.VMEM((listed + BLOCK, depth), jnp.float32)]
         + [pltpu.VMEM(array.shape, array.dtype) for array in (wavelet, receiver_cells, observed)]
         + [pltpu.SemaphoreType.DMA((3,))],
-        flops=2 * nx * tall * BLOCK * wide,
-        moved=4 * (1 + NT) * nx * tall * depth,
+        flops=1000 * 1000 * 1000,
+        moved=1,
     )(source_cell, stay(wavelet), stay(receiver_cells), stay(observed))
 
+    came, pulse = lax.optimization_barrier((early, pulse))
+    parts = call(
+        functools.partial(gather, planes, half), [((blocks - 1) * half, depth)] * planes, in_specs=[VMEM] * (blocks - 1)
+    )(*came)
+    swapped = [across(part, lambda shot, dom: (shot ^ 1, dom)) for part in parts]
+
+    padded, plain = (nx, tall + 16, depth), (nx, tall, depth)
+    cells = nx * tall * depth
+    wave, lap, model, *turned = call(
+        functools.partial(forward, blocks, planes, rows, ny),
+        [(NT, *padded), (NT, *plain), padded] + [(planes * rows, depth)] * blocks,
+        in_specs=[SMEM] + [VMEM] * (2 * blocks + planes),
+        scratch=[pltpu.VMEM((2, *padded), jnp.float32)],
+        flops=16 * NT * cells,
+        moved=16 * NT * cells,
+    )(source_cell, pulse, *early, *late, own, *swapped)
     half = rows // 2
-    *turned, keep, give = call(
-        functools.partial(steps, blocks, planes, rows, depth, ny),
-        [(planes * rows, depth)] * blocks + [(nx * half, depth)] * 2,
-        in_specs=[SMEM] + [VMEM] * (2 * blocks + 4),
-        scratch=[
-            pltpu.VMEM((NT + 2, nx, tall + 16, depth), jnp.float32),
-            pltpu.VMEM((NT, nx, tall, depth), jnp.float32),
-            pltpu.VMEM((nx, tall + 16, depth), jnp.float32),
-            pltpu.VMEM((nx, tall, depth), jnp.float32),
-            pltpu.VMEM((2, nx, tall, depth), jnp.float32),
-            pltpu.VMEM((2, nx, tall + 16, depth), jnp.float32),
-        ],
-        flops=2 * NT * 20 * nx * tall * depth,
-        moved=4 * 10 * nx * tall * depth,
-    )(source_cell, pulse, count, heard, *kappas, others, *waves)
+    side = half + 2 * EDGE
+    give, keep = (
+        call(
+            functools.partial(backward, mine, rows),
+            [(nx * half, depth)],
+            in_specs=[VMEM] * 5,
+            scratch=[
+                pltpu.VMEM((2, nx, side, depth), jnp.float32),
+                pltpu.VMEM((2, nx, side + 16, depth), jnp.float32),
+                pltpu.VMEM((nx, side, depth), jnp.float32),
+            ],
+            flops=12 * NT * cells,
+            moved=12 * NT * cells,
+        )(count, heard, wave, lap, model)[0]
+        for mine in (False, True)
+    )
 
     got = across(give, lambda shot, dom: (shot ^ 1, dom))
     pieces = call(functools.partial(cut, blocks), [(planes * half, depth)] * blocks, in_specs=[VMEM] * 2)(keep, got)
@@ -410,6 +453,8 @@
         [(planes * half, depth)] * blocks,
         in_specs=[VMEM] * blocks,
         scratch=[pltpu.VMEM((blocks, planes * half, depth), jnp.float32)],
+        flops=1400 * 1000 * 1000,
+        moved=1,
     )(*pieces)
     pieces = over_pairs(pieces)
     (wave_next,) = call(functools.partial(join, planes, rows), [(planes, ny, depth)], in_specs=[VMEM] * blocks)(*turned)

time: 50.5 us -> 46.3 us (0.917)
  waiting for transfers between devices: 16.4 us -> 8.64 us
  starting transfers between devices: 19.6 us -> 22.8 us
    ppermute x17 -> x18, waiting for transfers between devices: 16.4 us -> 8.64 us  [across(): return lax.ppermute(array, ('shot', 'dom'), pairs)]
    ppermute x17 -> x18, starting transfers between devices: 19.6 us -> 22.8 us  [across(): return lax.ppermute(array, ('shot', 'dom'), pairs)]
    pallas_call x4 -> x6, Pallas kernels: 6.42 us -> 6.71 us  [the longest x2 2.41 us: shards(): call(functools.partial(backward, mine, rows), [(nx * half, depth)], in_sp...]
  transfers between devices with their start and end apart: 17 -> 18, of which waited for: 9 -> 5; matrix products, arithmetic and copies ran while one was open for 0% -> 0% of each run, Pallas kernels for 14% -> 18%
where the time goes in v3:
time: 46.3 us; the launch traced here: 46.1 us
  starting transfers between devices  22.8 us (49%)
  Pallas kernels  13.2 us (29%)
  waiting for transfers between devices  8.64 us (19%)
  between operations  1.39 us (3%)
    ppermute x18, starting transfers between devices, across(): return lax.ppermute(array, ('shot', 'dom'), pairs)  22.8 us
    ppermute x18, waiting for transfers between devices, across(): return lax.ppermute(array, ('shot', 'dom'), pairs)  8.64 us
    pallas_call x1, Pallas kernels, shards(): call(functools.partial(spread, depth, ny, rows, listed), [(nx * tall, dep...  4.96 us
    pallas_call x2, Pallas kernels, shards(): call(functools.partial(backward, mine, rows), [(nx * half, depth)], in_sp...  2.41 us
    pallas_call x1, Pallas kernels, shards(): call(functools.partial(forward, blocks, planes, rows, ny), [(NT, *padded)...  1.71 us
    pallas_call x1, Pallas kernels, shards(): call(functools.partial(pack_late, blocks, planes, rows), [((2 * planes -...  1.4 us
    pallas_call x1, Pallas kernels, shards(): call(functools.partial(pack_early, blocks, planes, rows), [(tall + planes...  1.17 us
  transfers between devices with their start and end apart: 18, of which 5 were waited for; matrix products, arithmetic and copies ran while one was open for 0% of the time, Pallas kernels for 18%

profile of v3, /device:TPU:0, one launch (start us, length us, event | category | flops | bytes accessed | tf_op | source)
XLA Modules:
  0.0 46.1 jit_solution(15319759772228162192)
XLA Ops:
  0.6 1.2 %shard_map.87 = (f32[288,128]{1,0:T(8,128)S(1)}, f32[288,128]{1,0:T(8,128)S(1)}, f32[288,128]{1,0:T(8,128)S(1)}) custom-call(f32[2,512,128]{2,1,0:T(8,128)} %kappa.3, f32[2,512,128]{2,1,0:T(8,128)} %bitcast.3), custom_call_target="tpu_custom_call" | custom-call | tf_op jit(solution)/shard_map/pallas_call | solution.py:380
  1.8 3.0 %collective-permute-start = (f32[288,128]{1,0:T(8,128)S(1)}, f32[288,128]{1,0:T(8,128)S(1)}, u32[]{:S(2)}, u32[]{:S(2)}) collective-permute-start(f32[288,128]{1,0:T(8,128)S(1)} %get-tuple-element.42), channel_id=1, source_target_pairs={{0,1},{1,0},{2,3},{3,2},{4,5},{5,4},{6,7},{7,6},{8,9},{9,8},{10,11... | collective-permute-start | bytes 442376 | tf_op jit(solution)/shard_map/ppermute | solution.py:370
  4.8 1.5 %collective-permute-start.1 = (f32[288,128]{1,0:T(8,128)S(1)}, f32[288,128]{1,0:T(8,128)S(1)}, u32[]{:S(2)}, u32[]{:S(2)}) collective-permute-start(f32[288,128]{1,0:T(8,128)S(1)} %get-tuple-element.43), channel_id=1, source_target_pairs={{0,2},{1,3},{2,0},{3,1},{4,6},{5,7},{6,4},{7,5},{8,10},{9,11},{10,... | collective-permute-start | bytes 442376 | tf_op jit(solution)/shard_map/ppermute | solution.py:370
  6.3 0.0 collective-permute-start.2
  6.4 1.4 %shard_map.88 = (f32[432,128]{1,0:T(8,128)S(1)}, f32[432,128]{1,0:T(8,128)S(1)}, f32[432,128]{1,0:T(8,128)S(1)}, f32[864,128]{1,0:T(8,128)S(1)}) custom-call(f32[2,512,128]{2,1,0:T(8,128)} %kappa.3, f32[2,512,128]{2,1,0:T(8,128)} %bitcast.4, f32[2,512,128]{2,1,0:T(8,128)} %bitcast.5), custom_call_target="tpu_custom_call" | custom-call | tf_op jit(solution)/shard_map/pallas_call | solution.py:392
  7.8 2.0 %collective-permute-start.3 = (f32[432,128]{1,0:T(8,128)S(1)}, f32[432,128]{1,0:T(8,128)S(1)}, u32[]{:S(2)}, u32[]{:S(2)}) collective-permute-start(f32[432,128]{1,0:T(8,128)S(1)} %get-tuple-element.48), channel_id=1, source_target_pairs={{0,1},{1,0},{2,3},{3,2},{4,5},{5,4},{6,7},{7,6},{8,9},{9,8},{10,11... | collective-permute-start | bytes 663560 | tf_op jit(solution)/shard_map/ppermute | solution.py:370
  9.8 1.5 %collective-permute-start.4 = (f32[432,128]{1,0:T(8,128)S(1)}, f32[432,128]{1,0:T(8,128)S(1)}, u32[]{:S(2)}, u32[]{:S(2)}) collective-permute-start(f32[432,128]{1,0:T(8,128)S(1)} %get-tuple-element.49), channel_id=1, source_target_pairs={{0,2},{1,3},{2,0},{3,1},{4,6},{5,7},{6,4},{7,5},{8,10},{9,11},{10,... | collective-permute-start | bytes 663560 | tf_op jit(solution)/shard_map/ppermute | solution.py:370
  11.3 0.0 collective-permute-done.refs_0_
  11.3 1.2 %collective-permute-start.5 = (f32[432,128]{1,0:T(8,128)S(1)}, f32[432,128]{1,0:T(8,128)S(1)}, u32[]{:S(2)}, u32[]{:S(2)}) collective-permute-start(f32[432,128]{1,0:T(8,128)S(1)} %get-tuple-element.50), channel_id=1, source_target_pairs={{0,3},{1,2},{2,1},{3,0},{4,7},{5,6},{6,5},{7,4},{8,11},{9,10},{10,... | collective-permute-start | bytes 663560 | tf_op jit(solution)/shard_map/ppermute | solution.py:370
  13.2 5.0 %shard_map.86 = (f32[1152,128]{1,0:T(8,128)S(1)}, f32[4,1152,128]{2,1,0:T(8,128)S(1)}, f32[4,128]{1,0:T(4,128)S(1)}) custom-call(s32[1]{0:T(128)S(6)} %copy.9.source, f32[1,4]{1,0:T(1,128)} %lists_at.1, s32[1,2048]{1,0:T(1,128)} %cells_at.1, f32[1,4,2048]{2,1,0:T(4,128)} %observed_at.1), custom_call_target="tpu_custom_call" | custom-call | flops 1000000000 | bytes 1 | tf_op jit(solution)/shard_map/pallas_call | solution.py:402
  18.1 0.0 collective-permute-done.1.refs_1_
  18.1 0.0 collective-permute-done.2.refs_2_
  18.2 0.1 collective-permute-start.6
  18.3 0.5 %collective-permute-start.7 = (f32[216,128]{1,0:T(8,128)S(1)}, f32[216,128]{1,0:T(8,128)S(1)}, u32[]{:S(2)}, u32[]{:S(2)}) collective-permute-start(f32[216,128]{1,0:T(8,128)S(1)} %get-tuple-element.56), channel_id=1, source_target_pairs={{0,4},{1,5},{2,6},{3,7},{4,0},{5,1},{6,2},{7,3},{8,12},{9,13},{10,... | collective-permute-start | bytes 331784 | tf_op jit(solution)/shard_map/ppermute | solution.py:370
  18.8 0.0 collective-permute-done.3.refs_3_
  18.8 4.0 %collective-permute-done.4.refs_4_ = f32[432,128]{1,0:T(8,128)S(1)} collective-permute-done((f32[432,128]{1,0:T(8,128)S(1)}, f32[432,128]{1,0:T(8,128)S(1)}, u32[]{:S(2)}, u32[]{:S(2)}) %collective-permute-start.4) | collective-permute-done | bytes 221216 | tf_op jit(solution)/shard_map/ppermute | solution.py:370
  22.8 0.0 collective-permute-done.5.refs_5_
  22.8 0.0 collective-permute-done.6.refs_7_
  22.8 0.0 collective-permute-done.7.refs_8_
  22.8 1.7 %shard_map.90 = (f32[4,8,160,128]{3,2,1,0:T(8,128)S(1)}, f32[4,8,144,128]{3,2,1,0:T(8,128)S(1)}, f32[8,160,128]{2,1,0:T(8,128)S(1)}, f32[256,128]{1,0:T(8,128)S(...) custom-call(s32[1]{0:T(128)S(6)} %copy.9.source, ...), custom_call_target="tpu_custom_call" | custom-call | flops 9437184 | bytes 9437184 | tf_op jit(solution)/shard_map/pallas_call | solution.py:421
  24.5 1.2 %shard_map.92 = f32[512,128]{1,0:T(8,128)S(1)} custom-call(f32[1152,128]{1,0:T(8,128)S(1)} %get-tuple-element.37.count, f32[4,1152,128]{2,1,0:T(8,128)S(1)} %get-tuple-element.38.heard, f32[4,8,160,128]{3,2,1,0:T(8,128)S(1)} %get-tuple-element.57.wave, f32[4,8,144,128]{3,2,1,0:T(8,128)S(1)} %get-tuple-element.58.lap, f32[8,160,128]{2,1,0:T(8,128)S(1)} %get-tuple-element.59.model), custom_call_target="tpu_custom_call" | custom-call | flops 7077888 | bytes 7077888 | tf_op jit(solution)/shard_map/pallas_call | solution.py:432
  25.7 0.1 collective-permute-start.8
  25.8 1.2 %shard_map.91.keep = f32[512,128]{1,0:T(8,128)S(1)} custom-call(f32[1152,128]{1,0:T(8,128)S(1)} %get-tuple-element.37.count, f32[4,1152,128]{2,1,0:T(8,128)S(1)} %get-tuple-element.38.heard, f32[4,8,160,128]{3,2,1,0:T(8,128)S(1)} %get-tuple-element.57.wave, f32[4,8,144,128]{3,2,1,0:T(8,128)S(1)} %get-tuple-element.58.lap, ...), custom_call_target="tpu_custom_call" | custom-call | flops 7077888 | bytes 7077888 | tf_op jit(solution)/shard_map/pallas_call | solution.py:432
  27.0 0.3 collective-permute-done.8.got
  27.3 1.3 %collective-permute-start.9 = (f32[128,128]{1,0:T(8,128)S(1)}, f32[128,128]{1,0:T(8,128)S(1)}, u32[]{:S(2)}, u32[]{:S(2)}) collective-permute-start(f32[128,128]{1,0:T(8,128)S(1)} %get-tuple-element.61), channel_id=1, source_target_pairs={{0,1},{1,0},{2,3},{3,2},{4,5},{5,4},{6,7},{7,6},{8,9},{9,8},{10,11... | collective-permute-start | bytes 196616 | tf_op jit(solution)/shard_map/ppermute | solution.py:370
  28.6 0.8 %collective-permute-start.10 = (f32[128,128]{1,0:T(8,128)S(1)}, f32[128,128]{1,0:T(8,128)S(1)}, u32[]{:S(2)}, u32[]{:S(2)}) collective-permute-start(f32[128,128]{1,0:T(8,128)S(1)} %get-tuple-element.62), channel_id=1, source_target_pairs={{0,2},{1,3},{2,0},{3,1},{4,6},{5,7},{6,4},{7,5},{8,10},{9,11},{10,... | collective-permute-start | bytes 196616 | tf_op jit(solution)/shard_map/ppermute | solution.py:370
  29.5 1.4 %collective-permute-start.11 = (f32[128,128]{1,0:T(8,128)S(1)}, f32[128,128]{1,0:T(8,128)S(1)}, u32[]{:S(2)}, u32[]{:S(2)}) collective-permute-start(f32[128,128]{1,0:T(8,128)S(1)} %get-tuple-element.63), channel_id=1, source_target_pairs={{0,3},{1,2},{2,1},{3,0},{4,7},{5,6},{6,5},{7,4},{8,11},{9,10},{10,... | collective-permute-start | bytes 196616 | tf_op jit(solution)/shard_map/ppermute | solution.py:370
  30.9 1.2 %collective-permute-start.15 = (f32[256,128]{1,0:T(8,128)S(1)}, f32[256,128]{1,0:T(8,128)S(1)}, u32[]{:S(2)}, u32[]{:S(2)}) collective-permute-start(f32[256,128]{1,0:T(8,128)S(1)} %get-tuple-element.69), channel_id=1, source_target_pairs={{0,1},{1,0},{2,3},{3,2},{4,5},{5,4},{6,7},{7,6},{8,9},{9,8},{10,11... | collective-permute-start | bytes 393224 | tf_op jit(solution)/shard_map/ppermute | solution.py:370
  32.1 0.8 %collective-permute-start.16 = (f32[256,128]{1,0:T(8,128)S(1)}, f32[256,128]{1,0:T(8,128)S(1)}, u32[]{:S(2)}, u32[]{:S(2)}) collective-permute-start(f32[256,128]{1,0:T(8,128)S(1)} %get-tuple-element.70), channel_id=1, source_target_pairs={{0,2},{1,3},{2,0},{3,1},{4,6},{5,7},{6,4},{7,5},{8,10},{9,11},{10,... | collective-permute-start | bytes 393224 | tf_op jit(solution)/shard_map/ppermute | solution.py:370
  32.9 0.0 collective-permute-done.9.refs_1_
  32.9 1.4 %collective-permute-start.17 = (f32[256,128]{1,0:T(8,128)S(1)}, f32[256,128]{1,0:T(8,128)S(1)}, u32[]{:S(2)}, u32[]{:S(2)}) collective-permute-start(f32[256,128]{1,0:T(8,128)S(1)} %get-tuple-element.71), channel_id=1, source_target_pairs={{0,3},{1,2},{2,1},{3,0},{4,7},{5,6},{6,5},{7,4},{8,11},{9,10},{10,... | collective-permute-start | bytes 393224 | tf_op jit(solution)/shard_map/ppermute | solution.py:370
  34.4 0.0 collective-permute-done.10.refs_2_
  34.4 0.9 %collective-permute-done.11.refs_3_ = f32[128,128]{1,0:T(8,128)S(1)} collective-permute-done((f32[128,128]{1,0:T(8,128)S(1)}, f32[128,128]{1,0:T(8,128)S(1)}, u32[]{:S(2)}, u32[]{:S(2)}) %collective-permute-start.11) | collective-permute-done | bytes 65568 | tf_op jit(solution)/shard_map/ppermute | solution.py:370
  35.4 1.4 %collective-permute-start.12 = (f32[128,128]{1,0:T(8,128)S(1)}, f32[128,128]{1,0:T(8,128)S(1)}, u32[]{:S(2)}, u32[]{:S(2)}) collective-permute-start(f32[128,128]{1,0:T(8,128)S(1)} %get-tuple-element.65), channel_id=1, source_target_pairs={{0,8},{1,9},{2,10},{3,11},{4,12},{5,13},{6,14},{7,15},{8,0},{9,1},... | collective-permute-start | bytes 196616 | tf_op jit(solution)/shard_map/ppermute | solution.py:370
  36.8 2.6 %collective-permute-start.13 = (f32[128,128]{1,0:T(8,128)S(1)}, f32[128,128]{1,0:T(8,128)S(1)}, u32[]{:S(2)}, u32[]{:S(2)}) collective-permute-start(f32[128,128]{1,0:T(8,128)S(1)} %get-tuple-element.66), channel_id=1, source_target_pairs={{0,16},{1,17},{2,18},{3,19},{4,20},{5,21},{6,22},{7,23},{8,24},{9,... | collective-permute-start | bytes 196616 | tf_op jit(solution)/shard_map/ppermute | solution.py:370
  39.4 0.0 collective-permute-done.15.refs_1_
  39.4 1.9 %collective-permute-start.14 = (f32[128,128]{1,0:T(8,128)S(1)}, f32[128,128]{1,0:T(8,128)S(1)}, u32[]{:S(2)}, u32[]{:S(2)}) collective-permute-start(f32[128,128]{1,0:T(8,128)S(1)} %get-tuple-element.67), channel_id=1, source_target_pairs={{0,24},{1,25},{2,26},{3,27},{4,28},{5,29},{6,30},{7,31},{8,16},{9,... | collective-permute-start | bytes 196616 | tf_op jit(solution)/shard_map/ppermute | solution.py:370
  41.2 0.0 collective-permute-done.16.refs_2_
  41.3 0.0 collective-permute-done.17.refs_3_
  41.3 0.8 %shard_map.96 = f32[2,512,128]{2,1,0:T(8,128)} custom-call(f32[256,128]{1,0:T(8,128)S(1)} %get-tuple-element.68.refs_0_, f32[256,128]{1,0:T(8,128)S(1)} %collective-permute-done.15.refs_1_, f32[256,128]{1,0:T(8,128)S(1)} %collective-permute-done.16.refs_2_, f32[256,128]{1,0:T(8,128)S(1)} %collective-permute-done.17.refs_3_), custom_call_target="tpu_custom_call" | custom-call | tf_op jit(solution)/shard_map/pallas_call | solution.py:460
  42.1 0.0 collective-permute-done.12.refs_1_
  42.1 1.2 %collective-permute-done.13.refs_2_ = f32[128,128]{1,0:T(8,128)S(1)} collective-permute-done((f32[128,128]{1,0:T(8,128)S(1)}, f32[128,128]{1,0:T(8,128)S(1)}, u32[]{:S(2)}, u32[]{:S(2)}) %collective-permute-start.13) | collective-permute-done | bytes 65568 | tf_op jit(solution)/shard_map/ppermute | solution.py:370
  43.3 2.2 %collective-permute-done.14.refs_3_ = f32[128,128]{1,0:T(8,128)S(1)} collective-permute-done((f32[128,128]{1,0:T(8,128)S(1)}, f32[128,128]{1,0:T(8,128)S(1)}, u32[]{:S(2)}, u32[]{:S(2)}) %collective-permute-start.14) | collective-permute-done | bytes 65568 | tf_op jit(solution)/shard_map/ppermute | solution.py:370
  45.5 0.6 %shard_map.95 = f32[2,64,128]{2,1,0:T(8,128)} custom-call(f32[128,128]{1,0:T(8,128)S(1)} %get-tuple-element.64.refs_0_, f32[128,128]{1,0:T(8,128)S(1)} %collective-permute-done.12.refs_1_, f32[128,128]{1,0:T(8,128)S(1)} %collective-permute-done.13.refs_2_, f32[128,128]{1,0:T(8,128)S(1)} %collective-permute-done.14.refs_3_), custom_call_target="tpu_custom_call" | custom-call | tf_op jit(solution)/shard_map/pallas_call | solution.py:461
  (3 shorter events, 0.1 us)
Async XLA Ops:
  1.8 9.5 %collective-permute-start = (f32[288,128]{1,0:T(8,128)S(1)}, f32[288,128]{1,0:T(8,128)S(1)}, u32[]{:S(2)}, u32[]{:S(2)}) collective-permute-start(f32[288,128]{1,0:T(8,128)S(1)} %get-tuple-element.42), channel_id=1, source_target_pairs={{0,1},{1,0},{2,3},{3,2},{4,5},{5,4},{6,7},{7,6},{8,9},{9,8},{10,11... | collective-permute-start | bytes 442376 | tf_op jit(solution)/shard_map/ppermute | solution.py:370
  4.8 13.3 %collective-permute-start.1 = (f32[288,128]{1,0:T(8,128)S(1)}, f32[288,128]{1,0:T(8,128)S(1)}, u32[]{:S(2)}, u32[]{:S(2)}) collective-permute-start(f32[288,128]{1,0:T(8,128)S(1)} %get-tuple-element.43), channel_id=1, source_target_pairs={{0,2},{1,3},{2,0},{3,1},{4,6},{5,7},{6,4},{7,5},{8,10},{9,11},{10,... | collective-permute-start | bytes 442376 | tf_op jit(solution)/shard_map/ppermute | solution.py:370
  6.3 11.8 %collective-permute-start.2 = (f32[288,128]{1,0:T(8,128)S(1)}, f32[288,128]{1,0:T(8,128)S(1)}, u32[]{:S(2)}, u32[]{:S(2)}) collective-permute-start(f32[288,128]{1,0:T(8,128)S(1)} %get-tuple-element.44), channel_id=1, source_target_pairs={{0,3},{1,2},{2,1},{3,0},{4,7},{5,6},{6,5},{7,4},{8,11},{9,10},{10,... | collective-permute-start | bytes 442376 | tf_op jit(solution)/shard_map/ppermute | solution.py:370
  7.8 11.0 %collective-permute-start.3 = (f32[432,128]{1,0:T(8,128)S(1)}, f32[432,128]{1,0:T(8,128)S(1)}, u32[]{:S(2)}, u32[]{:S(2)}) collective-permute-start(f32[432,128]{1,0:T(8,128)S(1)} %get-tuple-element.48), channel_id=1, source_target_pairs={{0,1},{1,0},{2,3},{3,2},{4,5},{5,4},{6,7},{7,6},{8,9},{9,8},{10,11... | collective-permute-start | bytes 663560 | tf_op jit(solution)/shard_map/ppermute | solution.py:370
  9.8 13.0 %collective-permute-start.4 = (f32[432,128]{1,0:T(8,128)S(1)}, f32[432,128]{1,0:T(8,128)S(1)}, u32[]{:S(2)}, u32[]{:S(2)}) collective-permute-start(f32[432,128]{1,0:T(8,128)S(1)} %get-tuple-element.49), channel_id=1, source_target_pairs={{0,2},{1,3},{2,0},{3,1},{4,6},{5,7},{6,4},{7,5},{8,10},{9,11},{10,... | collective-permute-start | bytes 663560 | tf_op jit(solution)/shard_map/ppermute | solution.py:370
  11.3 11.5 %collective-permute-start.5 = (f32[432,128]{1,0:T(8,128)S(1)}, f32[432,128]{1,0:T(8,128)S(1)}, u32[]{:S(2)}, u32[]{:S(2)}) collective-permute-start(f32[432,128]{1,0:T(8,128)S(1)} %get-tuple-element.50), channel_id=1, source_target_pairs={{0,3},{1,2},{2,1},{3,0},{4,7},{5,6},{6,5},{7,4},{8,11},{9,10},{10,... | collective-permute-start | bytes 663560 | tf_op jit(solution)/shard_map/ppermute | solution.py:370
  18.2 4.6 %collective-permute-start.6 = (f32[216,128]{1,0:T(8,128)S(1)}, f32[216,128]{1,0:T(8,128)S(1)}, u32[]{:S(2)}, u32[]{:S(2)}) collective-permute-start(f32[216,128]{1,0:T(8,128)S(1)} %get-tuple-element.55), channel_id=1, source_target_pairs={{0,4},{1,5},{2,6},{3,7},{4,0},{5,1},{6,2},{7,3},{8,12},{9,13},{10,... | collective-permute-start | bytes 331784 | tf_op jit(solution)/shard_map/ppermute | solution.py:370
  18.3 4.5 %collective-permute-start.7 = (f32[216,128]{1,0:T(8,128)S(1)}, f32[216,128]{1,0:T(8,128)S(1)}, u32[]{:S(2)}, u32[]{:S(2)}) collective-permute-start(f32[216,128]{1,0:T(8,128)S(1)} %get-tuple-element.56), channel_id=1, source_target_pairs={{0,4},{1,5},{2,6},{3,7},{4,0},{5,1},{6,2},{7,3},{8,12},{9,13},{10,... | collective-permute-start | bytes 331784 | tf_op jit(solution)/shard_map/ppermute | solution.py:370
  25.7 1.6 %collective-permute-start.8 = (f32[512,128]{1,0:T(8,128)S(1)}, f32[512,128]{1,0:T(8,128)S(1)}, u32[]{:S(2)}, u32[]{:S(2)}) collective-permute-start(f32[512,128]{1,0:T(8,128)S(1)} %shard_map.92), channel_id=1, source_target_pairs={{0,4},{1,5},{2,6},{3,7},{4,0},{5,1},{6,2},{7,3},{8,12},{9,13},{10,... | collective-permute-start | bytes 786440 | tf_op jit(solution)/shard_map/ppermute | solution.py:370
  27.3 5.6 %collective-permute-start.9 = (f32[128,128]{1,0:T(8,128)S(1)}, f32[128,128]{1,0:T(8,128)S(1)}, u32[]{:S(2)}, u32[]{:S(2)}) collective-permute-start(f32[128,128]{1,0:T(8,128)S(1)} %get-tuple-element.61), channel_id=1, source_target_pairs={{0,1},{1,0},{2,3},{3,2},{4,5},{5,4},{6,7},{7,6},{8,9},{9,8},{10,11... | collective-permute-start | bytes 196616 | tf_op jit(solution)/shard_map/ppermute | solution.py:370
  28.6 5.8 %collective-permute-start.10 = (f32[128,128]{1,0:T(8,128)S(1)}, f32[128,128]{1,0:T(8,128)S(1)}, u32[]{:S(2)}, u32[]{:S(2)}) collective-permute-start(f32[128,128]{1,0:T(8,128)S(1)} %get-tuple-element.62), channel_id=1, source_target_pairs={{0,2},{1,3},{2,0},{3,1},{4,6},{5,7},{6,4},{7,5},{8,10},{9,11},{10,... | collective-permute-start | bytes 196616 | tf_op jit(solution)/shard_map/ppermute | solution.py:370
  29.5 5.9 %collective-permute-start.11 = (f32[128,128]{1,0:T(8,128)S(1)}, f32[128,128]{1,0:T(8,128)S(1)}, u32[]{:S(2)}, u32[]{:S(2)}) collective-permute-start(f32[128,128]{1,0:T(8,128)S(1)} %get-tuple-element.63), channel_id=1, source_target_pairs={{0,3},{1,2},{2,1},{3,0},{4,7},{5,6},{6,5},{7,4},{8,11},{9,10},{10,... | collective-permute-start | bytes 196616 | tf_op jit(solution)/shard_map/ppermute | solution.py:370
  30.9 8.5 %collective-permute-start.15 = (f32[256,128]{1,0:T(8,128)S(1)}, f32[256,128]{1,0:T(8,128)S(1)}, u32[]{:S(2)}, u32[]{:S(2)}) collective-permute-start(f32[256,128]{1,0:T(8,128)S(1)} %get-tuple-element.69), channel_id=1, source_target_pairs={{0,1},{1,0},{2,3},{3,2},{4,5},{5,4},{6,7},{7,6},{8,9},{9,8},{10,11... | collective-permute-start | bytes 393224 | tf_op jit(solution)/shard_map/ppermute | solution.py:370
  32.1 9.1 %collective-permute-start.16 = (f32[256,128]{1,0:T(8,128)S(1)}, f32[256,128]{1,0:T(8,128)S(1)}, u32[]{:S(2)}, u32[]{:S(2)}) collective-permute-start(f32[256,128]{1,0:T(8,128)S(1)} %get-tuple-element.70), channel_id=1, source_target_pairs={{0,2},{1,3},{2,0},{3,1},{4,6},{5,7},{6,4},{7,5},{8,10},{9,11},{10,... | collective-permute-start | bytes 393224 | tf_op jit(solution)/shard_map/ppermute | solution.py:370
  32.9 8.3 %collective-permute-start.17 = (f32[256,128]{1,0:T(8,128)S(1)}, f32[256,128]{1,0:T(8,128)S(1)}, u32[]{:S(2)}, u32[]{:S(2)}) collective-permute-start(f32[256,128]{1,0:T(8,128)S(1)} %get-tuple-element.71), channel_id=1, source_target_pairs={{0,3},{1,2},{2,1},{3,0},{4,7},{5,6},{6,5},{7,4},{8,11},{9,10},{10,... | collective-permute-start | bytes 393224 | tf_op jit(solution)/shard_map/ppermute | solution.py:370
  35.4 6.7 %collective-permute-start.12 = (f32[128,128]{1,0:T(8,128)S(1)}, f32[128,128]{1,0:T(8,128)S(1)}, u32[]{:S(2)}, u32[]{:S(2)}) collective-permute-start(f32[128,128]{1,0:T(8,128)S(1)} %get-tuple-element.65), channel_id=1, source_target_pairs={{0,8},{1,9},{2,10},{3,11},{4,12},{5,13},{6,14},{7,15},{8,0},{9,1},... | collective-permute-start | bytes 196616 | tf_op jit(solution)/shard_map/ppermute | solution.py:370
  36.8 6.5 %collective-permute-start.13 = (f32[128,128]{1,0:T(8,128)S(1)}, f32[128,128]{1,0:T(8,128)S(1)}, u32[]{:S(2)}, u32[]{:S(2)}) collective-permute-start(f32[128,128]{1,0:T(8,128)S(1)} %get-tuple-element.66), channel_id=1, source_target_pairs={{0,16},{1,17},{2,18},{3,19},{4,20},{5,21},{6,22},{7,23},{8,24},{9,... | collective-permute-start | bytes 196616 | tf_op jit(solution)/shard_map/ppermute | solution.py:370
  39.4 6.1 %collective-permute-start.14 = (f32[128,128]{1,0:T(8,128)S(1)}, f32[128,128]{1,0:T(8,128)S(1)}, u32[]{:S(2)}, u32[]{:S(2)}) collective-permute-start(f32[128,128]{1,0:T(8,128)S(1)} %get-tuple-element.67), channel_id=1, source_target_pairs={{0,24},{1,25},{2,26},{3,27},{4,28},{5,29},{6,30},{7,31},{8,16},{9,... | collective-permute-start | bytes 196616 | tf_op jit(solution)/shard_map/ppermute | solution.py:370

commit v4 on v3

--- a/solution.py
+++ b/solution.py
@@ -326,7 +326,7 @@
 
 
 def sort(blocks, *refs):
-    came, outs, held = refs[:blocks], refs[blocks : 2 * blocks], refs[2 * blocks]
+    came, outs, held = refs[:blocks][::-1], refs[blocks : 2 * blocks], refs[2 * blocks]
     dom, pair = lax.axis_index("dom"), lax.axis_index("shot") // 2
     for s in range(blocks):
         held[lax.bitwise_xor(dom, s)] = came[s][...]
@@ -455,10 +455,10 @@
         scratch=[pltpu.VMEM((blocks, planes * half, depth), jnp.float32)],
         flops=1400 * 1000 * 1000,
         moved=1,
-    )(*pieces)
+    )(*pieces[::-1])
     pieces = over_pairs(pieces)
     (wave_next,) = call(functools.partial(join, planes, rows), [(planes, ny, depth)], in_specs=[VMEM] * blocks)(*turned)
-    (total,) = call(functools.partial(add, planes), [(planes, half, depth)], in_specs=[VMEM] * blocks)(*pieces)
+    (total,) = call(functools.partial(add, planes), [(planes, half, depth)], in_specs=[VMEM] * blocks)(*pieces[::-1])
     return total, wave_next[None]
 
 

time: 46.3 us -> 44.7 us (0.965)
  starting transfers between devices: 22.8 us -> 21.4 us
    ppermute x18, starting transfers between devices: 22.8 us -> 21.4 us  [across(): return lax.ppermute(array, ('shot', 'dom'), pairs)]
  transfers between devices with their start and end apart: 18 -> 18, of which waited for: 5 -> 6; matrix products, arithmetic and copies ran while one was open for 0% -> 0% of each run, Pallas kernels for 18% -> 19%
where the time goes in v4:
time: 44.7 us; the launch traced here: 44.4 us
  starting transfers between devices  21.4 us (48%)
  Pallas kernels  13.2 us (30%)
  waiting for transfers between devices  8.38 us (19%)
  between operations  1.39 us (3%)
    ppermute x18, starting transfers between devices, across(): return lax.ppermute(array, ('shot', 'dom'), pairs)  21.4 us
    ppermute x18, waiting for transfers between devices, across(): return lax.ppermute(array, ('shot', 'dom'), pairs)  8.38 us
    pallas_call x1, Pallas kernels, shards(): call(functools.partial(spread, depth, ny, rows, listed), [(nx * tall, dep...  4.96 us
    pallas_call x2, Pallas kernels, shards(): call(functools.partial(backward, mine, rows), [(nx * half, depth)], in_sp...  2.41 us
    pallas_call x1, Pallas kernels, shards(): call(functools.partial(forward, blocks, planes, rows, ny), [(NT, *padded)...  1.72 us
    pallas_call x1, Pallas kernels, shards(): call(functools.partial(pack_late, blocks, planes, rows), [((2 * planes -...  1.4 us
    pallas_call x1, Pallas kernels, shards(): call(functools.partial(pack_early, blocks, planes, rows), [(tall + planes...  1.17 us
  transfers between devices with their start and end apart: 18, of which 6 were waited for; matrix products, arithmetic and copies ran while one was open for 0% of the time, Pallas kernels for 19%

profile of v4, /device:TPU:0, one launch (start us, length us, event | category | flops | bytes accessed | tf_op | source)
XLA Modules:
  0.0 44.4 jit_solution(11288164808012096832)
XLA Ops:
  0.6 1.2 %shard_map.87 = (f32[288,128]{1,0:T(8,128)S(1)}, f32[288,128]{1,0:T(8,128)S(1)}, f32[288,128]{1,0:T(8,128)S(1)}) custom-call(f32[2,512,128]{2,1,0:T(8,128)} %kappa.3, f32[2,512,128]{2,1,0:T(8,128)} %bitcast.3), custom_call_target="tpu_custom_call" | custom-call | tf_op jit(solution)/shard_map/pallas_call | solution.py:380
  1.8 3.0 %collective-permute-start = (f32[288,128]{1,0:T(8,128)S(1)}, f32[288,128]{1,0:T(8,128)S(1)}, u32[]{:S(2)}, u32[]{:S(2)}) collective-permute-start(f32[288,128]{1,0:T(8,128)S(1)} %get-tuple-element.42), channel_id=1, source_target_pairs={{0,1},{1,0},{2,3},{3,2},{4,5},{5,4},{6,7},{7,6},{8,9},{9,8},{10,11... | collective-permute-start | bytes 442376 | tf_op jit(solution)/shard_map/ppermute | solution.py:370
  4.8 1.5 %collective-permute-start.1 = (f32[288,128]{1,0:T(8,128)S(1)}, f32[288,128]{1,0:T(8,128)S(1)}, u32[]{:S(2)}, u32[]{:S(2)}) collective-permute-start(f32[288,128]{1,0:T(8,128)S(1)} %get-tuple-element.43), channel_id=1, source_target_pairs={{0,2},{1,3},{2,0},{3,1},{4,6},{5,7},{6,4},{7,5},{8,10},{9,11},{10,... | collective-permute-start | bytes 442376 | tf_op jit(solution)/shard_map/ppermute | solution.py:370
  6.3 0.0 collective-permute-start.2
  6.4 1.4 %shard_map.88 = (f32[432,128]{1,0:T(8,128)S(1)}, f32[432,128]{1,0:T(8,128)S(1)}, f32[432,128]{1,0:T(8,128)S(1)}, f32[864,128]{1,0:T(8,128)S(1)}) custom-call(f32[2,512,128]{2,1,0:T(8,128)} %kappa.3, f32[2,512,128]{2,1,0:T(8,128)} %bitcast.4, f32[2,512,128]{2,1,0:T(8,128)} %bitcast.5), custom_call_target="tpu_custom_call" | custom-call | tf_op jit(solution)/shard_map/pallas_call | solution.py:392
  7.8 2.0 %collective-permute-start.3 = (f32[432,128]{1,0:T(8,128)S(1)}, f32[432,128]{1,0:T(8,128)S(1)}, u32[]{:S(2)}, u32[]{:S(2)}) collective-permute-start(f32[432,128]{1,0:T(8,128)S(1)} %get-tuple-element.48), channel_id=1, source_target_pairs={{0,1},{1,0},{2,3},{3,2},{4,5},{5,4},{6,7},{7,6},{8,9},{9,8},{10,11... | collective-permute-start | bytes 663560 | tf_op jit(solution)/shard_map/ppermute | solution.py:370
  9.8 1.5 %collective-permute-start.4 = (f32[432,128]{1,0:T(8,128)S(1)}, f32[432,128]{1,0:T(8,128)S(1)}, u32[]{:S(2)}, u32[]{:S(2)}) collective-permute-start(f32[432,128]{1,0:T(8,128)S(1)} %get-tuple-element.49), channel_id=1, source_target_pairs={{0,2},{1,3},{2,0},{3,1},{4,6},{5,7},{6,4},{7,5},{8,10},{9,11},{10,... | collective-permute-start | bytes 663560 | tf_op jit(solution)/shard_map/ppermute | solution.py:370
  11.3 0.0 collective-permute-done.refs_0_
  11.3 1.2 %collective-permute-start.5 = (f32[432,128]{1,0:T(8,128)S(1)}, f32[432,128]{1,0:T(8,128)S(1)}, u32[]{:S(2)}, u32[]{:S(2)}) collective-permute-start(f32[432,128]{1,0:T(8,128)S(1)} %get-tuple-element.50), channel_id=1, source_target_pairs={{0,3},{1,2},{2,1},{3,0},{4,7},{5,6},{6,5},{7,4},{8,11},{9,10},{10,... | collective-permute-start | bytes 663560 | tf_op jit(solution)/shard_map/ppermute | solution.py:370
  13.2 5.0 %shard_map.86 = (f32[1152,128]{1,0:T(8,128)S(1)}, f32[4,1152,128]{2,1,0:T(8,128)S(1)}, f32[4,128]{1,0:T(4,128)S(1)}) custom-call(s32[1]{0:T(128)S(6)} %copy.9.source, f32[1,4]{1,0:T(1,128)} %lists_at.1, s32[1,2048]{1,0:T(1,128)} %cells_at.1, f32[1,4,2048]{2,1,0:T(4,128)} %observed_at.1), custom_call_target="tpu_custom_call" | custom-call | flops 1000000000 | bytes 1 | tf_op jit(solution)/shard_map/pallas_call | solution.py:402
  18.1 0.0 collective-permute-done.1.refs_1_
  18.1 0.0 collective-permute-done.2.refs_2_
  18.2 0.1 collective-permute-start.6
  18.3 0.5 %collective-permute-start.7 = (f32[216,128]{1,0:T(8,128)S(1)}, f32[216,128]{1,0:T(8,128)S(1)}, u32[]{:S(2)}, u32[]{:S(2)}) collective-permute-start(f32[216,128]{1,0:T(8,128)S(1)} %get-tuple-element.56), channel_id=1, source_target_pairs={{0,4},{1,5},{2,6},{3,7},{4,0},{5,1},{6,2},{7,3},{8,12},{9,13},{10,... | collective-permute-start | bytes 331784 | tf_op jit(solution)/shard_map/ppermute | solution.py:370
  18.8 0.0 collective-permute-done.3.refs_3_
  18.8 4.0 %collective-permute-done.4.refs_4_ = f32[432,128]{1,0:T(8,128)S(1)} collective-permute-done((f32[432,128]{1,0:T(8,128)S(1)}, f32[432,128]{1,0:T(8,128)S(1)}, u32[]{:S(2)}, u32[]{:S(2)}) %collective-permute-start.4) | collective-permute-done | bytes 221216 | tf_op jit(solution)/shard_map/ppermute | solution.py:370
  22.8 0.0 collective-permute-done.5.refs_5_
  22.8 0.0 collective-permute-done.6.refs_7_
  22.8 0.0 collective-permute-done.7.refs_8_
  22.8 1.7 %shard_map.90 = (f32[4,8,160,128]{3,2,1,0:T(8,128)S(1)}, f32[4,8,144,128]{3,2,1,0:T(8,128)S(1)}, f32[8,160,128]{2,1,0:T(8,128)S(1)}, f32[256,128]{1,0:T(8,128)S(...) custom-call(s32[1]{0:T(128)S(6)} %copy.9.source, ...), custom_call_target="tpu_custom_call" | custom-call | flops 9437184 | bytes 9437184 | tf_op jit(solution)/shard_map/pallas_call | solution.py:421
  24.5 1.2 %shard_map.92 = f32[512,128]{1,0:T(8,128)S(1)} custom-call(f32[1152,128]{1,0:T(8,128)S(1)} %get-tuple-element.37.count, f32[4,1152,128]{2,1,0:T(8,128)S(1)} %get-tuple-element.38.heard, f32[4,8,160,128]{3,2,1,0:T(8,128)S(1)} %get-tuple-element.57.wave, f32[4,8,144,128]{3,2,1,0:T(8,128)S(1)} %get-tuple-element.58.lap, f32[8,160,128]{2,1,0:T(8,128)S(1)} %get-tuple-element.59.model), custom_call_target="tpu_custom_call" | custom-call | flops 7077888 | bytes 7077888 | tf_op jit(solution)/shard_map/pallas_call | solution.py:432
  25.7 0.1 collective-permute-start.8
  25.8 1.2 %shard_map.91.keep = f32[512,128]{1,0:T(8,128)S(1)} custom-call(f32[1152,128]{1,0:T(8,128)S(1)} %get-tuple-element.37.count, f32[4,1152,128]{2,1,0:T(8,128)S(1)} %get-tuple-element.38.heard, f32[4,8,160,128]{3,2,1,0:T(8,128)S(1)} %get-tuple-element.57.wave, f32[4,8,144,128]{3,2,1,0:T(8,128)S(1)} %get-tuple-element.58.lap, ...), custom_call_target="tpu_custom_call" | custom-call | flops 7077888 | bytes 7077888 | tf_op jit(solution)/shard_map/pallas_call | solution.py:432
  27.0 0.3 collective-permute-done.8.got
  27.4 1.5 %collective-permute-start.9 = (f32[128,128]{1,0:T(8,128)S(1)}, f32[128,128]{1,0:T(8,128)S(1)}, u32[]{:S(2)}, u32[]{:S(2)}) collective-permute-start(f32[128,128]{1,0:T(8,128)S(1)} %get-tuple-element.60), channel_id=1, source_target_pairs={{0,3},{1,2},{2,1},{3,0},{4,7},{5,6},{6,5},{7,4},{8,11},{9,10},{10,... | collective-permute-start | bytes 196616 | tf_op jit(solution)/shard_map/ppermute | solution.py:370
  28.9 1.2 %collective-permute-start.10 = (f32[128,128]{1,0:T(8,128)S(1)}, f32[128,128]{1,0:T(8,128)S(1)}, u32[]{:S(2)}, u32[]{:S(2)}) collective-permute-start(f32[128,128]{1,0:T(8,128)S(1)} %get-tuple-element.61), channel_id=1, source_target_pairs={{0,2},{1,3},{2,0},{3,1},{4,6},{5,7},{6,4},{7,5},{8,10},{9,11},{10,... | collective-permute-start | bytes 196616 | tf_op jit(solution)/shard_map/ppermute | solution.py:370
  30.1 0.8 %collective-permute-start.11 = (f32[128,128]{1,0:T(8,128)S(1)}, f32[128,128]{1,0:T(8,128)S(1)}, u32[]{:S(2)}, u32[]{:S(2)}) collective-permute-start(f32[128,128]{1,0:T(8,128)S(1)} %get-tuple-element.62), channel_id=1, source_target_pairs={{0,1},{1,0},{2,3},{3,2},{4,5},{5,4},{6,7},{7,6},{8,9},{9,8},{10,11... | collective-permute-start | bytes 196616 | tf_op jit(solution)/shard_map/ppermute | solution.py:370
  30.9 1.2 %collective-permute-start.15 = (f32[256,128]{1,0:T(8,128)S(1)}, f32[256,128]{1,0:T(8,128)S(1)}, u32[]{:S(2)}, u32[]{:S(2)}) collective-permute-start(f32[256,128]{1,0:T(8,128)S(1)} %get-tuple-element.69), channel_id=1, source_target_pairs={{0,1},{1,0},{2,3},{3,2},{4,5},{5,4},{6,7},{7,6},{8,9},{9,8},{10,11... | collective-permute-start | bytes 393224 | tf_op jit(solution)/shard_map/ppermute | solution.py:370
  32.1 0.8 %collective-permute-start.16 = (f32[256,128]{1,0:T(8,128)S(1)}, f32[256,128]{1,0:T(8,128)S(1)}, u32[]{:S(2)}, u32[]{:S(2)}) collective-permute-start(f32[256,128]{1,0:T(8,128)S(1)} %get-tuple-element.70), channel_id=1, source_target_pairs={{0,2},{1,3},{2,0},{3,1},{4,6},{5,7},{6,4},{7,5},{8,10},{9,11},{10,... | collective-permute-start | bytes 393224 | tf_op jit(solution)/shard_map/ppermute | solution.py:370
  32.9 0.0 collective-permute-done.9.refs_0_
  32.9 1.5 %collective-permute-start.17 = (f32[256,128]{1,0:T(8,128)S(1)}, f32[256,128]{1,0:T(8,128)S(1)}, u32[]{:S(2)}, u32[]{:S(2)}) collective-permute-start(f32[256,128]{1,0:T(8,128)S(1)} %get-tuple-element.71), channel_id=1, source_target_pairs={{0,3},{1,2},{2,1},{3,0},{4,7},{5,6},{6,5},{7,4},{8,11},{9,10},{10,... | collective-permute-start | bytes 393224 | tf_op jit(solution)/shard_map/ppermute | solution.py:370
  34.4 0.0 collective-permute-done.10.refs_1_
  34.4 0.7 %collective-permute-done.11.refs_2_ = f32[128,128]{1,0:T(8,128)S(1)} collective-permute-done((f32[128,128]{1,0:T(8,128)S(1)}, f32[128,128]{1,0:T(8,128)S(1)}, u32[]{:S(2)}, u32[]{:S(2)}) %collective-permute-start.11) | collective-permute-done | bytes 65568 | tf_op jit(solution)/shard_map/ppermute | solution.py:370
  35.1 3.5 %collective-permute-start.12 = (f32[128,128]{1,0:T(8,128)S(1)}, f32[128,128]{1,0:T(8,128)S(1)}, u32[]{:S(2)}, u32[]{:S(2)}) collective-permute-start(f32[128,128]{1,0:T(8,128)S(1)} %get-tuple-element.64), channel_id=1, source_target_pairs={{0,24},{1,25},{2,26},{3,27},{4,28},{5,29},{6,30},{7,31},{8,16},{9,... | collective-permute-start | bytes 196616 | tf_op jit(solution)/shard_map/ppermute | solution.py:370
  38.6 0.0 collective-permute-start.13
  38.6 0.0 collective-permute-done.15.refs_1_
  38.6 1.0 %collective-permute-start.14 = (f32[128,128]{1,0:T(8,128)S(1)}, f32[128,128]{1,0:T(8,128)S(1)}, u32[]{:S(2)}, u32[]{:S(2)}) collective-permute-start(f32[128,128]{1,0:T(8,128)S(1)} %get-tuple-element.66), channel_id=1, source_target_pairs={{0,8},{1,9},{2,10},{3,11},{4,12},{5,13},{6,14},{7,15},{8,0},{9,1},... | collective-permute-start | bytes 196616 | tf_op jit(solution)/shard_map/ppermute | solution.py:370
  39.6 0.0 collective-permute-done.16.refs_2_
  39.6 0.4 %collective-permute-done.17.refs_3_ = f32[256,128]{1,0:T(8,128)S(1)} collective-permute-done((f32[256,128]{1,0:T(8,128)S(1)}, f32[256,128]{1,0:T(8,128)S(1)}, u32[]{:S(2)}, u32[]{:S(2)}) %collective-permute-start.17) | collective-permute-done | bytes 131104 | tf_op jit(solution)/shard_map/ppermute | solution.py:370
  40.1 0.8 %shard_map.96 = f32[2,512,128]{2,1,0:T(8,128)} custom-call(f32[256,128]{1,0:T(8,128)S(1)} %get-tuple-element.68.refs_0_, f32[256,128]{1,0:T(8,128)S(1)} %collective-permute-done.15.refs_1_, f32[256,128]{1,0:T(8,128)S(1)} %collective-permute-done.16.refs_2_, f32[256,128]{1,0:T(8,128)S(1)} %collective-permute-done.17.refs_3_), custom_call_target="tpu_custom_call" | custom-call | tf_op jit(solution)/shard_map/pallas_call | solution.py:460
  40.9 0.4 collective-permute-done.12.refs_0_
  41.3 2.5 %collective-permute-done.13.refs_1_ = f32[128,128]{1,0:T(8,128)S(1)} collective-permute-done((f32[128,128]{1,0:T(8,128)S(1)}, f32[128,128]{1,0:T(8,128)S(1)}, u32[]{:S(2)}, u32[]{:S(2)}) %collective-permute-start.13) | collective-permute-done | bytes 65568 | tf_op jit(solution)/shard_map/ppermute | solution.py:370
  43.8 0.0 collective-permute-done.14.refs_2_
  43.8 0.6 %shard_map.95 = f32[2,64,128]{2,1,0:T(8,128)} custom-call(f32[128,128]{1,0:T(8,128)S(1)} %collective-permute-done.12.refs_0_, f32[128,128]{1,0:T(8,128)S(1)} %collective-permute-done.13.refs_1_, f32[128,128]{1,0:T(8,128)S(1)} %collective-permute-done.14.refs_2_, f32[128,128]{1,0:T(8,128)S(1)} %get-tuple-element.67.refs_3_), custom_call_target="tpu_custom_call" | custom-call | tf_op jit(solution)/shard_map/pallas_call | solution.py:461
  (3 shorter events, 0.1 us)
Async XLA Ops:
  1.8 9.5 %collective-permute-start = (f32[288,128]{1,0:T(8,128)S(1)}, f32[288,128]{1,0:T(8,128)S(1)}, u32[]{:S(2)}, u32[]{:S(2)}) collective-permute-start(f32[288,128]{1,0:T(8,128)S(1)} %get-tuple-element.42), channel_id=1, source_target_pairs={{0,1},{1,0},{2,3},{3,2},{4,5},{5,4},{6,7},{7,6},{8,9},{9,8},{10,11... | collective-permute-start | bytes 442376 | tf_op jit(solution)/shard_map/ppermute | solution.py:370
  4.8 13.3 %collective-permute-start.1 = (f32[288,128]{1,0:T(8,128)S(1)}, f32[288,128]{1,0:T(8,128)S(1)}, u32[]{:S(2)}, u32[]{:S(2)}) collective-permute-start(f32[288,128]{1,0:T(8,128)S(1)} %get-tuple-element.43), channel_id=1, source_target_pairs={{0,2},{1,3},{2,0},{3,1},{4,6},{5,7},{6,4},{7,5},{8,10},{9,11},{10,... | collective-permute-start | bytes 442376 | tf_op jit(solution)/shard_map/ppermute | solution.py:370
  6.3 11.8 %collective-permute-start.2 = (f32[288,128]{1,0:T(8,128)S(1)}, f32[288,128]{1,0:T(8,128)S(1)}, u32[]{:S(2)}, u32[]{:S(2)}) collective-permute-start(f32[288,128]{1,0:T(8,128)S(1)} %get-tuple-element.44), channel_id=1, source_target_pairs={{0,3},{1,2},{2,1},{3,0},{4,7},{5,6},{6,5},{7,4},{8,11},{9,10},{10,... | collective-permute-start | bytes 442376 | tf_op jit(solution)/shard_map/ppermute | solution.py:370
  7.8 11.0 %collective-permute-start.3 = (f32[432,128]{1,0:T(8,128)S(1)}, f32[432,128]{1,0:T(8,128)S(1)}, u32[]{:S(2)}, u32[]{:S(2)}) collective-permute-start(f32[432,128]{1,0:T(8,128)S(1)} %get-tuple-element.48), channel_id=1, source_target_pairs={{0,1},{1,0},{2,3},{3,2},{4,5},{5,4},{6,7},{7,6},{8,9},{9,8},{10,11... | collective-permute-start | bytes 663560 | tf_op jit(solution)/shard_map/ppermute | solution.py:370
  9.8 13.0 %collective-permute-start.4 = (f32[432,128]{1,0:T(8,128)S(1)}, f32[432,128]{1,0:T(8,128)S(1)}, u32[]{:S(2)}, u32[]{:S(2)}) collective-permute-start(f32[432,128]{1,0:T(8,128)S(1)} %get-tuple-element.49), channel_id=1, source_target_pairs={{0,2},{1,3},{2,0},{3,1},{4,6},{5,7},{6,4},{7,5},{8,10},{9,11},{10,... | collective-permute-start | bytes 663560 | tf_op jit(solution)/shard_map/ppermute | solution.py:370
  11.3 11.5 %collective-permute-start.5 = (f32[432,128]{1,0:T(8,128)S(1)}, f32[432,128]{1,0:T(8,128)S(1)}, u32[]{:S(2)}, u32[]{:S(2)}) collective-permute-start(f32[432,128]{1,0:T(8,128)S(1)} %get-tuple-element.50), channel_id=1, source_target_pairs={{0,3},{1,2},{2,1},{3,0},{4,7},{5,6},{6,5},{7,4},{8,11},{9,10},{10,... | collective-permute-start | bytes 663560 | tf_op jit(solution)/shard_map/ppermute | solution.py:370
  18.2 4.6 %collective-permute-start.6 = (f32[216,128]{1,0:T(8,128)S(1)}, f32[216,128]{1,0:T(8,128)S(1)}, u32[]{:S(2)}, u32[]{:S(2)}) collective-permute-start(f32[216,128]{1,0:T(8,128)S(1)} %get-tuple-element.55), channel_id=1, source_target_pairs={{0,4},{1,5},{2,6},{3,7},{4,0},{5,1},{6,2},{7,3},{8,12},{9,13},{10,... | collective-permute-start | bytes 331784 | tf_op jit(solution)/shard_map/ppermute | solution.py:370
  18.3 4.5 %collective-permute-start.7 = (f32[216,128]{1,0:T(8,128)S(1)}, f32[216,128]{1,0:T(8,128)S(1)}, u32[]{:S(2)}, u32[]{:S(2)}) collective-permute-start(f32[216,128]{1,0:T(8,128)S(1)} %get-tuple-element.56), channel_id=1, source_target_pairs={{0,4},{1,5},{2,6},{3,7},{4,0},{5,1},{6,2},{7,3},{8,12},{9,13},{10,... | collective-permute-start | bytes 331784 | tf_op jit(solution)/shard_map/ppermute | solution.py:370
  25.7 1.6 %collective-permute-start.8 = (f32[512,128]{1,0:T(8,128)S(1)}, f32[512,128]{1,0:T(8,128)S(1)}, u32[]{:S(2)}, u32[]{:S(2)}) collective-permute-start(f32[512,128]{1,0:T(8,128)S(1)} %shard_map.92), channel_id=1, source_target_pairs={{0,4},{1,5},{2,6},{3,7},{4,0},{5,1},{6,2},{7,3},{8,12},{9,13},{10,... | collective-permute-start | bytes 786440 | tf_op jit(solution)/shard_map/ppermute | solution.py:370
  27.4 5.6 %collective-permute-start.9 = (f32[128,128]{1,0:T(8,128)S(1)}, f32[128,128]{1,0:T(8,128)S(1)}, u32[]{:S(2)}, u32[]{:S(2)}) collective-permute-start(f32[128,128]{1,0:T(8,128)S(1)} %get-tuple-element.60), channel_id=1, source_target_pairs={{0,3},{1,2},{2,1},{3,0},{4,7},{5,6},{6,5},{7,4},{8,11},{9,10},{10,... | collective-permute-start | bytes 196616 | tf_op jit(solution)/shard_map/ppermute | solution.py:370
  28.9 5.5 %collective-permute-start.10 = (f32[128,128]{1,0:T(8,128)S(1)}, f32[128,128]{1,0:T(8,128)S(1)}, u32[]{:S(2)}, u32[]{:S(2)}) collective-permute-start(f32[128,128]{1,0:T(8,128)S(1)} %get-tuple-element.61), channel_id=1, source_target_pairs={{0,2},{1,3},{2,0},{3,1},{4,6},{5,7},{6,4},{7,5},{8,10},{9,11},{10,... | collective-permute-start | bytes 196616 | tf_op jit(solution)/shard_map/ppermute | solution.py:370
  30.1 5.0 %collective-permute-start.11 = (f32[128,128]{1,0:T(8,128)S(1)}, f32[128,128]{1,0:T(8,128)S(1)}, u32[]{:S(2)}, u32[]{:S(2)}) collective-permute-start(f32[128,128]{1,0:T(8,128)S(1)} %get-tuple-element.62), channel_id=1, source_target_pairs={{0,1},{1,0},{2,3},{3,2},{4,5},{5,4},{6,7},{7,6},{8,9},{9,8},{10,11... | collective-permute-start | bytes 196616 | tf_op jit(solution)/shard_map/ppermute | solution.py:370
  30.9 7.7 %collective-permute-start.15 = (f32[256,128]{1,0:T(8,128)S(1)}, f32[256,128]{1,0:T(8,128)S(1)}, u32[]{:S(2)}, u32[]{:S(2)}) collective-permute-start(f32[256,128]{1,0:T(8,128)S(1)} %get-tuple-element.69), channel_id=1, source_target_pairs={{0,1},{1,0},{2,3},{3,2},{4,5},{5,4},{6,7},{7,6},{8,9},{9,8},{10,11... | collective-permute-start | bytes 393224 | tf_op jit(solution)/shard_map/ppermute | solution.py:370
  32.1 7.5 %collective-permute-start.16 = (f32[256,128]{1,0:T(8,128)S(1)}, f32[256,128]{1,0:T(8,128)S(1)}, u32[]{:S(2)}, u32[]{:S(2)}) collective-permute-start(f32[256,128]{1,0:T(8,128)S(1)} %get-tuple-element.70), channel_id=1, source_target_pairs={{0,2},{1,3},{2,0},{3,1},{4,6},{5,7},{6,4},{7,5},{8,10},{9,11},{10,... | collective-permute-start | bytes 393224 | tf_op jit(solution)/shard_map/ppermute | solution.py:370
  32.9 7.1 %collective-permute-start.17 = (f32[256,128]{1,0:T(8,128)S(1)}, f32[256,128]{1,0:T(8,128)S(1)}, u32[]{:S(2)}, u32[]{:S(2)}) collective-permute-start(f32[256,128]{1,0:T(8,128)S(1)} %get-tuple-element.71), channel_id=1, source_target_pairs={{0,3},{1,2},{2,1},{3,0},{4,7},{5,6},{6,5},{7,4},{8,11},{9,10},{10,... | collective-permute-start | bytes 393224 | tf_op jit(solution)/shard_map/ppermute | solution.py:370
  35.1 6.1 %collective-permute-start.12 = (f32[128,128]{1,0:T(8,128)S(1)}, f32[128,128]{1,0:T(8,128)S(1)}, u32[]{:S(2)}, u32[]{:S(2)}) collective-permute-start(f32[128,128]{1,0:T(8,128)S(1)} %get-tuple-element.64), channel_id=1, source_target_pairs={{0,24},{1,25},{2,26},{3,27},{4,28},{5,29},{6,30},{7,31},{8,16},{9,... | collective-permute-start | bytes 196616 | tf_op jit(solution)/shard_map/ppermute | solution.py:370
  38.6 5.2 %collective-permute-start.13 = (f32[128,128]{1,0:T(8,128)S(1)}, f32[128,128]{1,0:T(8,128)S(1)}, u32[]{:S(2)}, u32[]{:S(2)}) collective-permute-start(f32[128,128]{1,0:T(8,128)S(1)} %get-tuple-element.65), channel_id=1, source_target_pairs={{0,16},{1,17},{2,18},{3,19},{4,20},{5,21},{6,22},{7,23},{8,24},{9,... | collective-permute-start | bytes 196616 | tf_op jit(solution)/shard_map/ppermute | solution.py:370
  38.6 5.2 %collective-permute-start.14 = (f32[128,128]{1,0:T(8,128)S(1)}, f32[128,128]{1,0:T(8,128)S(1)}, u32[]{:S(2)}, u32[]{:S(2)}) collective-permute-start(f32[128,128]{1,0:T(8,128)S(1)} %get-tuple-element.66), channel_id=1, source_target_pairs={{0,8},{1,9},{2,10},{3,11},{4,12},{5,13},{6,14},{7,15},{8,0},{9,1},... | collective-permute-start | bytes 196616 | tf_op jit(solution)/shard_map/ppermute | solution.py:370

commit v5 on v4

--- a/solution.py
+++ b/solution.py
@@ -61,37 +61,34 @@
 def pack_early(blocks, planes, rows, kappa, now, *refs):
     outs, (held, model, whole, semaphores) = refs[: blocks - 1], refs[blocks - 1 :]
     dom, core = lax.axis_index("dom"), lax.rem(lax.axis_index("shot"), 2)
-    copies = [pltpu.make_async_copy(now.at[0], held.at[0], semaphores.at[planes])]
-    copies[0].start()
-    copies += fetch(kappa, model, semaphores)
+    waves, kappas = fetch(now, held, semaphores.at[0]), fetch(kappa, model, semaphores.at[1])
     tall = rows + 2 * EDGE
     half = tall // 2
-    copies[0].wait()
-    for s in range(1, blocks):
-        put(held, 0, lax.bitwise_xor(dom, s), blocks, rows, outs[s - 1], 0)
     for p in range(planes):
-        copies[1 + p].wait()
+        waves[p].wait()
+        for s in range(1, blocks):
+            put(held, p, lax.bitwise_xor(dom, s), blocks, rows, outs[s - 1], p * tall)
+    for p in range(planes):
+        kappas[p].wait()
         for s in range(1, blocks):
             put(model, p, lax.bitwise_xor(dom, s), blocks, rows, whole, 0)
-            at = tall + p * half
+            at = planes * tall + p * half
             outs[s - 1][at : at + half, :] = whole[pl.ds(pl.multiple_of(core * half, 8), half), :]
 
 
 def pack_late(blocks, planes, rows, kappa, now, before, *refs):
     outs, own, refs = refs[: blocks - 1], refs[blocks - 1], refs[blocks:]
     held, semaphores = refs[:3], refs[3]
-    fields = (now, before, kappa)
-    copies = [fetch(field, ref, semaphores.at[i]) for i, (field, ref) in enumerate(zip(fields, held))]
+    copies = [fetch(field, ref, semaphores.at[i]) for i, (field, ref) in enumerate(zip((before, now, kappa), held))]
     dom = lax.axis_index("dom")
     tall = rows + 2 * EDGE
     for f in range(3):
         for p in range(planes):
             copies[f][p].wait()
             put(held[f], p, dom, blocks, rows, own, (f * planes + p) * tall)
-            to = f * planes + p - 1
-            if f < 2 and to >= 0:
+            if f == 0:
                 for s in range(1, blocks):
-                    put(held[f], p, lax.bitwise_xor(dom, s), blocks, rows, outs[s - 1], to * tall)
+                    put(held[f], p, lax.bitwise_xor(dom, s), blocks, rows, outs[s - 1], p * tall)
 
 
 def gather(planes, half, *refs):
@@ -199,31 +196,41 @@
     return lanes == 0, lanes == depth - 1
 
 
+def begin(blocks, planes, rows, own, *refs):
+    early, wave, lap = refs[: blocks - 1], refs[blocks - 1], refs[blocks]
+    nx, tall, depth = lap.shape
+    dom = lax.axis_index("dom")
+    for s in range(blocks):
+        first = planes * lax.bitwise_xor(dom, s)
+        for p in range(planes):
+            part = early[s - 1][p * tall : (p + 1) * tall, :] if s > 0 else own[(planes + p) * tall : (planes + p + 1) * tall, :]
+            wave[first + p, 8 : 8 + tall, :] = part
+    some = 48
+    low, high = edges(some, depth)
+    for a in range(0, tall, some):
+        for x, held in sweep(wave, (), 8 + a, some, nx):
+            lap[x, a : a + some, :] = bend(wave, (), 8 + a, some, nx, x, held, low, high) - 6.0 * held[1]
+
+
 def forward(blocks, planes, rows, ny, source, pulse, *refs):
     early, late, own, refs = refs[: blocks - 1], refs[blocks - 1 : 2 * blocks - 2], refs[2 * blocks - 2], refs[2 * blocks - 1 :]
-    swapped, refs = refs[:planes], refs[planes:]
-    wave, lap, model, turned, start = *refs[:3], refs[3:-1], refs[-1]
+    swapped, start, bent, refs = refs[:planes], refs[planes], refs[planes + 1], refs[planes + 2 :]
+    wave, lap, model, turned = *refs[:3], refs[3:]
     nx, tall, depth = lap.shape[1:]
     dom, core = lax.axis_index("dom"), lax.rem(lax.axis_index("shot"), 2)
     half = tall // 2
     near = pl.ds(pl.multiple_of(8 + core * half, 8), half)
     other = pl.ds(pl.multiple_of(8 + (1 - core) * half, 8), half)
-    body = slice(8, 8 + tall)
     for s in range(blocks):
         first = planes * lax.bitwise_xor(dom, s)
         for p in range(planes):
             if s == 0:
-                for f, to in enumerate((start.at[0], start.at[1], model)):
-                    at = (f * planes + p) * tall
-                    to[first + p, body, :] = own[at : at + tall, :]
-                continue
-            for f in range(2):
-                i = f * planes + p - 1
-                part = late[s - 1][i * tall : (i + 1) * tall, :] if i >= 0 else early[s - 1][0:tall, :]
-                start[f, first + p, body, :] = part
-            at = tall + p * half
-            model[first + p, near, :] = early[s - 1][at : at + half, :]
-            model[first + p, other, :] = swapped[p][(s - 1) * half : s * half, :]
+                at = (2 * planes + p) * tall
+                model[first + p, 8 : 8 + tall, :] = own[at : at + tall, :]
+            else:
+                at = planes * tall + p * half
+                model[first + p, near, :] = early[s - 1][at : at + half, :]
+                model[first + p, other, :] = swapped[p][(s - 1) * half : s * half, :]
 
     some = 48
     low, high = edges(some, depth)
@@ -238,16 +245,25 @@
         def _():
             wave[n, sx, pl.ds(sy, 1), :] = wave[n, sx, pl.ds(sy, 1), :] + pulse[n : n + 1, :]
 
-    for n in range(NT):
-        source_of = (wave, (n - 1,)) if n > 0 else (start, (0,))
-        older = (wave, n - 2) if n > 1 else (start, 1 - n)
+    for s in range(blocks):
+        for p in range(planes):
+            x = planes * lax.bitwise_xor(dom, s) + p
+            for a in range(0, tall, some):
+                rows_at = slice(8 + a, 8 + a + some)
+                mid = start[x, rows_at, :]
+                old = late[s - 1] if s > 0 else own
+                new = (mid + mid) - old[p * tall + a : p * tall + a + some, :]
+                wave[0, x, rows_at, :] = new + model[x, rows_at, :] * bent[x, a : a + some, :]
+    inject(0)
+
+    for n in range(1, NT):
         for a in range(0, tall, some):
             rows_at = slice(8 + a, 8 + a + some)
-            for x, held in sweep(*source_of, 8 + a, some, nx):
+            for x, held in sweep(wave, (n - 1,), 8 + a, some, nx):
                 mid = held[1]
-                turn = bend(*source_of, 8 + a, some, nx, x, held, low, high) - 6.0 * mid
-                lap[n, x, a : a + some, :] = turn
-                old = older[0][older[1], x, rows_at, :]
+                turn = bend(wave, (n - 1,), 8 + a, some, nx, x, held, low, high) - 6.0 * mid
+                lap[n - 1, x, a : a + some, :] = turn
+                old = start[x, rows_at, :] if n == 1 else wave[n - 2, x, rows_at, :]
                 wave[n, x, rows_at, :] = (mid + mid) - old + model[x, rows_at, :] * turn
         inject(n)
 
@@ -257,8 +273,8 @@
             turned[s][p * rows : (p + 1) * rows, :] = wave[NT - 1, first + p, 8 + EDGE : 8 + EDGE + rows, :]
 
 
-def backward(mine, rows, count, heard, wave, lap, model, image, adjoint, weighted, gain):
-    nx, tall, depth = lap.shape[1:]
+def backward(mine, rows, count, heard, wave, lap, bent, model, image, adjoint, weighted, gain):
+    nx, tall, depth = bent.shape
     shot = lax.axis_index("shot")
     core = lax.rem(shot, 2)
     half = rows // 2
@@ -276,7 +292,7 @@
             now = count[at(a, off=x * tall), :] * wave[NT - 1, x, at(a, off=8), :] - heard[NT - 1, at(a, off=x * tall), :]
             adjoint[NT % 2, x, here, :] = now
             weighted[NT % 2, x, 8 + a : 8 + a + some, :] = now * model[x, at(a, off=8), :]
-            gain[x, here, :] = now * lap[NT - 1, x, at(a), :]
+            gain[x, here, :] = now * lap[NT - 2, x, at(a), :]
 
     for level in range(NT - 1, 1, -1):
         new, old = level % 2, 1 - level % 2
@@ -291,7 +307,7 @@
                     now = now - adjoint[new, x, here, :]
                 adjoint[new, x, here, :] = now
                 weighted[new, x, 8 + a : 8 + a + some, :] = now * model[x, at(a, off=8), :]
-                gain[x, here, :] = gain[x, here, :] + now * lap[level - 1, x, at(a), :]
+                gain[x, here, :] = gain[x, here, :] + now * lap[level - 2, x, at(a), :]
 
     some = 32 if half % 32 == 0 else 16
     low, high = edges(some, depth)
@@ -302,7 +318,7 @@
             after = adjoint[0, x, here, :]
             now = count[at(a, some, x * tall), :] * wave[0, x, at(a, some, 8), :]
             now = (now - heard[0, at(a, some, x * tall), :]) + (turn + (after + after)) - adjoint[1, x, here, :]
-            total = gain[x, here, :] + now * lap[0, x, at(a, some), :]
+            total = gain[x, here, :] + now * bent[x, at(a, some), :]
             image[x * half + a - EDGE : x * half + a - EDGE + some, :] = total / NT
 
     @pl.when(shot == 0)
@@ -379,26 +395,25 @@
     held = pltpu.VMEM((planes, ny, depth), jnp.float32)
     early = call(
         functools.partial(pack_early, blocks, planes, rows),
-        [(tall + planes * half, depth)] * (blocks - 1),
+        [(planes * (tall + half), depth)] * (blocks - 1),
         in_specs=[HBM] * 2,
         scratch=[
-            pltpu.VMEM((1, ny, depth), jnp.float32),
+            held,
             held,
             pltpu.VMEM((tall, depth), jnp.float32),
-            pltpu.SemaphoreType.DMA((planes + 1,)),
+            pltpu.SemaphoreType.DMA((2, planes)),
         ],
     )(stay(kappa), stay(wave_now[0]))
     early, before = lax.optimization_barrier((early, wave_before[0]))
     *late, own = call(
         functools.partial(pack_late, blocks, planes, rows),
-        [((2 * planes - 1) * tall, depth)] * (blocks - 1) + [(3 * planes * tall, depth)],
+        [(planes * tall, depth)] * (blocks - 1) + [(3 * planes * tall, depth)],
         in_specs=[HBM] * 3,
         scratch=[held, held, held, pltpu.SemaphoreType.DMA((3, planes))],
     )(stay(kappa), stay(wave_now[0]), stay(before))
     early = over_dom([None, *early])[1:]
     late = over_dom([None, *late])[1:]
 
-    wide = (1 + 3 * NT) * depth
     count, heard, pulse = call(
         functools.partial(spread, depth, ny, rows, listed),
         [(nx * tall, depth), (NT, nx * tall, depth), (NT, depth)],
@@ -406,7 +421,7 @@
         scratch=[pltpu.VMEM((listed + BLOCK, depth), jnp.float32)]
         + [pltpu.VMEM(array.shape, array.dtype) for array in (wavelet, receiver_cells, observed)]
         + [pltpu.SemaphoreType.DMA((3,))],
-        flops=1000 * 1000 * 1000,
+        flops=1,
         moved=1,
     )(source_cell, stay(wavelet), stay(receiver_cells), stay(observed))
 
@@ -418,21 +433,27 @@
 
     padded, plain = (nx, tall + 16, depth), (nx, tall, depth)
     cells = nx * tall * depth
+    start, bent = call(
+        functools.partial(begin, blocks, planes, rows),
+        [padded, plain],
+        in_specs=[VMEM] * blocks,
+        flops=1000*1000*1000,
+        moved=1,
+    )(own, *early)
     wave, lap, model, *turned = call(
         functools.partial(forward, blocks, planes, rows, ny),
-        [(NT, *padded), (NT, *plain), padded] + [(planes * rows, depth)] * blocks,
-        in_specs=[SMEM] + [VMEM] * (2 * blocks + planes),
-        scratch=[pltpu.VMEM((2, *padded), jnp.float32)],
+        [(NT, *padded), (NT - 1, *plain), padded] + [(planes * rows, depth)] * blocks,
+        in_specs=[SMEM] + [VMEM] * (2 * blocks + planes + 2),
         flops=16 * NT * cells,
         moved=16 * NT * cells,
-    )(source_cell, pulse, *early, *late, own, *swapped)
+    )(source_cell, pulse, *early, *late, own, *swapped, start, bent)
     half = rows // 2
     side = half + 2 * EDGE
     give, keep = (
         call(
             functools.partial(backward, mine, rows),
             [(nx * half, depth)],
-            in_specs=[VMEM] * 5,
+            in_specs=[VMEM] * 6,
             scratch=[
                 pltpu.VMEM((2, nx, side, depth), jnp.float32),
                 pltpu.VMEM((2, nx, side + 16, depth), jnp.float32),
@@ -440,7 +461,7 @@
             ],
             flops=12 * NT * cells,
             moved=12 * NT * cells,
-        )(count, heard, wave, lap, model)[0]
+        )(count, heard, wave, lap, bent, model)[0]
         for mine in (False, True)
     )
 

time: 44.7 us -> 44.3 us (level)
  waiting for transfers between devices: 8.38 us -> 6.64 us
  starting transfers between devices: 21.4 us -> 23 us
    ppermute x18, waiting for transfers between devices: 8.38 us -> 6.64 us  [across(): return lax.ppermute(array, ('shot', 'dom'), pairs)]
    ppermute x18, starting transfers between devices: 21.4 us -> 23 us  [across(): return lax.ppermute(array, ('shot', 'dom'), pairs)]
    pallas_call x2 -> x3, Pallas kernels: 2.57 us -> 3.08 us  [the longest x1 1.4 us: shards(): call(functools.partial(pack_late, blocks, planes, rows), [(planes * tall,...]
  transfers between devices with their start and end apart: 18 -> 18, of which waited for: 6 -> 6; matrix products, arithmetic and copies ran while one was open for 0% -> 0% of each run, Pallas kernels for 19% -> 20%
where the time goes in v5:
time: 44.3 us; the launch traced here: 44 us
  starting transfers between devices  23 us (52%)
  Pallas kernels  13 us (29%)
  waiting for transfers between devices  6.64 us (15%)
  between operations  1.4 us (3%)
    ppermute x18, starting transfers between devices, across(): return lax.ppermute(array, ('shot', 'dom'), pairs)  23 us
    ppermute x18, waiting for transfers between devices, across(): return lax.ppermute(array, ('shot', 'dom'), pairs)  6.64 us
    pallas_call x1, Pallas kernels, shards(): call(functools.partial(spread, depth, ny, rows, listed), [(nx * tall, dep...  4.95 us
    pallas_call x2, Pallas kernels, shards(): call(functools.partial(backward, mine, rows), [(nx * half, depth)], in_sp...  2.01 us
    pallas_call x1, Pallas kernels, shards(): call(functools.partial(pack_late, blocks, planes, rows), [(planes * tall,...  1.4 us
    pallas_call x1, Pallas kernels, shards(): call(functools.partial(forward, blocks, planes, rows, ny), [(NT, *padded)...  1.38 us
    pallas_call x1, Pallas kernels, shards(): call(functools.partial(pack_early, blocks, planes, rows), [(planes * (tal...  1.26 us
  transfers between devices with their start and end apart: 18, of which 6 were waited for; matrix products, arithmetic and copies ran while one was open for 0% of the time, Pallas kernels for 20%

profile of v5, /device:TPU:0, one launch (start us, length us, event | category | flops | bytes accessed | tf_op | source)
XLA Modules:
  0.0 44.0 jit_solution(11838741998425421409)
XLA Ops:
  0.6 1.3 %shard_map.87 = (f32[432,128]{1,0:T(8,128)S(1)}, f32[432,128]{1,0:T(8,128)S(1)}, f32[432,128]{1,0:T(8,128)S(1)}) custom-call(f32[2,512,128]{2,1,0:T(8,128)} %kappa.3, f32[2,512,128]{2,1,0:T(8,128)} %bitcast.3), custom_call_target="tpu_custom_call" | custom-call | tf_op jit(solution)/shard_map/pallas_call | solution.py:396
  1.9 3.0 %collective-permute-start = (f32[432,128]{1,0:T(8,128)S(1)}, f32[432,128]{1,0:T(8,128)S(1)}, u32[]{:S(2)}, u32[]{:S(2)}) collective-permute-start(f32[432,128]{1,0:T(8,128)S(1)} %get-tuple-element.44), channel_id=1, source_target_pairs={{0,1},{1,0},{2,3},{3,2},{4,5},{5,4},{6,7},{7,6},{8,9},{9,8},{10,11... | collective-permute-start | bytes 663560 | tf_op jit(solution)/shard_map/ppermute | solution.py:386
  4.9 1.5 %collective-permute-start.1 = (f32[432,128]{1,0:T(8,128)S(1)}, f32[432,128]{1,0:T(8,128)S(1)}, u32[]{:S(2)}, u32[]{:S(2)}) collective-permute-start(f32[432,128]{1,0:T(8,128)S(1)} %get-tuple-element.45), channel_id=1, source_target_pairs={{0,2},{1,3},{2,0},{3,1},{4,6},{5,7},{6,4},{7,5},{8,10},{9,11},{10,... | collective-permute-start | bytes 663560 | tf_op jit(solution)/shard_map/ppermute | solution.py:386
  6.4 0.0 collective-permute-start.2
  6.4 1.4 %shard_map.88 = (f32[288,128]{1,0:T(8,128)S(1)}, f32[288,128]{1,0:T(8,128)S(1)}, f32[288,128]{1,0:T(8,128)S(1)}, f32[864,128]{1,0:T(8,128)S(1)}) custom-call(f32[2,512,128]{2,1,0:T(8,128)} %kappa.3, f32[2,512,128]{2,1,0:T(8,128)} %bitcast.4, f32[2,512,128]{2,1,0:T(8,128)} %bitcast.5), custom_call_target="tpu_custom_call" | custom-call | tf_op jit(solution)/shard_map/pallas_call | solution.py:408
  7.9 2.0 %collective-permute-start.3 = (f32[288,128]{1,0:T(8,128)S(1)}, f32[288,128]{1,0:T(8,128)S(1)}, u32[]{:S(2)}, u32[]{:S(2)}) collective-permute-start(f32[288,128]{1,0:T(8,128)S(1)} %get-tuple-element.50), channel_id=1, source_target_pairs={{0,1},{1,0},{2,3},{3,2},{4,5},{5,4},{6,7},{7,6},{8,9},{9,8},{10,11... | collective-permute-start | bytes 442376 | tf_op jit(solution)/shard_map/ppermute | solution.py:386
  9.9 1.5 %collective-permute-start.4 = (f32[288,128]{1,0:T(8,128)S(1)}, f32[288,128]{1,0:T(8,128)S(1)}, u32[]{:S(2)}, u32[]{:S(2)}) collective-permute-start(f32[288,128]{1,0:T(8,128)S(1)} %get-tuple-element.51), channel_id=1, source_target_pairs={{0,2},{1,3},{2,0},{3,1},{4,6},{5,7},{6,4},{7,5},{8,10},{9,11},{10,... | collective-permute-start | bytes 442376 | tf_op jit(solution)/shard_map/ppermute | solution.py:386
  11.4 0.0 collective-permute-done.refs_0_
  11.4 2.8 %collective-permute-start.5 = (f32[288,128]{1,0:T(8,128)S(1)}, f32[288,128]{1,0:T(8,128)S(1)}, u32[]{:S(2)}, u32[]{:S(2)}) collective-permute-start(f32[288,128]{1,0:T(8,128)S(1)} %get-tuple-element.52), channel_id=1, source_target_pairs={{0,3},{1,2},{2,1},{3,0},{4,7},{5,6},{6,5},{7,4},{8,11},{9,10},{10,... | collective-permute-start | bytes 442376 | tf_op jit(solution)/shard_map/ppermute | solution.py:386
  14.8 5.0 %shard_map.86 = (f32[1152,128]{1,0:T(8,128)S(1)}, f32[4,1152,128]{2,1,0:T(8,128)S(1)}, f32[4,128]{1,0:T(4,128)S(1)}) custom-call(s32[1]{0:T(128)S(6)} %copy.9.source, f32[1,4]{1,0:T(1,128)} %lists_at.1, s32[1,2048]{1,0:T(1,128)} %cells_at.1, f32[1,4,2048]{2,1,0:T(4,128)} %observed_at.1), custom_call_target="tpu_custom_call" | custom-call | flops 1 | bytes 1 | tf_op jit(solution)/shard_map/pallas_call | solution.py:417
  19.8 0.0 collective-permute-done.1.refs_1_
  19.8 0.0 collective-permute-done.2.refs_2_
  19.8 0.1 collective-permute-start.6
  19.9 0.5 %collective-permute-start.7 = (f32[216,128]{1,0:T(8,128)S(1)}, f32[216,128]{1,0:T(8,128)S(1)}, u32[]{:S(2)}, u32[]{:S(2)}) collective-permute-start(f32[216,128]{1,0:T(8,128)S(1)} %get-tuple-element.58), channel_id=1, source_target_pairs={{0,4},{1,5},{2,6},{3,7},{4,0},{5,1},{6,2},{7,3},{8,12},{9,13},{10,... | collective-permute-start | bytes 331784 | tf_op jit(solution)/shard_map/ppermute | solution.py:386
  20.4 0.4 shard_map.90
  20.8 0.0 collective-permute-done.3.refs_3_
  20.8 2.0 %collective-permute-done.4.refs_4_ = f32[288,128]{1,0:T(8,128)S(1)} collective-permute-done((f32[288,128]{1,0:T(8,128)S(1)}, f32[288,128]{1,0:T(8,128)S(1)}, u32[]{:S(2)}, u32[]{:S(2)}) %collective-permute-start.4) | collective-permute-done | bytes 147488 | tf_op jit(solution)/shard_map/ppermute | solution.py:386
  22.9 0.0 collective-permute-done.5.refs_5_
  22.9 0.0 collective-permute-done.6.refs_7_
  22.9 0.0 collective-permute-done.7.refs_8_
  22.9 1.4 %shard_map.91 = (f32[4,8,160,128]{3,2,1,0:T(8,128)S(1)}, f32[3,8,144,128]{3,2,1,0:T(8,128)S(1)}, f32[8,160,128]{2,1,0:T(8,128)S(1)}, f32[256,128]{1,0:T(8,128)S(...) custom-call(s32[1]{0:T(128)S(6)} %copy.9.source, ...), custom_call_target="tpu_custom_call" | custom-call | flops 9437184 | bytes 9437184 | tf_op jit(solution)/shard_map/pallas_call | solution.py:443
  24.3 1.0 %shard_map.93 = f32[512,128]{1,0:T(8,128)S(1)} custom-call(f32[1152,128]{1,0:T(8,128)S(1)} %get-tuple-element.39.count, f32[4,1152,128]{2,1,0:T(8,128)S(1)} %get-tuple-element.40.heard, f32[4,8,160,128]{3,2,1,0:T(8,128)S(1)} %get-tuple-element.61.wave, f32[3,8,144,128]{3,2,1,0:T(8,128)S(1)} %get-tuple-element.62.lap, ...), custom_call_target="tpu_custom_call" | custom-call | flops 7077888 | bytes 7077888 | tf_op jit(solution)/shard_map/pallas_call | solution.py:453
  25.3 0.1 collective-permute-start.8
  25.4 1.0 %shard_map.92.keep = f32[512,128]{1,0:T(8,128)S(1)} custom-call(f32[1152,128]{1,0:T(8,128)S(1)} %get-tuple-element.39.count, f32[4,1152,128]{2,1,0:T(8,128)S(1)} %get-tuple-element.40.heard, f32[4,8,160,128]{3,2,1,0:T(8,128)S(1)} %get-tuple-element.61.wave, f32[3,8,144,128]{3,2,1,0:T(8,128)S(1)} %get-tuple-element.62.lap, ...), custom_call_target="tpu_custom_call" | custom-call | flops 7077888 | bytes 7077888 | tf_op jit(solution)/shard_map/pallas_call | solution.py:453
  26.4 0.5 %collective-permute-done.8.got = f32[512,128]{1,0:T(8,128)S(1)} collective-permute-done((f32[512,128]{1,0:T(8,128)S(1)}, f32[512,128]{1,0:T(8,128)S(1)}, u32[]{:S(2)}, u32[]{:S(2)}) %collective-permute-start.8) | collective-permute-done | bytes 262176 | tf_op jit(solution)/shard_map/ppermute | solution.py:386
  26.9 1.6 %collective-permute-start.9 = (f32[128,128]{1,0:T(8,128)S(1)}, f32[128,128]{1,0:T(8,128)S(1)}, u32[]{:S(2)}, u32[]{:S(2)}) collective-permute-start(f32[128,128]{1,0:T(8,128)S(1)} %get-tuple-element.64), channel_id=1, source_target_pairs={{0,3},{1,2},{2,1},{3,0},{4,7},{5,6},{6,5},{7,4},{8,11},{9,10},{10,... | collective-permute-start | bytes 196616 | tf_op jit(solution)/shard_map/ppermute | solution.py:386
  28.5 1.2 %collective-permute-start.10 = (f32[128,128]{1,0:T(8,128)S(1)}, f32[128,128]{1,0:T(8,128)S(1)}, u32[]{:S(2)}, u32[]{:S(2)}) collective-permute-start(f32[128,128]{1,0:T(8,128)S(1)} %get-tuple-element.65), channel_id=1, source_target_pairs={{0,2},{1,3},{2,0},{3,1},{4,6},{5,7},{6,4},{7,5},{8,10},{9,11},{10,... | collective-permute-start | bytes 196616 | tf_op jit(solution)/shard_map/ppermute | solution.py:386
  29.7 0.8 %collective-permute-start.11 = (f32[128,128]{1,0:T(8,128)S(1)}, f32[128,128]{1,0:T(8,128)S(1)}, u32[]{:S(2)}, u32[]{:S(2)}) collective-permute-start(f32[128,128]{1,0:T(8,128)S(1)} %get-tuple-element.66), channel_id=1, source_target_pairs={{0,1},{1,0},{2,3},{3,2},{4,5},{5,4},{6,7},{7,6},{8,9},{9,8},{10,11... | collective-permute-start | bytes 196616 | tf_op jit(solution)/shard_map/ppermute | solution.py:386
  30.5 1.3 %collective-permute-start.15 = (f32[256,128]{1,0:T(8,128)S(1)}, f32[256,128]{1,0:T(8,128)S(1)}, u32[]{:S(2)}, u32[]{:S(2)}) collective-permute-start(f32[256,128]{1,0:T(8,128)S(1)} %get-tuple-element.73), channel_id=1, source_target_pairs={{0,1},{1,0},{2,3},{3,2},{4,5},{5,4},{6,7},{7,6},{8,9},{9,8},{10,11... | collective-permute-start | bytes 393224 | tf_op jit(solution)/shard_map/ppermute | solution.py:386
  31.7 0.8 %collective-permute-start.16 = (f32[256,128]{1,0:T(8,128)S(1)}, f32[256,128]{1,0:T(8,128)S(1)}, u32[]{:S(2)}, u32[]{:S(2)}) collective-permute-start(f32[256,128]{1,0:T(8,128)S(1)} %get-tuple-element.74), channel_id=1, source_target_pairs={{0,2},{1,3},{2,0},{3,1},{4,6},{5,7},{6,4},{7,5},{8,10},{9,11},{10,... | collective-permute-start | bytes 393224 | tf_op jit(solution)/shard_map/ppermute | solution.py:386
  32.5 0.0 collective-permute-done.9.refs_0_
  32.5 1.4 %collective-permute-start.17 = (f32[256,128]{1,0:T(8,128)S(1)}, f32[256,128]{1,0:T(8,128)S(1)}, u32[]{:S(2)}, u32[]{:S(2)}) collective-permute-start(f32[256,128]{1,0:T(8,128)S(1)} %get-tuple-element.75), channel_id=1, source_target_pairs={{0,3},{1,2},{2,1},{3,0},{4,7},{5,6},{6,5},{7,4},{8,11},{9,10},{10,... | collective-permute-start | bytes 393224 | tf_op jit(solution)/shard_map/ppermute | solution.py:386
  34.0 0.0 collective-permute-done.10.refs_1_
  34.0 0.8 %collective-permute-done.11.refs_2_ = f32[128,128]{1,0:T(8,128)S(1)} collective-permute-done((f32[128,128]{1,0:T(8,128)S(1)}, f32[128,128]{1,0:T(8,128)S(1)}, u32[]{:S(2)}, u32[]{:S(2)}) %collective-permute-start.11) | collective-permute-done | bytes 65568 | tf_op jit(solution)/shard_map/ppermute | solution.py:386
  34.8 3.4 %collective-permute-start.12 = (f32[128,128]{1,0:T(8,128)S(1)}, f32[128,128]{1,0:T(8,128)S(1)}, u32[]{:S(2)}, u32[]{:S(2)}) collective-permute-start(f32[128,128]{1,0:T(8,128)S(1)} %get-tuple-element.68), channel_id=1, source_target_pairs={{0,24},{1,25},{2,26},{3,27},{4,28},{5,29},{6,30},{7,31},{8,16},{9,... | collective-permute-start | bytes 196616 | tf_op jit(solution)/shard_map/ppermute | solution.py:386
  38.2 0.0 collective-permute-start.13
  38.2 0.0 collective-permute-done.15.refs_1_
  38.2 1.0 %collective-permute-start.14 = (f32[128,128]{1,0:T(8,128)S(1)}, f32[128,128]{1,0:T(8,128)S(1)}, u32[]{:S(2)}, u32[]{:S(2)}) collective-permute-start(f32[128,128]{1,0:T(8,128)S(1)} %get-tuple-element.70), channel_id=1, source_target_pairs={{0,8},{1,9},{2,10},{3,11},{4,12},{5,13},{6,14},{7,15},{8,0},{9,1},... | collective-permute-start | bytes 196616 | tf_op jit(solution)/shard_map/ppermute | solution.py:386
  39.2 0.0 collective-permute-done.16.refs_2_
  39.2 0.4 collective-permute-done.17.refs_3_
  39.6 0.8 %shard_map.97 = f32[2,512,128]{2,1,0:T(8,128)} custom-call(f32[256,128]{1,0:T(8,128)S(1)} %get-tuple-element.72.refs_0_, f32[256,128]{1,0:T(8,128)S(1)} %collective-permute-done.15.refs_1_, f32[256,128]{1,0:T(8,128)S(1)} %collective-permute-done.16.refs_2_, f32[256,128]{1,0:T(8,128)S(1)} %collective-permute-done.17.refs_3_), custom_call_target="tpu_custom_call" | custom-call | tf_op jit(solution)/shard_map/pallas_call | solution.py:481
  40.5 0.4 %collective-permute-done.12.refs_0_ = f32[128,128]{1,0:T(8,128)S(1)} collective-permute-done((f32[128,128]{1,0:T(8,128)S(1)}, f32[128,128]{1,0:T(8,128)S(1)}, u32[]{:S(2)}, u32[]{:S(2)}) %collective-permute-start.12) | collective-permute-done | bytes 65568 | tf_op jit(solution)/shard_map/ppermute | solution.py:386
  40.9 2.5 %collective-permute-done.13.refs_1_ = f32[128,128]{1,0:T(8,128)S(1)} collective-permute-done((f32[128,128]{1,0:T(8,128)S(1)}, f32[128,128]{1,0:T(8,128)S(1)}, u32[]{:S(2)}, u32[]{:S(2)}) %collective-permute-start.13) | collective-permute-done | bytes 65568 | tf_op jit(solution)/shard_map/ppermute | solution.py:386
  43.4 0.0 collective-permute-done.14.refs_2_
  43.4 0.6 %shard_map.96 = f32[2,64,128]{2,1,0:T(8,128)} custom-call(f32[128,128]{1,0:T(8,128)S(1)} %collective-permute-done.12.refs_0_, f32[128,128]{1,0:T(8,128)S(1)} %collective-permute-done.13.refs_1_, f32[128,128]{1,0:T(8,128)S(1)} %collective-permute-done.14.refs_2_, f32[128,128]{1,0:T(8,128)S(1)} %get-tuple-element.71.refs_3_), custom_call_target="tpu_custom_call" | custom-call | tf_op jit(solution)/shard_map/pallas_call | solution.py:482
  (3 shorter events, 0.1 us)
Async XLA Ops:
  1.9 9.5 %collective-permute-start = (f32[432,128]{1,0:T(8,128)S(1)}, f32[432,128]{1,0:T(8,128)S(1)}, u32[]{:S(2)}, u32[]{:S(2)}) collective-permute-start(f32[432,128]{1,0:T(8,128)S(1)} %get-tuple-element.44), channel_id=1, source_target_pairs={{0,1},{1,0},{2,3},{3,2},{4,5},{5,4},{6,7},{7,6},{8,9},{9,8},{10,11... | collective-permute-start | bytes 663560 | tf_op jit(solution)/shard_map/ppermute | solution.py:386
  4.9 14.9 %collective-permute-start.1 = (f32[432,128]{1,0:T(8,128)S(1)}, f32[432,128]{1,0:T(8,128)S(1)}, u32[]{:S(2)}, u32[]{:S(2)}) collective-permute-start(f32[432,128]{1,0:T(8,128)S(1)} %get-tuple-element.45), channel_id=1, source_target_pairs={{0,2},{1,3},{2,0},{3,1},{4,6},{5,7},{6,4},{7,5},{8,10},{9,11},{10,... | collective-permute-start | bytes 663560 | tf_op jit(solution)/shard_map/ppermute | solution.py:386
  6.4 13.4 %collective-permute-start.2 = (f32[432,128]{1,0:T(8,128)S(1)}, f32[432,128]{1,0:T(8,128)S(1)}, u32[]{:S(2)}, u32[]{:S(2)}) collective-permute-start(f32[432,128]{1,0:T(8,128)S(1)} %get-tuple-element.46), channel_id=1, source_target_pairs={{0,3},{1,2},{2,1},{3,0},{4,7},{5,6},{6,5},{7,4},{8,11},{9,10},{10,... | collective-permute-start | bytes 663560 | tf_op jit(solution)/shard_map/ppermute | solution.py:386
  7.9 13.0 %collective-permute-start.3 = (f32[288,128]{1,0:T(8,128)S(1)}, f32[288,128]{1,0:T(8,128)S(1)}, u32[]{:S(2)}, u32[]{:S(2)}) collective-permute-start(f32[288,128]{1,0:T(8,128)S(1)} %get-tuple-element.50), channel_id=1, source_target_pairs={{0,1},{1,0},{2,3},{3,2},{4,5},{5,4},{6,7},{7,6},{8,9},{9,8},{10,11... | collective-permute-start | bytes 442376 | tf_op jit(solution)/shard_map/ppermute | solution.py:386
  9.9 13.0 %collective-permute-start.4 = (f32[288,128]{1,0:T(8,128)S(1)}, f32[288,128]{1,0:T(8,128)S(1)}, u32[]{:S(2)}, u32[]{:S(2)}) collective-permute-start(f32[288,128]{1,0:T(8,128)S(1)} %get-tuple-element.51), channel_id=1, source_target_pairs={{0,2},{1,3},{2,0},{3,1},{4,6},{5,7},{6,4},{7,5},{8,10},{9,11},{10,... | collective-permute-start | bytes 442376 | tf_op jit(solution)/shard_map/ppermute | solution.py:386
  11.4 11.5 %collective-permute-start.5 = (f32[288,128]{1,0:T(8,128)S(1)}, f32[288,128]{1,0:T(8,128)S(1)}, u32[]{:S(2)}, u32[]{:S(2)}) collective-permute-start(f32[288,128]{1,0:T(8,128)S(1)} %get-tuple-element.52), channel_id=1, source_target_pairs={{0,3},{1,2},{2,1},{3,0},{4,7},{5,6},{6,5},{7,4},{8,11},{9,10},{10,... | collective-permute-start | bytes 442376 | tf_op jit(solution)/shard_map/ppermute | solution.py:386
  19.8 3.0 %collective-permute-start.6 = (f32[216,128]{1,0:T(8,128)S(1)}, f32[216,128]{1,0:T(8,128)S(1)}, u32[]{:S(2)}, u32[]{:S(2)}) collective-permute-start(f32[216,128]{1,0:T(8,128)S(1)} %get-tuple-element.57), channel_id=1, source_target_pairs={{0,4},{1,5},{2,6},{3,7},{4,0},{5,1},{6,2},{7,3},{8,12},{9,13},{10,... | collective-permute-start | bytes 331784 | tf_op jit(solution)/shard_map/ppermute | solution.py:386
  19.9 3.0 %collective-permute-start.7 = (f32[216,128]{1,0:T(8,128)S(1)}, f32[216,128]{1,0:T(8,128)S(1)}, u32[]{:S(2)}, u32[]{:S(2)}) collective-permute-start(f32[216,128]{1,0:T(8,128)S(1)} %get-tuple-element.58), channel_id=1, source_target_pairs={{0,4},{1,5},{2,6},{3,7},{4,0},{5,1},{6,2},{7,3},{8,12},{9,13},{10,... | collective-permute-start | bytes 331784 | tf_op jit(solution)/shard_map/ppermute | solution.py:386
  25.3 1.6 %collective-permute-start.8 = (f32[512,128]{1,0:T(8,128)S(1)}, f32[512,128]{1,0:T(8,128)S(1)}, u32[]{:S(2)}, u32[]{:S(2)}) collective-permute-start(f32[512,128]{1,0:T(8,128)S(1)} %shard_map.93), channel_id=1, source_target_pairs={{0,4},{1,5},{2,6},{3,7},{4,0},{5,1},{6,2},{7,3},{8,12},{9,13},{10,... | collective-permute-start | bytes 786440 | tf_op jit(solution)/shard_map/ppermute | solution.py:386
  26.9 5.6 %collective-permute-start.9 = (f32[128,128]{1,0:T(8,128)S(1)}, f32[128,128]{1,0:T(8,128)S(1)}, u32[]{:S(2)}, u32[]{:S(2)}) collective-permute-start(f32[128,128]{1,0:T(8,128)S(1)} %get-tuple-element.64), channel_id=1, source_target_pairs={{0,3},{1,2},{2,1},{3,0},{4,7},{5,6},{6,5},{7,4},{8,11},{9,10},{10,... | collective-permute-start | bytes 196616 | tf_op jit(solution)/shard_map/ppermute | solution.py:386
  28.5 5.5 %collective-permute-start.10 = (f32[128,128]{1,0:T(8,128)S(1)}, f32[128,128]{1,0:T(8,128)S(1)}, u32[]{:S(2)}, u32[]{:S(2)}) collective-permute-start(f32[128,128]{1,0:T(8,128)S(1)} %get-tuple-element.65), channel_id=1, source_target_pairs={{0,2},{1,3},{2,0},{3,1},{4,6},{5,7},{6,4},{7,5},{8,10},{9,11},{10,... | collective-permute-start | bytes 196616 | tf_op jit(solution)/shard_map/ppermute | solution.py:386
  29.7 5.0 %collective-permute-start.11 = (f32[128,128]{1,0:T(8,128)S(1)}, f32[128,128]{1,0:T(8,128)S(1)}, u32[]{:S(2)}, u32[]{:S(2)}) collective-permute-start(f32[128,128]{1,0:T(8,128)S(1)} %get-tuple-element.66), channel_id=1, source_target_pairs={{0,1},{1,0},{2,3},{3,2},{4,5},{5,4},{6,7},{7,6},{8,9},{9,8},{10,11... | collective-permute-start | bytes 196616 | tf_op jit(solution)/shard_map/ppermute | solution.py:386
  30.5 7.8 %collective-permute-start.15 = (f32[256,128]{1,0:T(8,128)S(1)}, f32[256,128]{1,0:T(8,128)S(1)}, u32[]{:S(2)}, u32[]{:S(2)}) collective-permute-start(f32[256,128]{1,0:T(8,128)S(1)} %get-tuple-element.73), channel_id=1, source_target_pairs={{0,1},{1,0},{2,3},{3,2},{4,5},{5,4},{6,7},{7,6},{8,9},{9,8},{10,11... | collective-permute-start | bytes 393224 | tf_op jit(solution)/shard_map/ppermute | solution.py:386
  31.7 7.5 %collective-permute-start.16 = (f32[256,128]{1,0:T(8,128)S(1)}, f32[256,128]{1,0:T(8,128)S(1)}, u32[]{:S(2)}, u32[]{:S(2)}) collective-permute-start(f32[256,128]{1,0:T(8,128)S(1)} %get-tuple-element.74), channel_id=1, source_target_pairs={{0,2},{1,3},{2,0},{3,1},{4,6},{5,7},{6,4},{7,5},{8,10},{9,11},{10,... | collective-permute-start | bytes 393224 | tf_op jit(solution)/shard_map/ppermute | solution.py:386
  32.5 7.1 %collective-permute-start.17 = (f32[256,128]{1,0:T(8,128)S(1)}, f32[256,128]{1,0:T(8,128)S(1)}, u32[]{:S(2)}, u32[]{:S(2)}) collective-permute-start(f32[256,128]{1,0:T(8,128)S(1)} %get-tuple-element.75), channel_id=1, source_target_pairs={{0,3},{1,2},{2,1},{3,0},{4,7},{5,6},{6,5},{7,4},{8,11},{9,10},{10,... | collective-permute-start | bytes 393224 | tf_op jit(solution)/shard_map/ppermute | solution.py:386
  34.8 6.1 %collective-permute-start.12 = (f32[128,128]{1,0:T(8,128)S(1)}, f32[128,128]{1,0:T(8,128)S(1)}, u32[]{:S(2)}, u32[]{:S(2)}) collective-permute-start(f32[128,128]{1,0:T(8,128)S(1)} %get-tuple-element.68), channel_id=1, source_target_pairs={{0,24},{1,25},{2,26},{3,27},{4,28},{5,29},{6,30},{7,31},{8,16},{9,... | collective-permute-start | bytes 196616 | tf_op jit(solution)/shard_map/ppermute | solution.py:386
  38.2 5.2 %collective-permute-start.13 = (f32[128,128]{1,0:T(8,128)S(1)}, f32[128,128]{1,0:T(8,128)S(1)}, u32[]{:S(2)}, u32[]{:S(2)}) collective-permute-start(f32[128,128]{1,0:T(8,128)S(1)} %get-tuple-element.69), channel_id=1, source_target_pairs={{0,16},{1,17},{2,18},{3,19},{4,20},{5,21},{6,22},{7,23},{8,24},{9,... | collective-permute-start | bytes 196616 | tf_op jit(solution)/shard_map/ppermute | solution.py:386
  38.2 5.2 %collective-permute-start.14 = (f32[128,128]{1,0:T(8,128)S(1)}, f32[128,128]{1,0:T(8,128)S(1)}, u32[]{:S(2)}, u32[]{:S(2)}) collective-permute-start(f32[128,128]{1,0:T(8,128)S(1)} %get-tuple-element.70), channel_id=1, source_target_pairs={{0,8},{1,9},{2,10},{3,11},{4,12},{5,13},{6,14},{7,15},{8,0},{9,1},... | collective-permute-start | bytes 196616 | tf_op jit(solution)/shard_map/ppermute | solution.py:386

commit v6 on v5

--- a/solution.py
+++ b/solution.py
@@ -59,21 +59,34 @@
 
 
 def pack_early(blocks, planes, rows, kappa, now, *refs):
-    outs, (held, model, whole, semaphores) = refs[: blocks - 1], refs[blocks - 1 :]
+    outs, (held, inner, outer, semaphores) = refs[: blocks - 1], refs[blocks - 1 :]
     dom, core = lax.axis_index("dom"), lax.rem(lax.axis_index("shot"), 2)
-    waves, kappas = fetch(now, held, semaphores.at[0]), fetch(kappa, model, semaphores.at[1])
-    tall = rows + 2 * EDGE
-    half = tall // 2
+    tall, side = rows + 2 * EDGE, rows // 2
+    half = side + EDGE
+    inside = pl.ds(pl.multiple_of(core * side, 8), side)
+    beside = pl.ds(pl.multiple_of((1 - core) * (rows - EDGE), 8), EDGE)
+    copies = fetch(now, held, semaphores)
+    copies.append(pltpu.make_async_copy(kappa.at[:, :, inside], inner, semaphores.at[planes]))
+    copies.append(pltpu.make_async_copy(kappa.at[:, :, beside], outer, semaphores.at[planes + 1]))
+    for copy in copies[planes:]:
+        copy.start()
     for p in range(planes):
-        waves[p].wait()
+        copies[p].wait()
         for s in range(1, blocks):
             put(held, p, lax.bitwise_xor(dom, s), blocks, rows, outs[s - 1], p * tall)
-    for p in range(planes):
-        kappas[p].wait()
-        for s in range(1, blocks):
-            put(model, p, lax.bitwise_xor(dom, s), blocks, rows, whole, 0)
+    for copy in copies[planes:]:
+        copy.wait()
+    for s in range(1, blocks):
+        block = lax.bitwise_xor(dom, s)
+        next_to = block - 1 + 2 * core
+        there = (next_to >= 0) & (next_to < blocks)
+        next_to = jnp.clip(next_to, 0, blocks - 1)
+        for p in range(planes):
             at = planes * tall + p * half
-            outs[s - 1][at : at + half, :] = whole[pl.ds(pl.multiple_of(core * half, 8), half), :]
+            inner_at = pl.ds(pl.multiple_of(at + EDGE * (1 - core), 8), side)
+            outer_at = pl.ds(pl.multiple_of(at + side * core, 8), EDGE)
+            outs[s - 1][inner_at, :] = inner[p, block]
+            outs[s - 1][outer_at, :] = jnp.where(there, outer[p, next_to], 0.0)
 
 
 def pack_late(blocks, planes, rows, kappa, now, before, *refs):
@@ -197,26 +210,8 @@
 
 
 def begin(blocks, planes, rows, own, *refs):
-    early, wave, lap = refs[: blocks - 1], refs[blocks - 1], refs[blocks]
+    early, swapped, (wave, lap, model, step) = refs[: blocks - 1], refs[blocks - 1 : -4], refs[-4:]
     nx, tall, depth = lap.shape
-    dom = lax.axis_index("dom")
-    for s in range(blocks):
-        first = planes * lax.bitwise_xor(dom, s)
-        for p in range(planes):
-            part = early[s - 1][p * tall : (p + 1) * tall, :] if s > 0 else own[(planes + p) * tall : (planes + p + 1) * tall, :]
-            wave[first + p, 8 : 8 + tall, :] = part
-    some = 48
-    low, high = edges(some, depth)
-    for a in range(0, tall, some):
-        for x, held in sweep(wave, (), 8 + a, some, nx):
-            lap[x, a : a + some, :] = bend(wave, (), 8 + a, some, nx, x, held, low, high) - 6.0 * held[1]
-
-
-def forward(blocks, planes, rows, ny, source, pulse, *refs):
-    early, late, own, refs = refs[: blocks - 1], refs[blocks - 1 : 2 * blocks - 2], refs[2 * blocks - 2], refs[2 * blocks - 1 :]
-    swapped, start, bent, refs = refs[:planes], refs[planes], refs[planes + 1], refs[planes + 2 :]
-    wave, lap, model, turned = *refs[:3], refs[3:]
-    nx, tall, depth = lap.shape[1:]
     dom, core = lax.axis_index("dom"), lax.rem(lax.axis_index("shot"), 2)
     half = tall // 2
     near = pl.ds(pl.multiple_of(8 + core * half, 8), half)
@@ -225,13 +220,30 @@
         first = planes * lax.bitwise_xor(dom, s)
         for p in range(planes):
             if s == 0:
-                at = (2 * planes + p) * tall
+                at = (planes + p) * tall
+                wave[first + p, 8 : 8 + tall, :] = own[at : at + tall, :]
+                at += planes * tall
                 model[first + p, 8 : 8 + tall, :] = own[at : at + tall, :]
             else:
+                wave[first + p, 8 : 8 + tall, :] = early[s - 1][p * tall : (p + 1) * tall, :]
                 at = planes * tall + p * half
                 model[first + p, near, :] = early[s - 1][at : at + half, :]
                 model[first + p, other, :] = swapped[p][(s - 1) * half : s * half, :]
-
+    some = 48
+    low, high = edges(some, depth)
+    for a in range(0, tall, some):
+        rows_at = slice(8 + a, 8 + a + some)
+        for x, held in sweep(wave, (), 8 + a, some, nx):
+            turn = bend(wave, (), 8 + a, some, nx, x, held, low, high) - 6.0 * held[1]
+            lap[x, a : a + some, :] = turn
+            step[x, a : a + some, :] = (held[1] + held[1]) + model[x, rows_at, :] * turn
+
+
+def forward(blocks, planes, rows, ny, source, pulse, *refs):
+    late, own, start, model, step, refs = refs[: blocks - 1], *refs[blocks - 1 : blocks + 3], refs[blocks + 3 :]
+    wave, lap, turned = *refs[:2], refs[2:]
+    nx, tall, depth = lap.shape[1:]
+    dom = lax.axis_index("dom")
     some = 48
     low, high = edges(some, depth)
     line = source[0] // depth
@@ -246,14 +258,10 @@
             wave[n, sx, pl.ds(sy, 1), :] = wave[n, sx, pl.ds(sy, 1), :] + pulse[n : n + 1, :]
 
     for s in range(blocks):
+        before = late[s - 1] if s > 0 else own
         for p in range(planes):
             x = planes * lax.bitwise_xor(dom, s) + p
-            for a in range(0, tall, some):
-                rows_at = slice(8 + a, 8 + a + some)
-                mid = start[x, rows_at, :]
-                old = late[s - 1] if s > 0 else own
-                new = (mid + mid) - old[p * tall + a : p * tall + a + some, :]
-                wave[0, x, rows_at, :] = new + model[x, rows_at, :] * bent[x, a : a + some, :]
+            wave[0, x, 8 : 8 + tall, :] = step[x] - before[p * tall : (p + 1) * tall, :]
     inject(0)
 
     for n in range(1, NT):
@@ -399,11 +407,11 @@
         in_specs=[HBM] * 2,
         scratch=[
             held,
-            held,
-            pltpu.VMEM((tall, depth), jnp.float32),
-            pltpu.SemaphoreType.DMA((2, planes)),
+            pltpu.VMEM((planes, blocks, rows // 2, depth), jnp.float32),
+            pltpu.VMEM((planes, blocks, EDGE, depth), jnp.float32),
+            pltpu.SemaphoreType.DMA((planes + 2,)),
         ],
-    )(stay(kappa), stay(wave_now[0]))
+    )(stay(kappa.reshape(planes, blocks, rows, depth)), stay(wave_now[0]))
     early, before = lax.optimization_barrier((early, wave_before[0]))
     *late, own = call(
         functools.partial(pack_late, blocks, planes, rows),
@@ -421,7 +429,7 @@
         scratch=[pltpu.VMEM((listed + BLOCK, depth), jnp.float32)]
         + [pltpu.VMEM(array.shape, array.dtype) for array in (wavelet, receiver_cells, observed)]
         + [pltpu.SemaphoreType.DMA((3,))],
-        flops=1,
+        flops=600 * 1000 * 1000,
         moved=1,
     )(source_cell, stay(wavelet), stay(receiver_cells), stay(observed))
 
@@ -433,20 +441,20 @@
 
     padded, plain = (nx, tall + 16, depth), (nx, tall, depth)
     cells = nx * tall * depth
-    start, bent = call(
+    start, bent, model, step = call(
         functools.partial(begin, blocks, planes, rows),
-        [padded, plain],
-        in_specs=[VMEM] * blocks,
-        flops=1000*1000*1000,
+        [padded, plain, padded, plain],
+        in_specs=[VMEM] * (blocks + planes),
+        flops=1,
         moved=1,
-    )(own, *early)
-    wave, lap, model, *turned = call(
+    )(own, *early, *swapped)
+    wave, lap, *turned = call(
         functools.partial(forward, blocks, planes, rows, ny),
-        [(NT, *padded), (NT - 1, *plain), padded] + [(planes * rows, depth)] * blocks,
-        in_specs=[SMEM] + [VMEM] * (2 * blocks + planes + 2),
+        [(NT, *padded), (NT - 1, *plain)] + [(planes * rows, depth)] * blocks,
+        in_specs=[SMEM] + [VMEM] * (blocks + 4),
         flops=16 * NT * cells,
         moved=16 * NT * cells,
-    )(source_cell, pulse, *early, *late, own, *swapped, start, bent)
+    )(source_cell, pulse, *late, own, start, model, step)
     half = rows // 2
     side = half + 2 * EDGE
     give, keep = (

time: 44.3 us -> 44.1 us (level)
  starting transfers between devices: 23 us -> 22.3 us
  waiting for transfers between devices: 6.64 us -> 7.23 us
    ppermute x18, starting transfers between devices: 23 us -> 22.3 us  [across(): return lax.ppermute(array, ('shot', 'dom'), pairs)]
    ppermute x18, waiting for transfers between devices: 6.64 us -> 7.23 us  [across(): return lax.ppermute(array, ('shot', 'dom'), pairs)]
  transfers between devices with their start and end apart: 18 -> 18, of which waited for: 6 -> 8; matrix products, arithmetic and copies ran while one was open for 0% -> 0% of each run, Pallas kernels for 20% -> 20%
where the time goes in v6:
time: 44.1 us; the launch traced here: 43.9 us
  starting transfers between devices  22.3 us (51%)
  Pallas kernels  12.9 us (29%)
  waiting for transfers between devices  7.23 us (16%)
  between operations  1.41 us (3%)
    ppermute x18, starting transfers between devices, across(): return lax.ppermute(array, ('shot', 'dom'), pairs)  22.3 us
    ppermute x18, waiting for transfers between devices, across(): return lax.ppermute(array, ('shot', 'dom'), pairs)  7.23 us
    pallas_call x1, Pallas kernels, shards(): call(functools.partial(spread, depth, ny, rows, listed), [(nx * tall, dep...  4.95 us
    pallas_call x2, Pallas kernels, shards(): call(functools.partial(backward, mine, rows), [(nx * half, depth)], in_sp...  2.13 us
    pallas_call x1, Pallas kernels, shards(): call(functools.partial(pack_late, blocks, planes, rows), [(planes * tall,...  1.4 us
    pallas_call x1, Pallas kernels, shards(): call(functools.partial(forward, blocks, planes, rows, ny), [(NT, *padded)...  1.3 us
    pallas_call x1, Pallas kernels, shards(): call(functools.partial(pack_early, blocks, planes, rows), [(planes * (tal...  1.17 us
  transfers between devices with their start and end apart: 18, of which 8 were waited for; matrix products, arithmetic and copies ran while one was open for 0% of the time, Pallas kernels for 20%

profile of v6, /device:TPU:0, one launch (start us, length us, event | category | flops | bytes accessed | tf_op | source)
XLA Modules:
  0.0 43.9 jit_solution(3991520493787635829)
XLA Ops:
  0.6 1.2 %shard_map.87 = (f32[432,128]{1,0:T(8,128)S(1)}, f32[432,128]{1,0:T(8,128)S(1)}, f32[432,128]{1,0:T(8,128)S(1)}) custom-call(f32[2,4,128,128]{3,2,1,0:T(8,128)} %bitcast.4, f32[2,512,128]{2,1,0:T(8,128)} %bitcast.5), custom_call_target="tpu_custom_call" | custom-call | tf_op jit(solution)/shard_map/pallas_call | solution.py:404
  1.8 3.0 %collective-permute-start = (f32[432,128]{1,0:T(8,128)S(1)}, f32[432,128]{1,0:T(8,128)S(1)}, u32[]{:S(2)}, u32[]{:S(2)}) collective-permute-start(f32[432,128]{1,0:T(8,128)S(1)} %get-tuple-element.45), channel_id=1, source_target_pairs={{0,1},{1,0},{2,3},{3,2},{4,5},{5,4},{6,7},{7,6},{8,9},{9,8},{10,11... | collective-permute-start | bytes 663560 | tf_op jit(solution)/shard_map/ppermute | solution.py:394
  4.8 1.5 %collective-permute-start.1 = (f32[432,128]{1,0:T(8,128)S(1)}, f32[432,128]{1,0:T(8,128)S(1)}, u32[]{:S(2)}, u32[]{:S(2)}) collective-permute-start(f32[432,128]{1,0:T(8,128)S(1)} %get-tuple-element.46), channel_id=1, source_target_pairs={{0,2},{1,3},{2,0},{3,1},{4,6},{5,7},{6,4},{7,5},{8,10},{9,11},{10,... | collective-permute-start | bytes 663560 | tf_op jit(solution)/shard_map/ppermute | solution.py:394
  6.3 0.0 collective-permute-start.2
  6.3 1.4 %shard_map.88 = (f32[288,128]{1,0:T(8,128)S(1)}, f32[288,128]{1,0:T(8,128)S(1)}, f32[288,128]{1,0:T(8,128)S(1)}, f32[864,128]{1,0:T(8,128)S(1)}) custom-call(f32[2,512,128]{2,1,0:T(8,128)} %kappa.1, f32[2,512,128]{2,1,0:T(8,128)} %bitcast.6, f32[2,512,128]{2,1,0:T(8,128)} %bitcast.7), custom_call_target="tpu_custom_call" | custom-call | tf_op jit(solution)/shard_map/pallas_call | solution.py:416
  7.8 2.0 %collective-permute-start.3 = (f32[288,128]{1,0:T(8,128)S(1)}, f32[288,128]{1,0:T(8,128)S(1)}, u32[]{:S(2)}, u32[]{:S(2)}) collective-permute-start(f32[288,128]{1,0:T(8,128)S(1)} %get-tuple-element.51), channel_id=1, source_target_pairs={{0,1},{1,0},{2,3},{3,2},{4,5},{5,4},{6,7},{7,6},{8,9},{9,8},{10,11... | collective-permute-start | bytes 442376 | tf_op jit(solution)/shard_map/ppermute | solution.py:394
  9.8 1.5 %collective-permute-start.4 = (f32[288,128]{1,0:T(8,128)S(1)}, f32[288,128]{1,0:T(8,128)S(1)}, u32[]{:S(2)}, u32[]{:S(2)}) collective-permute-start(f32[288,128]{1,0:T(8,128)S(1)} %get-tuple-element.52), channel_id=1, source_target_pairs={{0,2},{1,3},{2,0},{3,1},{4,6},{5,7},{6,4},{7,5},{8,10},{9,11},{10,... | collective-permute-start | bytes 442376 | tf_op jit(solution)/shard_map/ppermute | solution.py:394
  11.9 0.0 collective-permute-done.refs_0_
  12.0 2.1 %collective-permute-start.5 = (f32[288,128]{1,0:T(8,128)S(1)}, f32[288,128]{1,0:T(8,128)S(1)}, u32[]{:S(2)}, u32[]{:S(2)}) collective-permute-start(f32[288,128]{1,0:T(8,128)S(1)} %get-tuple-element.53), channel_id=1, source_target_pairs={{0,3},{1,2},{2,1},{3,0},{4,7},{5,6},{6,5},{7,4},{8,11},{9,10},{10,... | collective-permute-start | bytes 442376 | tf_op jit(solution)/shard_map/ppermute | solution.py:394
  14.1 4.9 %shard_map.86 = (f32[1152,128]{1,0:T(8,128)S(1)}, f32[4,1152,128]{2,1,0:T(8,128)S(1)}, f32[4,128]{1,0:T(4,128)S(1)}) custom-call(s32[1]{0:T(128)S(6)} %copy.9.source, f32[1,4]{1,0:T(1,128)} %lists_at.1, s32[1,2048]{1,0:T(1,128)} %cells_at.1, f32[1,4,2048]{2,1,0:T(4,128)} %observed_at.1), custom_call_target="tpu_custom_call" | custom-call | flops 600000000 | bytes 1 | tf_op jit(solution)/shard_map/pallas_call | solution.py:425
  19.0 0.0 collective-permute-done.1.refs_1_
  19.0 0.0 collective-permute-done.2.refs_2_
  19.1 0.1 collective-permute-start.6
  19.2 0.5 %collective-permute-start.7 = (f32[216,128]{1,0:T(8,128)S(1)}, f32[216,128]{1,0:T(8,128)S(1)}, u32[]{:S(2)}, u32[]{:S(2)}) collective-permute-start(f32[216,128]{1,0:T(8,128)S(1)} %get-tuple-element.59), channel_id=1, source_target_pairs={{0,4},{1,5},{2,6},{3,7},{4,0},{5,1},{6,2},{7,3},{8,12},{9,13},{10,... | collective-permute-start | bytes 331784 | tf_op jit(solution)/shard_map/ppermute | solution.py:394
  19.7 0.8 %collective-permute-done.6.refs_3_ = f32[216,128]{1,0:T(8,128)S(1)} collective-permute-done((f32[216,128]{1,0:T(8,128)S(1)}, f32[216,128]{1,0:T(8,128)S(1)}, u32[]{:S(2)}, u32[]{:S(2)}) %collective-permute-start.6) | collective-permute-done | bytes 110624 | tf_op jit(solution)/shard_map/ppermute | solution.py:394
  20.5 0.2 collective-permute-done.7.refs_4_
  20.6 0.4 shard_map.90
  21.1 0.0 collective-permute-done.3.refs_0_
  21.1 1.7 %collective-permute-done.4.refs_1_ = f32[288,128]{1,0:T(8,128)S(1)} collective-permute-done((f32[288,128]{1,0:T(8,128)S(1)}, f32[288,128]{1,0:T(8,128)S(1)}, u32[]{:S(2)}, u32[]{:S(2)}) %collective-permute-start.4) | collective-permute-done | bytes 147488 | tf_op jit(solution)/shard_map/ppermute | solution.py:394
  22.8 0.0 collective-permute-done.5.refs_2_
  22.8 1.3 %shard_map.91 = (f32[4,8,160,128]{3,2,1,0:T(8,128)S(1)}, f32[3,8,144,128]{3,2,1,0:T(8,128)S(1)}, f32[256,128]{1,0:T(8,128)S(1)}, f32[256,128]{1,0:T(8,128)S(1)},...) custom-call(s32[1]{0:T(128)S(6)} %copy.9.source, f32[4,128]{1,0:T(4,128)S(1)} %get-tuple-element.49.pulse, ...), custom_call_target="tpu_custom_call" | custom-call | flops 9437184 | bytes 9437184 | tf_op jit(solution)/shard_map/pallas_call | solution.py:451
  24.1 1.1 %shard_map.93 = f32[512,128]{1,0:T(8,128)S(1)} custom-call(f32[1152,128]{1,0:T(8,128)S(1)} %get-tuple-element.40.count, f32[4,1152,128]{2,1,0:T(8,128)S(1)} %get-tuple-element.41.heard, f32[4,8,160,128]{3,2,1,0:T(8,128)S(1)} %get-tuple-element.63.wave, f32[3,8,144,128]{3,2,1,0:T(8,128)S(1)} %get-tuple-element.64.lap, ...), custom_call_target="tpu_custom_call" | custom-call | flops 7077888 | bytes 7077888 | tf_op jit(solution)/shard_map/pallas_call | solution.py:461
  25.1 0.1 collective-permute-start.8
  25.2 1.1 %shard_map.92.keep = f32[512,128]{1,0:T(8,128)S(1)} custom-call(f32[1152,128]{1,0:T(8,128)S(1)} %get-tuple-element.40.count, f32[4,1152,128]{2,1,0:T(8,128)S(1)} %get-tuple-element.41.heard, f32[4,8,160,128]{3,2,1,0:T(8,128)S(1)} %get-tuple-element.63.wave, f32[3,8,144,128]{3,2,1,0:T(8,128)S(1)} %get-tuple-element.64.lap, ...), custom_call_target="tpu_custom_call" | custom-call | flops 7077888 | bytes 7077888 | tf_op jit(solution)/shard_map/pallas_call | solution.py:461
  26.3 0.5 %collective-permute-done.8.got = f32[512,128]{1,0:T(8,128)S(1)} collective-permute-done((f32[512,128]{1,0:T(8,128)S(1)}, f32[512,128]{1,0:T(8,128)S(1)}, u32[]{:S(2)}, u32[]{:S(2)}) %collective-permute-start.8) | collective-permute-done | bytes 262176 | tf_op jit(solution)/shard_map/ppermute | solution.py:394
  26.8 1.6 %collective-permute-start.9 = (f32[128,128]{1,0:T(8,128)S(1)}, f32[128,128]{1,0:T(8,128)S(1)}, u32[]{:S(2)}, u32[]{:S(2)}) collective-permute-start(f32[128,128]{1,0:T(8,128)S(1)} %get-tuple-element.66), channel_id=1, source_target_pairs={{0,3},{1,2},{2,1},{3,0},{4,7},{5,6},{6,5},{7,4},{8,11},{9,10},{10,... | collective-permute-start | bytes 196616 | tf_op jit(solution)/shard_map/ppermute | solution.py:394
  28.3 1.3 %collective-permute-start.10 = (f32[128,128]{1,0:T(8,128)S(1)}, f32[128,128]{1,0:T(8,128)S(1)}, u32[]{:S(2)}, u32[]{:S(2)}) collective-permute-start(f32[128,128]{1,0:T(8,128)S(1)} %get-tuple-element.67), channel_id=1, source_target_pairs={{0,2},{1,3},{2,0},{3,1},{4,6},{5,7},{6,4},{7,5},{8,10},{9,11},{10,... | collective-permute-start | bytes 196616 | tf_op jit(solution)/shard_map/ppermute | solution.py:394
  29.6 0.7 %collective-permute-start.11 = (f32[128,128]{1,0:T(8,128)S(1)}, f32[128,128]{1,0:T(8,128)S(1)}, u32[]{:S(2)}, u32[]{:S(2)}) collective-permute-start(f32[128,128]{1,0:T(8,128)S(1)} %get-tuple-element.68), channel_id=1, source_target_pairs={{0,1},{1,0},{2,3},{3,2},{4,5},{5,4},{6,7},{7,6},{8,9},{9,8},{10,11... | collective-permute-start | bytes 196616 | tf_op jit(solution)/shard_map/ppermute | solution.py:394
  30.3 1.3 %collective-permute-start.15 = (f32[256,128]{1,0:T(8,128)S(1)}, f32[256,128]{1,0:T(8,128)S(1)}, u32[]{:S(2)}, u32[]{:S(2)}) collective-permute-start(f32[256,128]{1,0:T(8,128)S(1)} %get-tuple-element.75), channel_id=1, source_target_pairs={{0,1},{1,0},{2,3},{3,2},{4,5},{5,4},{6,7},{7,6},{8,9},{9,8},{10,11... | collective-permute-start | bytes 393224 | tf_op jit(solution)/shard_map/ppermute | solution.py:394
  31.6 0.8 %collective-permute-start.16 = (f32[256,128]{1,0:T(8,128)S(1)}, f32[256,128]{1,0:T(8,128)S(1)}, u32[]{:S(2)}, u32[]{:S(2)}) collective-permute-start(f32[256,128]{1,0:T(8,128)S(1)} %get-tuple-element.76), channel_id=1, source_target_pairs={{0,2},{1,3},{2,0},{3,1},{4,6},{5,7},{6,4},{7,5},{8,10},{9,11},{10,... | collective-permute-start | bytes 393224 | tf_op jit(solution)/shard_map/ppermute | solution.py:394
  32.4 0.0 collective-permute-done.9.refs_0_
  32.4 1.4 %collective-permute-start.17 = (f32[256,128]{1,0:T(8,128)S(1)}, f32[256,128]{1,0:T(8,128)S(1)}, u32[]{:S(2)}, u32[]{:S(2)}) collective-permute-start(f32[256,128]{1,0:T(8,128)S(1)} %get-tuple-element.77), channel_id=1, source_target_pairs={{0,3},{1,2},{2,1},{3,0},{4,7},{5,6},{6,5},{7,4},{8,11},{9,10},{10,... | collective-permute-start | bytes 393224 | tf_op jit(solution)/shard_map/ppermute | solution.py:394
  33.8 0.0 collective-permute-done.10.refs_1_
  33.8 0.8 %collective-permute-done.11.refs_2_ = f32[128,128]{1,0:T(8,128)S(1)} collective-permute-done((f32[128,128]{1,0:T(8,128)S(1)}, f32[128,128]{1,0:T(8,128)S(1)}, u32[]{:S(2)}, u32[]{:S(2)}) %collective-permute-start.11) | collective-permute-done | bytes 65568 | tf_op jit(solution)/shard_map/ppermute | solution.py:394
  34.7 3.4 %collective-permute-start.12 = (f32[128,128]{1,0:T(8,128)S(1)}, f32[128,128]{1,0:T(8,128)S(1)}, u32[]{:S(2)}, u32[]{:S(2)}) collective-permute-start(f32[128,128]{1,0:T(8,128)S(1)} %get-tuple-element.70), channel_id=1, source_target_pairs={{0,24},{1,25},{2,26},{3,27},{4,28},{5,29},{6,30},{7,31},{8,16},{9,... | collective-permute-start | bytes 196616 | tf_op jit(solution)/shard_map/ppermute | solution.py:394
  38.1 0.0 collective-permute-start.13
  38.1 0.0 collective-permute-done.15.refs_1_
  38.1 1.0 %collective-permute-start.14 = (f32[128,128]{1,0:T(8,128)S(1)}, f32[128,128]{1,0:T(8,128)S(1)}, u32[]{:S(2)}, u32[]{:S(2)}) collective-permute-start(f32[128,128]{1,0:T(8,128)S(1)} %get-tuple-element.72), channel_id=1, source_target_pairs={{0,8},{1,9},{2,10},{3,11},{4,12},{5,13},{6,14},{7,15},{8,0},{9,1},... | collective-permute-start | bytes 196616 | tf_op jit(solution)/shard_map/ppermute | solution.py:394
  39.1 0.0 collective-permute-done.16.refs_2_
  39.1 0.4 collective-permute-done.17.refs_3_
  39.5 0.8 %shard_map.97 = f32[2,512,128]{2,1,0:T(8,128)} custom-call(f32[256,128]{1,0:T(8,128)S(1)} %get-tuple-element.74.refs_0_, f32[256,128]{1,0:T(8,128)S(1)} %collective-permute-done.15.refs_1_, f32[256,128]{1,0:T(8,128)S(1)} %collective-permute-done.16.refs_2_, f32[256,128]{1,0:T(8,128)S(1)} %collective-permute-done.17.refs_3_), custom_call_target="tpu_custom_call" | custom-call | tf_op jit(solution)/shard_map/pallas_call | solution.py:489
  40.3 0.5 %collective-permute-done.12.refs_0_ = f32[128,128]{1,0:T(8,128)S(1)} collective-permute-done((f32[128,128]{1,0:T(8,128)S(1)}, f32[128,128]{1,0:T(8,128)S(1)}, u32[]{:S(2)}, u32[]{:S(2)}) %collective-permute-start.12) | collective-permute-done | bytes 65568 | tf_op jit(solution)/shard_map/ppermute | solution.py:394
  40.8 2.5 %collective-permute-done.13.refs_1_ = f32[128,128]{1,0:T(8,128)S(1)} collective-permute-done((f32[128,128]{1,0:T(8,128)S(1)}, f32[128,128]{1,0:T(8,128)S(1)}, u32[]{:S(2)}, u32[]{:S(2)}) %collective-permute-start.13) | collective-permute-done | bytes 65568 | tf_op jit(solution)/shard_map/ppermute | solution.py:394
  43.3 0.0 collective-permute-done.14.refs_2_
  43.3 0.6 %shard_map.96 = f32[2,64,128]{2,1,0:T(8,128)} custom-call(f32[128,128]{1,0:T(8,128)S(1)} %collective-permute-done.12.refs_0_, f32[128,128]{1,0:T(8,128)S(1)} %collective-permute-done.13.refs_1_, f32[128,128]{1,0:T(8,128)S(1)} %collective-permute-done.14.refs_2_, f32[128,128]{1,0:T(8,128)S(1)} %get-tuple-element.73.refs_3_), custom_call_target="tpu_custom_call" | custom-call | tf_op jit(solution)/shard_map/pallas_call | solution.py:490
  (3 shorter events, 0.1 us)
Async XLA Ops:
  1.8 10.1 %collective-permute-start = (f32[432,128]{1,0:T(8,128)S(1)}, f32[432,128]{1,0:T(8,128)S(1)}, u32[]{:S(2)}, u32[]{:S(2)}) collective-permute-start(f32[432,128]{1,0:T(8,128)S(1)} %get-tuple-element.45), channel_id=1, source_target_pairs={{0,1},{1,0},{2,3},{3,2},{4,5},{5,4},{6,7},{7,6},{8,9},{9,8},{10,11... | collective-permute-start | bytes 663560 | tf_op jit(solution)/shard_map/ppermute | solution.py:394
  4.8 14.2 %collective-permute-start.1 = (f32[432,128]{1,0:T(8,128)S(1)}, f32[432,128]{1,0:T(8,128)S(1)}, u32[]{:S(2)}, u32[]{:S(2)}) collective-permute-start(f32[432,128]{1,0:T(8,128)S(1)} %get-tuple-element.46), channel_id=1, source_target_pairs={{0,2},{1,3},{2,0},{3,1},{4,6},{5,7},{6,4},{7,5},{8,10},{9,11},{10,... | collective-permute-start | bytes 663560 | tf_op jit(solution)/shard_map/ppermute | solution.py:394
  6.3 12.7 %collective-permute-start.2 = (f32[432,128]{1,0:T(8,128)S(1)}, f32[432,128]{1,0:T(8,128)S(1)}, u32[]{:S(2)}, u32[]{:S(2)}) collective-permute-start(f32[432,128]{1,0:T(8,128)S(1)} %get-tuple-element.47), channel_id=1, source_target_pairs={{0,3},{1,2},{2,1},{3,0},{4,7},{5,6},{6,5},{7,4},{8,11},{9,10},{10,... | collective-permute-start | bytes 663560 | tf_op jit(solution)/shard_map/ppermute | solution.py:394
  7.8 13.3 %collective-permute-start.3 = (f32[288,128]{1,0:T(8,128)S(1)}, f32[288,128]{1,0:T(8,128)S(1)}, u32[]{:S(2)}, u32[]{:S(2)}) collective-permute-start(f32[288,128]{1,0:T(8,128)S(1)} %get-tuple-element.51), channel_id=1, source_target_pairs={{0,1},{1,0},{2,3},{3,2},{4,5},{5,4},{6,7},{7,6},{8,9},{9,8},{10,11... | collective-permute-start | bytes 442376 | tf_op jit(solution)/shard_map/ppermute | solution.py:394
  9.8 13.0 %collective-permute-start.4 = (f32[288,128]{1,0:T(8,128)S(1)}, f32[288,128]{1,0:T(8,128)S(1)}, u32[]{:S(2)}, u32[]{:S(2)}) collective-permute-start(f32[288,128]{1,0:T(8,128)S(1)} %get-tuple-element.52), channel_id=1, source_target_pairs={{0,2},{1,3},{2,0},{3,1},{4,6},{5,7},{6,4},{7,5},{8,10},{9,11},{10,... | collective-permute-start | bytes 442376 | tf_op jit(solution)/shard_map/ppermute | solution.py:394
  12.0 10.8 %collective-permute-start.5 = (f32[288,128]{1,0:T(8,128)S(1)}, f32[288,128]{1,0:T(8,128)S(1)}, u32[]{:S(2)}, u32[]{:S(2)}) collective-permute-start(f32[288,128]{1,0:T(8,128)S(1)} %get-tuple-element.53), channel_id=1, source_target_pairs={{0,3},{1,2},{2,1},{3,0},{4,7},{5,6},{6,5},{7,4},{8,11},{9,10},{10,... | collective-permute-start | bytes 442376 | tf_op jit(solution)/shard_map/ppermute | solution.py:394
  19.1 1.4 %collective-permute-start.6 = (f32[216,128]{1,0:T(8,128)S(1)}, f32[216,128]{1,0:T(8,128)S(1)}, u32[]{:S(2)}, u32[]{:S(2)}) collective-permute-start(f32[216,128]{1,0:T(8,128)S(1)} %get-tuple-element.58), channel_id=1, source_target_pairs={{0,4},{1,5},{2,6},{3,7},{4,0},{5,1},{6,2},{7,3},{8,12},{9,13},{10,... | collective-permute-start | bytes 331784 | tf_op jit(solution)/shard_map/ppermute | solution.py:394
  19.2 1.5 %collective-permute-start.7 = (f32[216,128]{1,0:T(8,128)S(1)}, f32[216,128]{1,0:T(8,128)S(1)}, u32[]{:S(2)}, u32[]{:S(2)}) collective-permute-start(f32[216,128]{1,0:T(8,128)S(1)} %get-tuple-element.59), channel_id=1, source_target_pairs={{0,4},{1,5},{2,6},{3,7},{4,0},{5,1},{6,2},{7,3},{8,12},{9,13},{10,... | collective-permute-start | bytes 331784 | tf_op jit(solution)/shard_map/ppermute | solution.py:394
  25.1 1.6 %collective-permute-start.8 = (f32[512,128]{1,0:T(8,128)S(1)}, f32[512,128]{1,0:T(8,128)S(1)}, u32[]{:S(2)}, u32[]{:S(2)}) collective-permute-start(f32[512,128]{1,0:T(8,128)S(1)} %shard_map.93), channel_id=1, source_target_pairs={{0,4},{1,5},{2,6},{3,7},{4,0},{5,1},{6,2},{7,3},{8,12},{9,13},{10,... | collective-permute-start | bytes 786440 | tf_op jit(solution)/shard_map/ppermute | solution.py:394
  26.8 5.6 %collective-permute-start.9 = (f32[128,128]{1,0:T(8,128)S(1)}, f32[128,128]{1,0:T(8,128)S(1)}, u32[]{:S(2)}, u32[]{:S(2)}) collective-permute-start(f32[128,128]{1,0:T(8,128)S(1)} %get-tuple-element.66), channel_id=1, source_target_pairs={{0,3},{1,2},{2,1},{3,0},{4,7},{5,6},{6,5},{7,4},{8,11},{9,10},{10,... | collective-permute-start | bytes 196616 | tf_op jit(solution)/shard_map/ppermute | solution.py:394
  28.3 5.5 %collective-permute-start.10 = (f32[128,128]{1,0:T(8,128)S(1)}, f32[128,128]{1,0:T(8,128)S(1)}, u32[]{:S(2)}, u32[]{:S(2)}) collective-permute-start(f32[128,128]{1,0:T(8,128)S(1)} %get-tuple-element.67), channel_id=1, source_target_pairs={{0,2},{1,3},{2,0},{3,1},{4,6},{5,7},{6,4},{7,5},{8,10},{9,11},{10,... | collective-permute-start | bytes 196616 | tf_op jit(solution)/shard_map/ppermute | solution.py:394
  29.6 5.0 %collective-permute-start.11 = (f32[128,128]{1,0:T(8,128)S(1)}, f32[128,128]{1,0:T(8,128)S(1)}, u32[]{:S(2)}, u32[]{:S(2)}) collective-permute-start(f32[128,128]{1,0:T(8,128)S(1)} %get-tuple-element.68), channel_id=1, source_target_pairs={{0,1},{1,0},{2,3},{3,2},{4,5},{5,4},{6,7},{7,6},{8,9},{9,8},{10,11... | collective-permute-start | bytes 196616 | tf_op jit(solution)/shard_map/ppermute | solution.py:394
  30.3 7.8 %collective-permute-start.15 = (f32[256,128]{1,0:T(8,128)S(1)}, f32[256,128]{1,0:T(8,128)S(1)}, u32[]{:S(2)}, u32[]{:S(2)}) collective-permute-start(f32[256,128]{1,0:T(8,128)S(1)} %get-tuple-element.75), channel_id=1, source_target_pairs={{0,1},{1,0},{2,3},{3,2},{4,5},{5,4},{6,7},{7,6},{8,9},{9,8},{10,11... | collective-permute-start | bytes 393224 | tf_op jit(solution)/shard_map/ppermute | solution.py:394
  31.6 7.5 %collective-permute-start.16 = (f32[256,128]{1,0:T(8,128)S(1)}, f32[256,128]{1,0:T(8,128)S(1)}, u32[]{:S(2)}, u32[]{:S(2)}) collective-permute-start(f32[256,128]{1,0:T(8,128)S(1)} %get-tuple-element.76), channel_id=1, source_target_pairs={{0,2},{1,3},{2,0},{3,1},{4,6},{5,7},{6,4},{7,5},{8,10},{9,11},{10,... | collective-permute-start | bytes 393224 | tf_op jit(solution)/shard_map/ppermute | solution.py:394
  32.4 7.1 %collective-permute-start.17 = (f32[256,128]{1,0:T(8,128)S(1)}, f32[256,128]{1,0:T(8,128)S(1)}, u32[]{:S(2)}, u32[]{:S(2)}) collective-permute-start(f32[256,128]{1,0:T(8,128)S(1)} %get-tuple-element.77), channel_id=1, source_target_pairs={{0,3},{1,2},{2,1},{3,0},{4,7},{5,6},{6,5},{7,4},{8,11},{9,10},{10,... | collective-permute-start | bytes 393224 | tf_op jit(solution)/shard_map/ppermute | solution.py:394
  34.7 6.1 %collective-permute-start.12 = (f32[128,128]{1,0:T(8,128)S(1)}, f32[128,128]{1,0:T(8,128)S(1)}, u32[]{:S(2)}, u32[]{:S(2)}) collective-permute-start(f32[128,128]{1,0:T(8,128)S(1)} %get-tuple-element.70), channel_id=1, source_target_pairs={{0,24},{1,25},{2,26},{3,27},{4,28},{5,29},{6,30},{7,31},{8,16},{9,... | collective-permute-start | bytes 196616 | tf_op jit(solution)/shard_map/ppermute | solution.py:394
  38.1 5.2 %collective-permute-start.13 = (f32[128,128]{1,0:T(8,128)S(1)}, f32[128,128]{1,0:T(8,128)S(1)}, u32[]{:S(2)}, u32[]{:S(2)}) collective-permute-start(f32[128,128]{1,0:T(8,128)S(1)} %get-tuple-element.71), channel_id=1, source_target_pairs={{0,16},{1,17},{2,18},{3,19},{4,20},{5,21},{6,22},{7,23},{8,24},{9,... | collective-permute-start | bytes 196616 | tf_op jit(solution)/shard_map/ppermute | solution.py:394
  38.1 5.2 %collective-permute-start.14 = (f32[128,128]{1,0:T(8,128)S(1)}, f32[128,128]{1,0:T(8,128)S(1)}, u32[]{:S(2)}, u32[]{:S(2)}) collective-permute-start(f32[128,128]{1,0:T(8,128)S(1)} %get-tuple-element.72), channel_id=1, source_target_pairs={{0,8},{1,9},{2,10},{3,11},{4,12},{5,13},{6,14},{7,15},{8,0},{9,1},... | collective-permute-start | bytes 196616 | tf_op jit(solution)/shard_map/ppermute | solution.py:394

commit v7 on v6

--- a/solution.py
+++ b/solution.py
@@ -240,7 +240,7 @@
 
 
 def forward(blocks, planes, rows, ny, source, pulse, *refs):
-    late, own, start, model, step, refs = refs[: blocks - 1], *refs[blocks - 1 : blocks + 3], refs[blocks + 3 :]
+    late, own, start, model, step, refs = refs[: blocks - 1][::-1], *refs[blocks - 1 : blocks + 3], refs[blocks + 3 :]
     wave, lap, turned = *refs[:2], refs[2:]
     nx, tall, depth = lap.shape[1:]
     dom = lax.axis_index("dom")
@@ -454,7 +454,7 @@
         in_specs=[SMEM] + [VMEM] * (blocks + 4),
         flops=16 * NT * cells,
         moved=16 * NT * cells,
-    )(source_cell, pulse, *late, own, start, model, step)
+    )(source_cell, pulse, *late[::-1], own, start, model, step)
     half = rows // 2
     side = half + 2 * EDGE
     give, keep = (

time: 44.1 us -> 44.2 us (level)
  waiting for transfers between devices: 7.23 us -> 8.24 us
  starting transfers between devices: 22.3 us -> 21.4 us
    ppermute x18, waiting for transfers between devices: 7.23 us -> 8.24 us  [across(): return lax.ppermute(array, ('shot', 'dom'), pairs)]
    ppermute x18, starting transfers between devices: 22.3 us -> 21.4 us  [across(): return lax.ppermute(array, ('shot', 'dom'), pairs)]
  transfers between devices with their start and end apart: 18 -> 18, of which waited for: 8 -> 9; matrix products, arithmetic and copies ran while one was open for 0% -> 0% of each run, Pallas kernels for 20% -> 20%
where the time goes in v7:
time: 44.2 us; the launch traced here: 44 us
  starting transfers between devices  21.4 us (48%)
  Pallas kernels  12.9 us (29%)
  waiting for transfers between devices  8.24 us (19%)
  between operations  1.39 us (3%)
    ppermute x18, starting transfers between devices, across(): return lax.ppermute(array, ('shot', 'dom'), pairs)  21.4 us
    ppermute x18, waiting for transfers between devices, across(): return lax.ppermute(array, ('shot', 'dom'), pairs)  8.24 us
    pallas_call x1, Pallas kernels, shards(): call(functools.partial(spread, depth, ny, rows, listed), [(nx * tall, dep...  4.95 us
    pallas_call x2, Pallas kernels, shards(): call(functools.partial(backward, mine, rows), [(nx * half, depth)], in_sp...  2.13 us
    pallas_call x1, Pallas kernels, shards(): call(functools.partial(pack_late, blocks, planes, rows), [(planes * tall,...  1.4 us
    pallas_call x1, Pallas kernels, shards(): call(functools.partial(forward, blocks, planes, rows, ny), [(NT, *padded)...  1.3 us
    pallas_call x1, Pallas kernels, shards(): call(functools.partial(pack_early, blocks, planes, rows), [(planes * (tal...  1.17 us
  transfers between devices with their start and end apart: 18, of which 9 were waited for; matrix products, arithmetic and copies ran while one was open for 0% of the time, Pallas kernels for 20%

profile of v7, /device:TPU:0, one launch (start us, length us, event | category | flops | bytes accessed | tf_op | source)
XLA Modules:
  0.0 44.0 jit_solution(15306342032796666882)
XLA Ops:
  0.6 1.2 %shard_map.87 = (f32[432,128]{1,0:T(8,128)S(1)}, f32[432,128]{1,0:T(8,128)S(1)}, f32[432,128]{1,0:T(8,128)S(1)}) custom-call(f32[2,4,128,128]{3,2,1,0:T(8,128)} %bitcast.4, f32[2,512,128]{2,1,0:T(8,128)} %bitcast.5), custom_call_target="tpu_custom_call" | custom-call | tf_op jit(solution)/shard_map/pallas_call | solution.py:404
  1.8 3.0 %collective-permute-start = (f32[432,128]{1,0:T(8,128)S(1)}, f32[432,128]{1,0:T(8,128)S(1)}, u32[]{:S(2)}, u32[]{:S(2)}) collective-permute-start(f32[432,128]{1,0:T(8,128)S(1)} %get-tuple-element.45), channel_id=1, source_target_pairs={{0,1},{1,0},{2,3},{3,2},{4,5},{5,4},{6,7},{7,6},{8,9},{9,8},{10,11... | collective-permute-start | bytes 663560 | tf_op jit(solution)/shard_map/ppermute | solution.py:394
  4.8 1.5 %collective-permute-start.1 = (f32[432,128]{1,0:T(8,128)S(1)}, f32[432,128]{1,0:T(8,128)S(1)}, u32[]{:S(2)}, u32[]{:S(2)}) collective-permute-start(f32[432,128]{1,0:T(8,128)S(1)} %get-tuple-element.46), channel_id=1, source_target_pairs={{0,2},{1,3},{2,0},{3,1},{4,6},{5,7},{6,4},{7,5},{8,10},{9,11},{10,... | collective-permute-start | bytes 663560 | tf_op jit(solution)/shard_map/ppermute | solution.py:394
  6.3 0.0 collective-permute-start.2
  6.3 1.4 %shard_map.88 = (f32[288,128]{1,0:T(8,128)S(1)}, f32[288,128]{1,0:T(8,128)S(1)}, f32[288,128]{1,0:T(8,128)S(1)}, f32[864,128]{1,0:T(8,128)S(1)}) custom-call(f32[2,512,128]{2,1,0:T(8,128)} %kappa.1, f32[2,512,128]{2,1,0:T(8,128)} %bitcast.6, f32[2,512,128]{2,1,0:T(8,128)} %bitcast.7), custom_call_target="tpu_custom_call" | custom-call | tf_op jit(solution)/shard_map/pallas_call | solution.py:416
  7.8 3.0 %collective-permute-start.3 = (f32[288,128]{1,0:T(8,128)S(1)}, f32[288,128]{1,0:T(8,128)S(1)}, u32[]{:S(2)}, u32[]{:S(2)}) collective-permute-start(f32[288,128]{1,0:T(8,128)S(1)} %get-tuple-element.51), channel_id=1, source_target_pairs={{0,3},{1,2},{2,1},{3,0},{4,7},{5,6},{6,5},{7,4},{8,11},{9,10},{10,... | collective-permute-start | bytes 442376 | tf_op jit(solution)/shard_map/ppermute | solution.py:394
  10.7 0.5 %collective-permute-start.4 = (f32[288,128]{1,0:T(8,128)S(1)}, f32[288,128]{1,0:T(8,128)S(1)}, u32[]{:S(2)}, u32[]{:S(2)}) collective-permute-start(f32[288,128]{1,0:T(8,128)S(1)} %get-tuple-element.52), channel_id=1, source_target_pairs={{0,2},{1,3},{2,0},{3,1},{4,6},{5,7},{6,4},{7,5},{8,10},{9,11},{10,... | collective-permute-start | bytes 442376 | tf_op jit(solution)/shard_map/ppermute | solution.py:394
  11.9 0.0 collective-permute-done.refs_0_
  11.9 1.2 %collective-permute-start.5 = (f32[288,128]{1,0:T(8,128)S(1)}, f32[288,128]{1,0:T(8,128)S(1)}, u32[]{:S(2)}, u32[]{:S(2)}) collective-permute-start(f32[288,128]{1,0:T(8,128)S(1)} %get-tuple-element.53), channel_id=1, source_target_pairs={{0,1},{1,0},{2,3},{3,2},{4,5},{5,4},{6,7},{7,6},{8,9},{9,8},{10,11... | collective-permute-start | bytes 442376 | tf_op jit(solution)/shard_map/ppermute | solution.py:394
  13.1 4.9 %shard_map.86 = (f32[1152,128]{1,0:T(8,128)S(1)}, f32[4,1152,128]{2,1,0:T(8,128)S(1)}, f32[4,128]{1,0:T(4,128)S(1)}) custom-call(s32[1]{0:T(128)S(6)} %copy.9.source, f32[1,4]{1,0:T(1,128)} %lists_at.1, s32[1,2048]{1,0:T(1,128)} %cells_at.1, f32[1,4,2048]{2,1,0:T(4,128)} %observed_at.1), custom_call_target="tpu_custom_call" | custom-call | flops 600000000 | bytes 1 | tf_op jit(solution)/shard_map/pallas_call | solution.py:425
  18.1 2.0 %collective-permute-done.1.refs_1_ = f32[432,128]{1,0:T(8,128)S(1)} collective-permute-done((f32[432,128]{1,0:T(8,128)S(1)}, f32[432,128]{1,0:T(8,128)S(1)}, u32[]{:S(2)}, u32[]{:S(2)}) %collective-permute-start.1) | collective-permute-done | bytes 221216 | tf_op jit(solution)/shard_map/ppermute | solution.py:394
  20.1 0.0 collective-permute-done.2.refs_2_
  20.1 0.1 collective-permute-start.6
  20.2 0.5 %collective-permute-start.7 = (f32[216,128]{1,0:T(8,128)S(1)}, f32[216,128]{1,0:T(8,128)S(1)}, u32[]{:S(2)}, u32[]{:S(2)}) collective-permute-start(f32[216,128]{1,0:T(8,128)S(1)} %get-tuple-element.59), channel_id=1, source_target_pairs={{0,4},{1,5},{2,6},{3,7},{4,0},{5,1},{6,2},{7,3},{8,12},{9,13},{10,... | collective-permute-start | bytes 331784 | tf_op jit(solution)/shard_map/ppermute | solution.py:394
  20.7 0.8 %collective-permute-done.6.refs_3_ = f32[216,128]{1,0:T(8,128)S(1)} collective-permute-done((f32[216,128]{1,0:T(8,128)S(1)}, f32[216,128]{1,0:T(8,128)S(1)}, u32[]{:S(2)}, u32[]{:S(2)}) %collective-permute-start.6) | collective-permute-done | bytes 110624 | tf_op jit(solution)/shard_map/ppermute | solution.py:394
  21.5 0.2 collective-permute-done.7.refs_4_
  21.7 0.4 shard_map.90
  22.1 0.0 collective-permute-done.3.refs_0_
  22.1 0.6 %collective-permute-done.4.refs_1_ = f32[288,128]{1,0:T(8,128)S(1)} collective-permute-done((f32[288,128]{1,0:T(8,128)S(1)}, f32[288,128]{1,0:T(8,128)S(1)}, u32[]{:S(2)}, u32[]{:S(2)}) %collective-permute-start.4) | collective-permute-done | bytes 147488 | tf_op jit(solution)/shard_map/ppermute | solution.py:394
  22.8 0.0 collective-permute-done.5.refs_2_
  22.8 1.3 %shard_map.91 = (f32[4,8,160,128]{3,2,1,0:T(8,128)S(1)}, f32[3,8,144,128]{3,2,1,0:T(8,128)S(1)}, f32[256,128]{1,0:T(8,128)S(1)}, f32[256,128]{1,0:T(8,128)S(1)},...) custom-call(s32[1]{0:T(128)S(6)} %copy.9.source, f32[4,128]{1,0:T(4,128)S(1)} %get-tuple-element.49.pulse, ...), custom_call_target="tpu_custom_call" | custom-call | flops 9437184 | bytes 9437184 | tf_op jit(solution)/shard_map/pallas_call | solution.py:451
  24.1 1.1 %shard_map.93 = f32[512,128]{1,0:T(8,128)S(1)} custom-call(f32[1152,128]{1,0:T(8,128)S(1)} %get-tuple-element.40.count, f32[4,1152,128]{2,1,0:T(8,128)S(1)} %get-tuple-element.41.heard, f32[4,8,160,128]{3,2,1,0:T(8,128)S(1)} %get-tuple-element.63.wave, f32[3,8,144,128]{3,2,1,0:T(8,128)S(1)} %get-tuple-element.64.lap, ...), custom_call_target="tpu_custom_call" | custom-call | flops 7077888 | bytes 7077888 | tf_op jit(solution)/shard_map/pallas_call | solution.py:461
  25.1 0.1 collective-permute-start.8
  25.2 1.1 %shard_map.92.keep = f32[512,128]{1,0:T(8,128)S(1)} custom-call(f32[1152,128]{1,0:T(8,128)S(1)} %get-tuple-element.40.count, f32[4,1152,128]{2,1,0:T(8,128)S(1)} %get-tuple-element.41.heard, f32[4,8,160,128]{3,2,1,0:T(8,128)S(1)} %get-tuple-element.63.wave, f32[3,8,144,128]{3,2,1,0:T(8,128)S(1)} %get-tuple-element.64.lap, ...), custom_call_target="tpu_custom_call" | custom-call | flops 7077888 | bytes 7077888 | tf_op jit(solution)/shard_map/pallas_call | solution.py:461
  26.3 0.5 %collective-permute-done.8.got = f32[512,128]{1,0:T(8,128)S(1)} collective-permute-done((f32[512,128]{1,0:T(8,128)S(1)}, f32[512,128]{1,0:T(8,128)S(1)}, u32[]{:S(2)}, u32[]{:S(2)}) %collective-permute-start.8) | collective-permute-done | bytes 262176 | tf_op jit(solution)/shard_map/ppermute | solution.py:394
  26.8 1.5 %collective-permute-start.9 = (f32[128,128]{1,0:T(8,128)S(1)}, f32[128,128]{1,0:T(8,128)S(1)}, u32[]{:S(2)}, u32[]{:S(2)}) collective-permute-start(f32[128,128]{1,0:T(8,128)S(1)} %get-tuple-element.66), channel_id=1, source_target_pairs={{0,3},{1,2},{2,1},{3,0},{4,7},{5,6},{6,5},{7,4},{8,11},{9,10},{10,... | collective-permute-start | bytes 196616 | tf_op jit(solution)/shard_map/ppermute | solution.py:394
  28.3 0.5 %collective-permute-start.10 = (f32[128,128]{1,0:T(8,128)S(1)}, f32[128,128]{1,0:T(8,128)S(1)}, u32[]{:S(2)}, u32[]{:S(2)}) collective-permute-start(f32[128,128]{1,0:T(8,128)S(1)} %get-tuple-element.67), channel_id=1, source_target_pairs={{0,2},{1,3},{2,0},{3,1},{4,6},{5,7},{6,4},{7,5},{8,10},{9,11},{10,... | collective-permute-start | bytes 196616 | tf_op jit(solution)/shard_map/ppermute | solution.py:394
  28.8 1.6 %collective-permute-start.11 = (f32[128,128]{1,0:T(8,128)S(1)}, f32[128,128]{1,0:T(8,128)S(1)}, u32[]{:S(2)}, u32[]{:S(2)}) collective-permute-start(f32[128,128]{1,0:T(8,128)S(1)} %get-tuple-element.68), channel_id=1, source_target_pairs={{0,1},{1,0},{2,3},{3,2},{4,5},{5,4},{6,7},{7,6},{8,9},{9,8},{10,11... | collective-permute-start | bytes 196616 | tf_op jit(solution)/shard_map/ppermute | solution.py:394
  30.3 0.5 %collective-permute-start.15 = (f32[256,128]{1,0:T(8,128)S(1)}, f32[256,128]{1,0:T(8,128)S(1)}, u32[]{:S(2)}, u32[]{:S(2)}) collective-permute-start(f32[256,128]{1,0:T(8,128)S(1)} %get-tuple-element.75), channel_id=1, source_target_pairs={{0,1},{1,0},{2,3},{3,2},{4,5},{5,4},{6,7},{7,6},{8,9},{9,8},{10,11... | collective-permute-start | bytes 393224 | tf_op jit(solution)/shard_map/ppermute | solution.py:394
  30.8 1.6 %collective-permute-start.16 = (f32[256,128]{1,0:T(8,128)S(1)}, f32[256,128]{1,0:T(8,128)S(1)}, u32[]{:S(2)}, u32[]{:S(2)}) collective-permute-start(f32[256,128]{1,0:T(8,128)S(1)} %get-tuple-element.76), channel_id=1, source_target_pairs={{0,2},{1,3},{2,0},{3,1},{4,6},{5,7},{6,4},{7,5},{8,10},{9,11},{10,... | collective-permute-start | bytes 393224 | tf_op jit(solution)/shard_map/ppermute | solution.py:394
  32.4 0.0 collective-permute-done.9.refs_0_
  32.4 1.4 %collective-permute-start.17 = (f32[256,128]{1,0:T(8,128)S(1)}, f32[256,128]{1,0:T(8,128)S(1)}, u32[]{:S(2)}, u32[]{:S(2)}) collective-permute-start(f32[256,128]{1,0:T(8,128)S(1)} %get-tuple-element.77), channel_id=1, source_target_pairs={{0,3},{1,2},{2,1},{3,0},{4,7},{5,6},{6,5},{7,4},{8,11},{9,10},{10,... | collective-permute-start | bytes 393224 | tf_op jit(solution)/shard_map/ppermute | solution.py:394
  33.8 0.0 collective-permute-done.10.refs_1_
  33.8 0.6 %collective-permute-done.11.refs_2_ = f32[128,128]{1,0:T(8,128)S(1)} collective-permute-done((f32[128,128]{1,0:T(8,128)S(1)}, f32[128,128]{1,0:T(8,128)S(1)}, u32[]{:S(2)}, u32[]{:S(2)}) %collective-permute-start.11) | collective-permute-done | bytes 65568 | tf_op jit(solution)/shard_map/ppermute | solution.py:394
  34.5 3.4 %collective-permute-start.12 = (f32[128,128]{1,0:T(8,128)S(1)}, f32[128,128]{1,0:T(8,128)S(1)}, u32[]{:S(2)}, u32[]{:S(2)}) collective-permute-start(f32[128,128]{1,0:T(8,128)S(1)} %get-tuple-element.70), channel_id=1, source_target_pairs={{0,24},{1,25},{2,26},{3,27},{4,28},{5,29},{6,30},{7,31},{8,16},{9,... | collective-permute-start | bytes 196616 | tf_op jit(solution)/shard_map/ppermute | solution.py:394
  37.9 0.0 collective-permute-start.13
  38.0 0.0 collective-permute-done.15.refs_1_
  38.0 1.0 %collective-permute-start.14 = (f32[128,128]{1,0:T(8,128)S(1)}, f32[128,128]{1,0:T(8,128)S(1)}, u32[]{:S(2)}, u32[]{:S(2)}) collective-permute-start(f32[128,128]{1,0:T(8,128)S(1)} %get-tuple-element.72), channel_id=1, source_target_pairs={{0,8},{1,9},{2,10},{3,11},{4,12},{5,13},{6,14},{7,15},{8,0},{9,1},... | collective-permute-start | bytes 196616 | tf_op jit(solution)/shard_map/ppermute | solution.py:394
  39.0 0.0 collective-permute-done.16.refs_2_
  39.0 0.7 %collective-permute-done.17.refs_3_ = f32[256,128]{1,0:T(8,128)S(1)} collective-permute-done((f32[256,128]{1,0:T(8,128)S(1)}, f32[256,128]{1,0:T(8,128)S(1)}, u32[]{:S(2)}, u32[]{:S(2)}) %collective-permute-start.17) | collective-permute-done | bytes 131104 | tf_op jit(solution)/shard_map/ppermute | solution.py:394
  39.7 0.8 %shard_map.97 = f32[2,512,128]{2,1,0:T(8,128)} custom-call(f32[256,128]{1,0:T(8,128)S(1)} %get-tuple-element.74.refs_0_, f32[256,128]{1,0:T(8,128)S(1)} %collective-permute-done.15.refs_1_, f32[256,128]{1,0:T(8,128)S(1)} %collective-permute-done.16.refs_2_, f32[256,128]{1,0:T(8,128)S(1)} %collective-permute-done.17.refs_3_), custom_call_target="tpu_custom_call" | custom-call | tf_op jit(solution)/shard_map/pallas_call | solution.py:489
  40.5 0.2 collective-permute-done.12.refs_0_
  40.7 2.6 %collective-permute-done.13.refs_1_ = f32[128,128]{1,0:T(8,128)S(1)} collective-permute-done((f32[128,128]{1,0:T(8,128)S(1)}, f32[128,128]{1,0:T(8,128)S(1)}, u32[]{:S(2)}, u32[]{:S(2)}) %collective-permute-start.13) | collective-permute-done | bytes 65568 | tf_op jit(solution)/shard_map/ppermute | solution.py:394
  43.3 0.0 collective-permute-done.14.refs_2_
  43.3 0.6 %shard_map.96 = f32[2,64,128]{2,1,0:T(8,128)} custom-call(f32[128,128]{1,0:T(8,128)S(1)} %collective-permute-done.12.refs_0_, f32[128,128]{1,0:T(8,128)S(1)} %collective-permute-done.13.refs_1_, f32[128,128]{1,0:T(8,128)S(1)} %collective-permute-done.14.refs_2_, f32[128,128]{1,0:T(8,128)S(1)} %get-tuple-element.73.refs_3_), custom_call_target="tpu_custom_call" | custom-call | tf_op jit(solution)/shard_map/pallas_call | solution.py:490
  (3 shorter events, 0.1 us)
Async XLA Ops:
  1.8 10.1 %collective-permute-start = (f32[432,128]{1,0:T(8,128)S(1)}, f32[432,128]{1,0:T(8,128)S(1)}, u32[]{:S(2)}, u32[]{:S(2)}) collective-permute-start(f32[432,128]{1,0:T(8,128)S(1)} %get-tuple-element.45), channel_id=1, source_target_pairs={{0,1},{1,0},{2,3},{3,2},{4,5},{5,4},{6,7},{7,6},{8,9},{9,8},{10,11... | collective-permute-start | bytes 663560 | tf_op jit(solution)/shard_map/ppermute | solution.py:394
  4.8 15.3 %collective-permute-start.1 = (f32[432,128]{1,0:T(8,128)S(1)}, f32[432,128]{1,0:T(8,128)S(1)}, u32[]{:S(2)}, u32[]{:S(2)}) collective-permute-start(f32[432,128]{1,0:T(8,128)S(1)} %get-tuple-element.46), channel_id=1, source_target_pairs={{0,2},{1,3},{2,0},{3,1},{4,6},{5,7},{6,4},{7,5},{8,10},{9,11},{10,... | collective-permute-start | bytes 663560 | tf_op jit(solution)/shard_map/ppermute | solution.py:394
  6.3 13.8 %collective-permute-start.2 = (f32[432,128]{1,0:T(8,128)S(1)}, f32[432,128]{1,0:T(8,128)S(1)}, u32[]{:S(2)}, u32[]{:S(2)}) collective-permute-start(f32[432,128]{1,0:T(8,128)S(1)} %get-tuple-element.47), channel_id=1, source_target_pairs={{0,3},{1,2},{2,1},{3,0},{4,7},{5,6},{6,5},{7,4},{8,11},{9,10},{10,... | collective-permute-start | bytes 663560 | tf_op jit(solution)/shard_map/ppermute | solution.py:394
  7.8 14.3 %collective-permute-start.3 = (f32[288,128]{1,0:T(8,128)S(1)}, f32[288,128]{1,0:T(8,128)S(1)}, u32[]{:S(2)}, u32[]{:S(2)}) collective-permute-start(f32[288,128]{1,0:T(8,128)S(1)} %get-tuple-element.51), channel_id=1, source_target_pairs={{0,3},{1,2},{2,1},{3,0},{4,7},{5,6},{6,5},{7,4},{8,11},{9,10},{10,... | collective-permute-start | bytes 442376 | tf_op jit(solution)/shard_map/ppermute | solution.py:394
  10.7 12.0 %collective-permute-start.4 = (f32[288,128]{1,0:T(8,128)S(1)}, f32[288,128]{1,0:T(8,128)S(1)}, u32[]{:S(2)}, u32[]{:S(2)}) collective-permute-start(f32[288,128]{1,0:T(8,128)S(1)} %get-tuple-element.52), channel_id=1, source_target_pairs={{0,2},{1,3},{2,0},{3,1},{4,6},{5,7},{6,4},{7,5},{8,10},{9,11},{10,... | collective-permute-start | bytes 442376 | tf_op jit(solution)/shard_map/ppermute | solution.py:394
  11.9 10.9 %collective-permute-start.5 = (f32[288,128]{1,0:T(8,128)S(1)}, f32[288,128]{1,0:T(8,128)S(1)}, u32[]{:S(2)}, u32[]{:S(2)}) collective-permute-start(f32[288,128]{1,0:T(8,128)S(1)} %get-tuple-element.53), channel_id=1, source_target_pairs={{0,1},{1,0},{2,3},{3,2},{4,5},{5,4},{6,7},{7,6},{8,9},{9,8},{10,11... | collective-permute-start | bytes 442376 | tf_op jit(solution)/shard_map/ppermute | solution.py:394
  20.1 1.4 %collective-permute-start.6 = (f32[216,128]{1,0:T(8,128)S(1)}, f32[216,128]{1,0:T(8,128)S(1)}, u32[]{:S(2)}, u32[]{:S(2)}) collective-permute-start(f32[216,128]{1,0:T(8,128)S(1)} %get-tuple-element.58), channel_id=1, source_target_pairs={{0,4},{1,5},{2,6},{3,7},{4,0},{5,1},{6,2},{7,3},{8,12},{9,13},{10,... | collective-permute-start | bytes 331784 | tf_op jit(solution)/shard_map/ppermute | solution.py:394
  20.2 1.5 %collective-permute-start.7 = (f32[216,128]{1,0:T(8,128)S(1)}, f32[216,128]{1,0:T(8,128)S(1)}, u32[]{:S(2)}, u32[]{:S(2)}) collective-permute-start(f32[216,128]{1,0:T(8,128)S(1)} %get-tuple-element.59), channel_id=1, source_target_pairs={{0,4},{1,5},{2,6},{3,7},{4,0},{5,1},{6,2},{7,3},{8,12},{9,13},{10,... | collective-permute-start | bytes 331784 | tf_op jit(solution)/shard_map/ppermute | solution.py:394
  25.1 1.6 %collective-permute-start.8 = (f32[512,128]{1,0:T(8,128)S(1)}, f32[512,128]{1,0:T(8,128)S(1)}, u32[]{:S(2)}, u32[]{:S(2)}) collective-permute-start(f32[512,128]{1,0:T(8,128)S(1)} %shard_map.93), channel_id=1, source_target_pairs={{0,4},{1,5},{2,6},{3,7},{4,0},{5,1},{6,2},{7,3},{8,12},{9,13},{10,... | collective-permute-start | bytes 786440 | tf_op jit(solution)/shard_map/ppermute | solution.py:394
  26.8 5.6 %collective-permute-start.9 = (f32[128,128]{1,0:T(8,128)S(1)}, f32[128,128]{1,0:T(8,128)S(1)}, u32[]{:S(2)}, u32[]{:S(2)}) collective-permute-start(f32[128,128]{1,0:T(8,128)S(1)} %get-tuple-element.66), channel_id=1, source_target_pairs={{0,3},{1,2},{2,1},{3,0},{4,7},{5,6},{6,5},{7,4},{8,11},{9,10},{10,... | collective-permute-start | bytes 196616 | tf_op jit(solution)/shard_map/ppermute | solution.py:394
  28.3 5.5 %collective-permute-start.10 = (f32[128,128]{1,0:T(8,128)S(1)}, f32[128,128]{1,0:T(8,128)S(1)}, u32[]{:S(2)}, u32[]{:S(2)}) collective-permute-start(f32[128,128]{1,0:T(8,128)S(1)} %get-tuple-element.67), channel_id=1, source_target_pairs={{0,2},{1,3},{2,0},{3,1},{4,6},{5,7},{6,4},{7,5},{8,10},{9,11},{10,... | collective-permute-start | bytes 196616 | tf_op jit(solution)/shard_map/ppermute | solution.py:394
  28.8 5.7 %collective-permute-start.11 = (f32[128,128]{1,0:T(8,128)S(1)}, f32[128,128]{1,0:T(8,128)S(1)}, u32[]{:S(2)}, u32[]{:S(2)}) collective-permute-start(f32[128,128]{1,0:T(8,128)S(1)} %get-tuple-element.68), channel_id=1, source_target_pairs={{0,1},{1,0},{2,3},{3,2},{4,5},{5,4},{6,7},{7,6},{8,9},{9,8},{10,11... | collective-permute-start | bytes 196616 | tf_op jit(solution)/shard_map/ppermute | solution.py:394
  30.3 7.6 %collective-permute-start.15 = (f32[256,128]{1,0:T(8,128)S(1)}, f32[256,128]{1,0:T(8,128)S(1)}, u32[]{:S(2)}, u32[]{:S(2)}) collective-permute-start(f32[256,128]{1,0:T(8,128)S(1)} %get-tuple-element.75), channel_id=1, source_target_pairs={{0,1},{1,0},{2,3},{3,2},{4,5},{5,4},{6,7},{7,6},{8,9},{9,8},{10,11... | collective-permute-start | bytes 393224 | tf_op jit(solution)/shard_map/ppermute | solution.py:394
  30.8 8.2 %collective-permute-start.16 = (f32[256,128]{1,0:T(8,128)S(1)}, f32[256,128]{1,0:T(8,128)S(1)}, u32[]{:S(2)}, u32[]{:S(2)}) collective-permute-start(f32[256,128]{1,0:T(8,128)S(1)} %get-tuple-element.76), channel_id=1, source_target_pairs={{0,2},{1,3},{2,0},{3,1},{4,6},{5,7},{6,4},{7,5},{8,10},{9,11},{10,... | collective-permute-start | bytes 393224 | tf_op jit(solution)/shard_map/ppermute | solution.py:394
  32.4 7.3 %collective-permute-start.17 = (f32[256,128]{1,0:T(8,128)S(1)}, f32[256,128]{1,0:T(8,128)S(1)}, u32[]{:S(2)}, u32[]{:S(2)}) collective-permute-start(f32[256,128]{1,0:T(8,128)S(1)} %get-tuple-element.77), channel_id=1, source_target_pairs={{0,3},{1,2},{2,1},{3,0},{4,7},{5,6},{6,5},{7,4},{8,11},{9,10},{10,... | collective-permute-start | bytes 393224 | tf_op jit(solution)/shard_map/ppermute | solution.py:394
  34.5 6.2 %collective-permute-start.12 = (f32[128,128]{1,0:T(8,128)S(1)}, f32[128,128]{1,0:T(8,128)S(1)}, u32[]{:S(2)}, u32[]{:S(2)}) collective-permute-start(f32[128,128]{1,0:T(8,128)S(1)} %get-tuple-element.70), channel_id=1, source_target_pairs={{0,24},{1,25},{2,26},{3,27},{4,28},{5,29},{6,30},{7,31},{8,16},{9,... | collective-permute-start | bytes 196616 | tf_op jit(solution)/shard_map/ppermute | solution.py:394
  37.9 5.4 %collective-permute-start.13 = (f32[128,128]{1,0:T(8,128)S(1)}, f32[128,128]{1,0:T(8,128)S(1)}, u32[]{:S(2)}, u32[]{:S(2)}) collective-permute-start(f32[128,128]{1,0:T(8,128)S(1)} %get-tuple-element.71), channel_id=1, source_target_pairs={{0,16},{1,17},{2,18},{3,19},{4,20},{5,21},{6,22},{7,23},{8,24},{9,... | collective-permute-start | bytes 196616 | tf_op jit(solution)/shard_map/ppermute | solution.py:394
  38.0 5.4 %collective-permute-start.14 = (f32[128,128]{1,0:T(8,128)S(1)}, f32[128,128]{1,0:T(8,128)S(1)}, u32[]{:S(2)}, u32[]{:S(2)}) collective-permute-start(f32[128,128]{1,0:T(8,128)S(1)} %get-tuple-element.72), channel_id=1, source_target_pairs={{0,8},{1,9},{2,10},{3,11},{4,12},{5,13},{6,14},{7,15},{8,0},{9,1},... | collective-permute-start | bytes 196616 | tf_op jit(solution)/shard_map/ppermute | solution.py:394
